TPU v7x, 32 devices: a whole 2x2x4 slice. The times are simulated.
32 devices in a mesh: ctx: 8 (over z, core), ch: 4 (over y, x).
Axes of the slice: x: 2, y: 2, z: 4, core: 2. Of those that a mesh axis runs over, the one named last changes fastest.
Arguments:
- g_out: bfloat16 [8192, 8192], P('ctx', 'ch'), may hold values from -6 to 6
- w_out: bfloat16 [1024, 8192], P(None, 'ch'), may hold values from -0.0625 to 0.0625
- gate_x1: bfloat16 [8192, 1024], P('ctx', 'ch'), may hold values from -6 to 6
- gate_x2: bfloat16 [8192, 1024], P('ctx', 'ch'), may hold values from -6 to 6
- value_v: bfloat16 [8192, 1024], P('ctx', 'ch'), may hold values from -6 to 6
- residue: float32 [1024, 16], P('ch'), may hold values from -4 to 4
- decay: float32 [1024, 16], P('ch'), may hold values from 6.1035156e-05 to 0.05
Outputs:
- grad_x1: bfloat16 [8192, 1024], P('ctx', 'ch')
- grad_x2: bfloat16 [8192, 1024], P('ctx', 'ch')
- grad_v: bfloat16 [8192, 1024], P('ctx', 'ch')
- residue_grad: float32 [1024, 16], P(('ch', 'ctx'))
- decay_grad: float32 [1024, 16], P(('ch', 'ctx'))
All inputs are finite; a program needn't handle non-finite values.
Results may differ from a plain program's by a relative error of at most 0.023.
Values may be sent and summed in bfloat16 or wider, within the bound.
No kernel may reach another device: no remote copies, remote signals or barrier semaphores. Data moves between devices by JAX's collectives and lax.ppermute only.
A program may use at most 128 MiB of HBM per device.

v0:
```python
import functools

import jax
import jax.numpy as jnp
from jax import lax
from jax.experimental import pallas as pl
from jax.experimental.pallas import tpu as pltpu
from jax.sharding import PartitionSpec as P

LANES = 128
BLOCKS = 8
F32 = jnp.float32
BF16 = jnp.bfloat16


def halving_layout(order):
    if not order:
        return [0]
    rest = halving_layout(order[1:])
    return [offset ^ order[0] for offset in rest] + rest


def xor_pairs(count, step):
    return [(index, index ^ step) for index in range(count)]


def params(vmem=48 * 2**20):
    return pltpu.CompilerParams(vmem_limit_bytes=vmem)


def project_body(which_ref, g_ref, w_ref, out_ref):
    out_ref[...] = lax.dot_general(
        g_ref[...], w_ref[...], (((1,), (1,)), ((), ())), preferred_element_type=F32
    ).astype(out_ref.dtype)


def project(which, g_out, w_out, start, rows, width, dtype):
    depth = g_out.shape[1]
    count = which.shape[0]
    tile = min(rows, 256)
    tiles = rows // tile
    first = start // tile
    spec = pltpu.PrefetchScalarGridSpec(
        num_scalar_prefetch=1,
        grid=(count, tiles),
        in_specs=[
            pl.BlockSpec((tile, depth), lambda j, i, s: (first + i, 0)),
            pl.BlockSpec((width, depth), lambda j, i, s: (s[j], 0)),
        ],
        out_specs=pl.BlockSpec((tile, width), lambda j, i, s: (i, j)),
    )
    return pl.pallas_call(
        project_body,
        grid_spec=spec,
        out_shape=jax.ShapeDtypeStruct((rows, count * width), dtype),
        compiler_params=params(),
        cost_estimate=pl.CostEstimate(
            flops=2 * rows * depth * count * width,
            bytes_accessed=2 * depth * (rows + count * width),
            transcendentals=0,
        ),
        name="project",
    )(which, g_out, w_out)


def spread(ref, row, lanes):
    return jnp.broadcast_to(ref[pl.ds(row, 1), lanes], (BLOCKS, LANES))


def forward_body(segments, modes, x2_ref, v_ref, a_ref, r_ref, decay_ref,
                 xperm_ref, yloc_ref, hb_ref, eb_ref, total_ref, nat):
    channels = x2_ref.shape[1]
    unroll = 4
    half = modes // 2
    for lane in range(channels // LANES):
        lanes = pl.ds(lane * LANES, LANES)
        mixed = (x2_ref[:, lanes].astype(F32) * v_ref[:, lanes].astype(F32)).astype(BF16)
        nat[lane] = mixed.astype(F32)
        for seg, (start, rows) in enumerate(segments):
            steps = rows // BLOCKS
            for part in range(2):
                decays = [spread(a_ref, part * half + m, lanes) for m in range(half)]
                weights = [spread(r_ref, part * half + m, lanes) for m in range(half)]

                def body(outer, carry):
                    h, e = list(carry[0]), list(carry[1])
                    for q in range(unroll):
                        i = outer * unroll + q
                        here = pl.ds(pl.multiple_of(start + i * BLOCKS, BLOCKS), BLOCKS)
                        if part == 0:
                            x = nat[lane, pl.ds(start + i, BLOCKS, stride=steps), :]
                            xperm_ref[lane, here, :] = x
                        else:
                            x = xperm_ref[lane, here, :]
                        y = None
                        for m in range(half):
                            e[m] = decays[m] * e[m] + h[m]
                            h[m] = decays[m] * h[m] + x
                            term = weights[m] * h[m]
                            y = term if y is None else y + term
                        if part == 1:
                            y = y + yloc_ref[lane, here, :]
                        yloc_ref[lane, here, :] = y
                    return tuple(h), tuple(e)

                zero = (jnp.zeros((BLOCKS, LANES), F32),) * half
                h, e = lax.fori_loop(0, steps // unroll, body, (zero, zero))
                for m in range(half):
                    row = pl.ds(part * half + m, BLOCKS, stride=modes)
                    hb_ref[lane, seg, row, :] = h[m]
                    eb_ref[lane, seg, row, :] = e[m]
        a = a_ref[:, lanes]
        state = jnp.zeros((modes, LANES), F32)
        moment = jnp.zeros((modes, LANES), F32)
        for seg, (start, rows) in enumerate(segments):
            steps = rows // BLOCKS
            power = jnp.exp(-decay_ref[:, lanes] * steps)
            for b in range(BLOCKS):
                rowsb = pl.ds(b * modes, modes)
                moment = power * (moment + steps * state) + a * eb_ref[lane, seg, rowsb, :]
                state = power * state + hb_ref[lane, seg, rowsb, :]
        total_ref[pl.ds(0, modes), lanes] = state
        total_ref[pl.ds(modes, modes), lanes] = moment


def respond_body(segments, modes, hb_ref, eb_ref, yloc_ref, a_ref, r_ref, decay_ref, carry_ref,
                 resp_ref, hin_ref, kin_ref):
    channels = a_ref.shape[1]
    unroll = 4
    for lane in range(channels // LANES):
        lanes = pl.ds(lane * LANES, LANES)
        a = a_ref[:, lanes]
        state = carry_ref[pl.ds(0, modes), lanes]
        moment = carry_ref[pl.ds(modes, modes), lanes]
        for seg, (start, rows) in enumerate(segments):
            steps = rows // BLOCKS
            power = jnp.exp(-decay_ref[:, lanes] * steps)
            for b in range(BLOCKS):
                rowsb = pl.ds(b * modes, modes)
                hin_ref[lane, seg, rowsb, :] = state
                kin_ref[lane, seg, rowsb, :] = moment
                moment = power * (moment + steps * state) + a * eb_ref[lane, seg, rowsb, :]
                state = power * state + hb_ref[lane, seg, rowsb, :]
        decays = [spread(a_ref, m, lanes) for m in range(modes)]
        for seg, (start, rows) in enumerate(segments):
            steps = rows // BLOCKS
            edge = tuple(
                spread(r_ref, m, lanes) * decays[m]
                * hin_ref[lane, seg, pl.ds(m, BLOCKS, stride=modes), :]
                for m in range(modes)
            )

            def body(outer, edge):
                edge = list(edge)
                for q in range(unroll):
                    i = outer * unroll + q
                    here = pl.ds(pl.multiple_of(start + i * BLOCKS, BLOCKS), BLOCKS)
                    y = yloc_ref[lane, here, :]
                    for m in range(modes):
                        y = y + edge[m]
                        edge[m] = edge[m] * decays[m]
                    resp_ref[lane, pl.ds(start + i, BLOCKS, stride=steps), :] = y
                return tuple(edge)

            lax.fori_loop(0, steps // unroll, body, edge)


def adjoint_body(segment, modes, own_ref, recv_ref, x1_ref, resp_ref, xperm_ref, hin_ref, kin_ref,
                 a_ref, r_ref, grad_ref, aloc_ref, gb_ref, sums_ref, nat, uperm, db, rb, mb):
    seg, start, rows = segment
    steps = rows // BLOCKS
    channels = own_ref.shape[1]
    unroll = 4
    half = modes // 2
    for lane in range(channels // LANES):
        lanes = pl.ds(lane * LANES, LANES)
        grad_in = own_ref[:, lanes] + recv_ref[:, lanes].astype(F32)
        window = pl.ds(start, rows)
        grad_ref[:, lanes] = (grad_in * resp_ref[lane, window, :]).astype(BF16)
        nat[lane] = (grad_in * x1_ref[window, lanes].astype(F32)).astype(BF16).astype(F32)
        for part in range(2):
            decays = [spread(a_ref, part * half + m, lanes) for m in range(half)]
            weights = [spread(r_ref, part * half + m, lanes) for m in range(half)]

            def body(outer, carry):
                g, d, racc, macc = (list(item) for item in carry)
                for q in range(unroll):
                    i = steps - 1 - (outer * unroll + q)
                    here = pl.ds(pl.multiple_of(i * BLOCKS, BLOCKS), BLOCKS)
                    if part == 0:
                        u = nat[lane, pl.ds(i, BLOCKS, stride=steps), :]
                        uperm[lane, here, :] = u
                    else:
                        u = uperm[lane, here, :]
                    x = xperm_ref[lane, pl.ds(pl.multiple_of(start + i * BLOCKS, BLOCKS), BLOCKS), :]
                    y = None
                    for m in range(half):
                        d[m] = decays[m] * d[m] + g[m]
                        g[m] = decays[m] * g[m] + u
                        racc[m] = racc[m] + x * g[m]
                        macc[m] = macc[m] + x * d[m]
                        term = weights[m] * g[m]
                        y = term if y is None else y + term
                    if part == 1:
                        y = y + aloc_ref[lane, here, :]
                    aloc_ref[lane, here, :] = y
                return tuple(g), tuple(d), tuple(racc), tuple(macc)

            zero = (jnp.zeros((BLOCKS, LANES), F32),) * half
            g, d, racc, macc = lax.fori_loop(0, steps // unroll, body, (zero,) * 4)
            for m in range(half):
                row = pl.ds(part * half + m, BLOCKS, stride=modes)
                gb_ref[lane, row, :] = g[m]
                db[row, :] = d[m]
                rb[row, :] = racc[m]
                mb[row, :] = macc[m]
        a = a_ref[:, lanes]
        total = jnp.zeros((modes, LANES), F32)
        moment = jnp.zeros((modes, LANES), F32)
        for b in range(BLOCKS):
            rowsb = pl.ds(b * modes, modes)
            hin = hin_ref[lane, seg, rowsb, :]
            ag = a * gb_ref[lane, rowsb, :]
            total = total + rb[rowsb, :] + ag * hin
            moment = moment + a * mb[rowsb, :] + (ag + a * a * db[rowsb, :]) * hin
            moment = moment + ag * kin_ref[lane, seg, rowsb, :]
        sums_ref[pl.ds(0, modes), lanes] = total
        sums_ref[pl.ds(modes, modes), lanes] = moment


def gather_body(segments, modes, *refs):
    count = len(segments)
    gb_refs, sums_refs = refs[:count], refs[count:2 * count]
    decay_ref, out_ref = refs[2 * count:]
    channels = decay_ref.shape[1]
    for lane in range(channels // LANES):
        lanes = pl.ds(lane * LANES, LANES)
        state = jnp.zeros((modes, LANES), F32)
        for seg in reversed(range(count)):
            power = jnp.exp(-decay_ref[:, lanes] * (segments[seg][1] // BLOCKS))
            for b in reversed(range(BLOCKS)):
                state = power * state + gb_refs[seg][lane, pl.ds(b * modes, modes), :]
        out_ref[pl.ds(0, modes), lanes] = state
    out_ref[pl.ds(modes, 2 * modes), :] = sum(ref[...] for ref in sums_refs)


def finish_body(segments, modes, length, index_ref, *refs):
    count = len(segments)
    aloc_refs, gb_refs = refs[:count], refs[count:2 * count]
    (a_ref, r_ref, decay_ref, carry_ref, sums_ref, x2_ref, v_ref,
     gx2_ref, gv_ref, rgrad_ref, dgrad_ref, gin, nat) = refs[2 * count:]
    channels = a_ref.shape[1]
    unroll = 4
    for lane in range(channels // LANES):
        lanes = pl.ds(lane * LANES, LANES)
        decays = [spread(a_ref, m, lanes) for m in range(modes)]
        state = carry_ref[:, lanes]
        for seg in reversed(range(count)):
            start, rows = segments[seg]
            steps = rows // BLOCKS
            power = jnp.exp(-decay_ref[:, lanes] * steps)
            for b in reversed(range(BLOCKS)):
                rowsb = pl.ds(b * modes, modes)
                gin[rowsb, :] = state
                state = power * state + gb_refs[seg][lane, rowsb, :]
            edge = tuple(
                spread(r_ref, m, lanes) * decays[m] * gin[pl.ds(m, BLOCKS, stride=modes), :]
                for m in range(modes)
            )

            def body(outer, edge):
                edge = list(edge)
                for q in range(unroll):
                    i = steps - 1 - (outer * unroll + q)
                    here = pl.ds(pl.multiple_of(i * BLOCKS, BLOCKS), BLOCKS)
                    y = aloc_refs[seg][lane, here, :]
                    for m in range(modes):
                        y = y + edge[m]
                        edge[m] = edge[m] * decays[m]
                    nat[lane, pl.ds(start + i, BLOCKS, stride=steps), :] = y
                return tuple(edge)

            lax.fori_loop(0, steps // unroll, body, edge)
        gx2_ref[:, lanes] = (nat[lane] * v_ref[:, lanes].astype(F32)).astype(BF16)
        gv_ref[:, lanes] = (nat[lane] * x2_ref[:, lanes].astype(F32)).astype(BF16)
    owned = rgrad_ref.shape[0]
    row = lax.broadcasted_iota(jnp.int32, (owned, channels), 0) + index_ref[0] * owned
    column = lax.broadcasted_iota(jnp.int32, (owned, channels), 1)
    pick = (row == column).astype(F32)

    def choose(values):
        return lax.dot_general(
            pick, values, (((1,), (1,)), ((), ())),
            precision=lax.Precision.HIGHEST, preferred_element_type=F32,
        )

    rgrad_ref[...] = choose(sums_ref[pl.ds(0, modes), :]) / length
    scale = r_ref[...] * decay_ref[...] * (float(length) ** 0.5)
    dgrad_ref[...] = -choose(scale * sums_ref[pl.ds(modes, modes), :]) / length


def on_device(g_out, w_out, gate_x1, gate_x2, value_v, residue, decay):
    tokens, channels = gate_x1.shape
    context_size = lax.axis_size("ctx")
    ch_size = lax.axis_size("ch")
    length = tokens * context_size
    modes = residue.shape[1]
    lane_tiles = channels // LANES
    context_index = lax.axis_index("ctx")
    ch_index = lax.axis_index("ch")
    owned = channels // context_size

    bits = [1 << bit for bit in range(ch_size.bit_length() - 1)]
    half_rows = tokens // 2
    chunks = [(0, half_rows, bits), (half_rows, half_rows, bits[::-1])]
    segments = [(start, rows) for start, rows, _ in chunks]
    count = len(chunks)

    sending, keeping = [], []
    for start, rows, order in chunks:
        offsets = halving_layout(order)
        cut = len(offsets) // 2
        which = jnp.array(offsets, jnp.int32) ^ ch_index
        sent = project(which[:cut], g_out, w_out, start, rows, channels, BF16)
        sending.append(lax.ppermute(sent, "ch", xor_pairs(ch_size, order[0])))
        keeping.append((which[cut:], start, rows, order))
    keeping = [
        (project(which, g_out, w_out, start, rows, channels, F32), order)
        for which, start, rows, order in keeping
    ]

    decay_t = decay.T
    residue_t = residue.T
    a = jnp.exp(-decay_t)
    r = residue_t * length ** (-0.5)

    state_shape = jax.ShapeDtypeStruct((lane_tiles, count, BLOCKS * modes, LANES), F32)
    perm_shape = jax.ShapeDtypeStruct((lane_tiles, tokens, LANES), F32)
    work = tokens * channels * modes
    xperm, yloc, hb, eb, total = pl.pallas_call(
        functools.partial(forward_body, segments, modes),
        out_shape=[perm_shape, perm_shape, state_shape, state_shape,
                   jax.ShapeDtypeStruct((2 * modes, channels), F32)],
        scratch_shapes=[pltpu.VMEM((lane_tiles, tokens, LANES), F32)],
        compiler_params=params(),
        cost_estimate=pl.CostEstimate(flops=work * 6, bytes_accessed=tokens * channels * 12, transcendentals=0),
        name="forward",
    )(gate_x2, value_v, a, r, decay_t)

    pair = context_index // 2
    core = context_index % 2
    pairs = context_size // 2
    whole_power = jnp.exp(-decay_t * tokens)

    partner = lax.ppermute(total, "ctx", xor_pairs(context_size, 1))
    first = jnp.where(core == 0, total, partner)
    second = jnp.where(core == 0, partner, total)
    pair_h = second[:modes] + whole_power * first[:modes]
    pair_k = second[modes:] + whole_power * (first[modes:] + tokens * first[:modes])
    both = jnp.concatenate([pair_h, pair_k], 0)
    carry_h = jnp.where(core == 1, first[:modes], 0.0)
    carry_k = jnp.where(core == 1, first[modes:], 0.0)
    for step in range(1, pairs):
        other = pair ^ step
        got = lax.ppermute(both, "ctx", xor_pairs(context_size, 2 * step))
        gap = ((2 * (pair - other - 1) + core) * tokens).astype(F32)
        weight = jnp.where(other < pair, jnp.exp(-decay_t * jnp.maximum(gap, 0.0)), 0.0)
        carry_h = carry_h + weight * got[:modes]
        carry_k = carry_k + weight * (got[modes:] + gap * got[:modes])
    carry = jnp.concatenate([carry_h, carry_k], 0)

    resp, hin, kin = pl.pallas_call(
        functools.partial(respond_body, segments, modes),
        out_shape=[perm_shape, state_shape, state_shape],
        compiler_params=params(),
        cost_estimate=pl.CostEstimate(flops=work * 2, bytes_accessed=tokens * channels * 8, transcendentals=0),
        name="respond",
    )(hb, eb, yloc, a, r, decay_t, carry)

    grads, alocs, gbs, sums = [], [], [], []
    arrived = []
    stages = [(sent, kept, order) for sent, (kept, order) in zip(sending, keeping)]
    for level in range(1, len(bits)):
        following = []
        for sent, kept, order in stages:
            cut = kept.shape[1] // 2
            away = (kept[:, :cut] + sent[:, :cut].astype(F32)).astype(BF16)
            stay = kept[:, cut:] + sent[:, cut:].astype(F32)
            moved = lax.ppermute(away, "ch", xor_pairs(ch_size, order[level]))
            following.append((moved, stay, order))
        stages = following
    for seg, (moved, stay, _) in enumerate(stages):
        start, rows = segments[seg]
        block_shape = jax.ShapeDtypeStruct((lane_tiles, BLOCKS * modes, LANES), F32)
        grad_x1, aloc, gb, partial_sums = pl.pallas_call(
            functools.partial(adjoint_body, (seg, start, rows), modes),
            out_shape=[jax.ShapeDtypeStruct((rows, channels), BF16),
                       jax.ShapeDtypeStruct((lane_tiles, rows, LANES), F32),
                       block_shape,
                       jax.ShapeDtypeStruct((2 * modes, channels), F32)],
            scratch_shapes=[pltpu.VMEM((lane_tiles, rows, LANES), F32)] * 2
            + [pltpu.VMEM((BLOCKS * modes, LANES), F32)] * 3,
            compiler_params=params(),
            cost_estimate=pl.CostEstimate(flops=rows * channels * modes * 10, bytes_accessed=rows * channels * 16, transcendentals=0),
            name="adjoint",
        )(stay, moved, gate_x1, resp, xperm, hin, kin, a, r)
        grads.append(grad_x1)
        alocs.append(aloc)
        gbs.append(gb)
        sums.append(partial_sums)

    message = pl.pallas_call(
        functools.partial(gather_body, segments, modes),
        out_shape=jax.ShapeDtypeStruct((3 * modes, channels), F32),
        compiler_params=params(),
        name="totals",
    )(*gbs, *sums, decay_t)
    partner = lax.ppermute(message, "ctx", xor_pairs(context_size, 1))
    first = jnp.where(core == 0, message[:modes], partner[:modes])
    second = jnp.where(core == 0, partner[:modes], message[:modes])
    both = jnp.concatenate([first + whole_power * second, message[modes:] + partner[modes:]], 0)
    carry_g = jnp.where(core == 0, second, 0.0)
    param_sums = both[modes:]
    for step in range(1, pairs):
        other = pair ^ step
        got = lax.ppermute(both, "ctx", xor_pairs(context_size, 2 * step))
        gap = ((2 * (other - pair - 1) + 1 - core) * tokens).astype(F32)
        weight = jnp.where(other > pair, jnp.exp(-decay_t * jnp.maximum(gap, 0.0)), 0.0)
        carry_g = carry_g + weight * got[:modes]
        param_sums = param_sums + got[modes:]

    vmem = pl.BlockSpec(memory_space=pltpu.VMEM)
    grad_x2, grad_v, residue_grad, decay_grad = pl.pallas_call(
        functools.partial(finish_body, segments, modes, length),
        in_specs=[pl.BlockSpec(memory_space=pltpu.SMEM)] + [vmem] * (2 * count + 7),
        out_specs=[vmem] * 4,
        out_shape=[jax.ShapeDtypeStruct((tokens, channels), BF16)] * 2
        + [jax.ShapeDtypeStruct((owned, modes), F32)] * 2,
        scratch_shapes=[pltpu.VMEM((BLOCKS * modes, LANES), F32),
                        pltpu.VMEM((lane_tiles, tokens, LANES), F32)],
        compiler_params=params(),
        cost_estimate=pl.CostEstimate(flops=work * 2, bytes_accessed=tokens * channels * 12, transcendentals=0),
        name="finish",
    )(context_index.reshape(1), *alocs, *gbs, a, r, decay_t, carry_g, param_sums, gate_x2, value_v)
    return jnp.concatenate(grads, 0), grad_x2, grad_v, residue_grad, decay_grad


def solution(mesh):
    return jax.shard_map(
        on_device,
        mesh=mesh,
        in_specs=(
            P("ctx", "ch"),
            P(None, "ch"),
            P("ctx", "ch"),
            P("ctx", "ch"),
            P("ctx", "ch"),
            P("ch", None),
            P("ch", None),
        ),
        out_specs=(
            P("ctx", "ch"),
            P("ctx", "ch"),
            P("ctx", "ch"),
            P(("ch", "ctx"), None),
            P(("ch", "ctx"), None),
        ),
        check_vma=False,
    )
```

profile of v0, /device:TPU:0, one launch (start us, length us, event | category | flops | bytes accessed | tf_op | source)
XLA Modules:
  0.0 79.5 jit_solution(6242036893344369754)
XLA Ops:
  0.6 0.7 broadcast_xor_fusion
  1.3 0.1 fusion.12
  1.4 2.2 %copy-done = bf16[1024,2048]{1,0:T(8,128)(2,1)S(1)} copy-done((bf16[1024,2048]{1,0:T(8,128)(2,1)S(1)}, bf16[1024,2048]{1,0:T(8,128)(2,1)}, u32[]{:S(2)}) %copy-start) | copy-done | bytes 4194328
  3.6 5.2 %project.7 = bf16[512,512]{1,0:T(8,128)(2,1)} custom-call(s32[2]{0:T(128)S(1)} %get-tuple-element.60.which_ref, bf16[1024,2048]{1,0:T(8,128)(2,1)S(1)} %copy-done, bf16[1024,2048]{1,0:T(8,128)(2,1)} %w_ref.7), custom_call_target="tpu_custom_call" | custom-call | flops 1073741824 | bytes 4194304 | tf_op jit(solution)/shard_map/project/pallas_call | solution.py:52
  8.7 3.0 %collective-permute-start.6 = (bf16[512,512]{1,0:T(8,128)(2,1)}, bf16[512,512]{1,0:T(8,128)(2,1)}, u32[]{:S(2)}, u32[]{:S(2)}) collective-permute-start(bf16[512,512]{1,0:T(8,128)(2,1)} %project.7), channel_id=1, source_target_pairs={{0,2},{1,3},{2,0},{3,1},{4,6},{5,7},{6,4},{7,5},{8,10},{9,11},{10,... | collective-permute-start | bytes 1572872 | tf_op jit(solution)/shard_map/ppermute | solution.py:325
  11.7 0.1 fusion.11
  11.8 5.5 %project.5 = bf16[512,512]{1,0:T(8,128)(2,1)} custom-call(s32[2]{0:T(128)S(1)} %get-tuple-element.58.which_ref, bf16[1024,2048]{1,0:T(8,128)(2,1)S(1)} %copy-done, bf16[1024,2048]{1,0:T(8,128)(2,1)} %w_ref.7), custom_call_target="tpu_custom_call" | custom-call | flops 1073741824 | bytes 4194304 | tf_op jit(solution)/shard_map/project/pallas_call | solution.py:52
  17.3 1.5 %collective-permute-start = (bf16[512,512]{1,0:T(8,128)(2,1)}, bf16[512,512]{1,0:T(8,128)(2,1)}, u32[]{:S(2)}, u32[]{:S(2)}) collective-permute-start(bf16[512,512]{1,0:T(8,128)(2,1)} %project.5), channel_id=1, source_target_pairs={{0,1},{1,0},{2,3},{3,2},{4,5},{5,4},{6,7},{7,6},{8,9},{9,8},{10,11... | collective-permute-start | bytes 1572872 | tf_op jit(solution)/shard_map/ppermute | solution.py:325
  18.8 0.0 copy-done.16
  18.8 0.0 copy-done.8
  18.8 0.0 copy-done.4
  18.8 0.0 copy-done.6
  18.8 5.1 %forward.1 = (f32[2,1024,128]{2,1,0:T(8,128)S(1)}, f32[2,1024,128]{2,1,0:T(8,128)S(1)}, f32[2,2,128,128]{3,2,1,0:T(8,128)S(1)}, f32[2,2,128,128]{3,2,1,0:T(8,128)S(1)}, f32[32,256]{1,0:T(8,128)S(1)}) custom-call(bf16[1024,256]{1,0:T(8,128)(2,1)S(1)} %copy-done.4, bf16[1024,256]{1,0:T(8,128)(2,1)S(1)} %copy-done.6, ...), custom_call_target="tpu_custom_call" | custom-call | flops 25165824 | bytes 3145728 | tf_op jit(solution)/shard_map/forward/pallas_call | solution.py:340
  24.0 0.0 copy-start.9
  24.0 1.0 %copy-done.9 = f32[2,1024,128]{2,1,0:T(8,128)} copy-done((f32[2,1024,128]{2,1,0:T(8,128)}, f32[2,1024,128]{2,1,0:T(8,128)S(1)}, u32[]{:S(2)}) %copy-start.9) | copy-done | bytes 1048600
  24.9 0.7 copy-done.13
  25.6 0.0 collective-permute-start.2
  25.6 0.0 copy-done.1
  25.7 4.5 %project.4 = f32[512,512]{1,0:T(8,128)S(1)} custom-call(s32[2]{0:T(128)S(1)} %get-tuple-element.59.which_ref, bf16[1024,2048]{1,0:T(8,128)(2,1)S(1)} %copy-done.1, bf16[1024,2048]{1,0:T(8,128)(2,1)} %w_ref.7), custom_call_target="tpu_custom_call" | custom-call | flops 1073741824 | bytes 4194304 | tf_op jit(solution)/shard_map/project/pallas_call | solution.py:52
  30.2 0.0 collective-permute-done.2
  30.2 0.6 pad_maximum_fusion.2
  30.9 3.6 %collective-permute-start.5 = (f32[32,256]{1,0:T(8,128)}, f32[32,256]{1,0:T(8,128)S(1)}, u32[]{:S(2)}, u32[]{:S(2)}) collective-permute-start(f32[32,256]{1,0:T(8,128)} %pad_maximum_fusion.2), channel_id=1, source_target_pairs={{0,24},{4,28},{8,16},{12,20},{16,8},{20,12},{24,0},{28,4},{1,25},{... | collective-permute-start | bytes 98312 | tf_op jit(solution)/shard_map/ppermute | solution.py:365
  34.5 0.0 collective-permute-start.4
  34.5 0.8 collective-permute-start.3
  35.3 2.2 %copy-done.2 = bf16[1024,2048]{1,0:T(8,128)(2,1)S(1)} copy-done((bf16[1024,2048]{1,0:T(8,128)(2,1)S(1)}, bf16[1024,2048]{1,0:T(8,128)(2,1)}, u32[]{:S(2)}) %copy-start.2) | copy-done | bytes 4194328
  37.4 4.5 %project.6 = f32[512,512]{1,0:T(8,128)S(1)} custom-call(s32[2]{0:T(128)S(1)} %get-tuple-element.61.which_ref, bf16[1024,2048]{1,0:T(8,128)(2,1)S(1)} %copy-done.2, bf16[1024,2048]{1,0:T(8,128)(2,1)} %w_ref.7), custom_call_target="tpu_custom_call" | custom-call | flops 1073741824 | bytes 4194304 | tf_op jit(solution)/shard_map/project/pallas_call | solution.py:52
  42.0 0.0 copy-start.10
  42.0 0.0 copy-start.14
  42.0 0.0 copy-start.3
  42.1 0.0 collective-permute-done.5
  42.1 0.0 collective-permute-done.4
  42.1 0.0 collective-permute-done.3
  42.1 0.9 %fusion.6 = f32[16,256]{1,0:T(8,128)S(1)} fusion(f32[32,256]{1,0:T(8,128)S(1)} %collective-permute-done.5, f32[32,256]{1,0:T(8,128)} %collective-permute-done.4, f32[32,256]{1,0:T(8,128)} %collective-permute-done.3, f32[32,256]{1,0:T(8,128)S(1)} %get-tuple-element.56, f32[]{:T(128)S(6)} %convert_element_type.41, f32[]{:T(128)S(6)} %convert_element_type.40, ...), kind=kLoop, calls=%fused_computation.22 | loop fusion | flops 81920 | bytes 147484 | tf_op jit(solution)/shard_map/add | solution.py:369
  43.0 0.0 collective-permute-done
  43.0 1.1 %fusion.1 = (bf16[512,256]{1,0:T(8,128)(2,1)S(1)}, f32[512,256]{1,0:T(8,128)S(1)}) fusion(f32[512,512]{1,0:T(8,128)S(1)} %project.4, bf16[512,512]{1,0:T(8,128)(2,1)} %collective-permute-done), kind=kLoop, calls=%fused_computation.4 | loop fusion | flops 655360 | bytes 2359296 | tf_op jit(solution)/shard_map/convert_element_type | solution.py:387
  44.2 0.6 collective-permute-start.1
  44.7 0.0 collective-permute-done.6
  44.7 1.1 %fusion = (bf16[512,256]{1,0:T(8,128)(2,1)S(1)}, f32[512,256]{1,0:T(8,128)S(1)}) fusion(f32[512,512]{1,0:T(8,128)S(1)} %project.6, bf16[512,512]{1,0:T(8,128)(2,1)} %collective-permute-done.6), kind=kLoop, calls=%fused_computation.1 | loop fusion | flops 655360 | bytes 2359296 | tf_op jit(solution)/shard_map/convert_element_type | solution.py:387
  45.9 0.4 collective-permute-start.7
  46.2 0.8 multiply_add_fusion.1
  47.0 0.0 copy-done.10
  47.0 2.2 %respond.1 = (f32[2,1024,128]{2,1,0:T(8,128)S(1)}, f32[2,2,128,128]{3,2,1,0:T(8,128)S(1)}, f32[2,2,128,128]{3,2,1,0:T(8,128)S(1)}) custom-call(f32[2,2,128,128]{3,2,1,0:T(8,128)S(1)} %get-tuple-element.25.hb_ref, f32[2,2,128,128]{3,2,1,0:T(8,128)S(1)} %copy-done.14, f32[2,1024,128]{2,1,0:T(8,128)S(1)} %copy-done.10, ...), custom_call_target="tpu_custom_call" | custom-call | flops 8388608 | bytes 2097152 | tf_op jit(solution)/shard_map/respond/pallas_call | solution.py:372
  49.2 4.4 %collective-permute-done.7.recv_ref = bf16[512,256]{1,0:T(8,128)(2,1)S(1)} collective-permute-done((bf16[512,256]{1,0:T(8,128)(2,1)S(1)}, bf16[512,256]{1,0:T(8,128)(2,1)S(1)}, u32[]{:S(2)}, u32[]{:S(2)}) %collective-permute-start.7) | collective-permute-done | bytes 262176 | tf_op jit(solution)/shard_map/ppermute | solution.py:389
  53.6 0.0 copy-done.3
  53.6 4.2 %adjoint.3 = (bf16[512,256]{1,0:T(8,128)(2,1)S(1)}, f32[2,512,128]{2,1,0:T(8,128)S(1)}, f32[2,128,128]{2,1,0:T(8,128)S(1)}, f32[32,256]{1,0:T(8,128)S(1)}) custom-call(f32[512,256]{1,0:T(8,128)S(1)} %get-tuple-element.53.own_ref, bf16[512,256]{1,0:T(8,128)(2,1)S(1)} %collective-permute-done.7.recv_ref, bf16[1024,256]{1,0:T(8,128)(2,1)S(1)} %copy-done.3, ...), custom_call_target="tpu_custom_call" | custom-call | flops 20971520 | bytes 2097152 | tf_op jit(solution)/shard_map/adjoint/pallas_call | solution.py:395
  57.8 0.0 collective-permute-done.1.recv_ref
  57.8 4.2 %adjoint.2 = (bf16[512,256]{1,0:T(8,128)(2,1)S(1)}, f32[2,512,128]{2,1,0:T(8,128)S(1)}, f32[2,128,128]{2,1,0:T(8,128)S(1)}, f32[32,256]{1,0:T(8,128)S(1)}) custom-call(f32[512,256]{1,0:T(8,128)S(1)} %get-tuple-element.51.own_ref, bf16[512,256]{1,0:T(8,128)(2,1)S(1)} %collective-permute-done.1.recv_ref, bf16[1024,256]{1,0:T(8,128)(2,1)S(1)} %copy-done.3, ...), custom_call_target="tpu_custom_call" | custom-call | flops 20971520 | bytes 2097152 | tf_op jit(solution)/shard_map/adjoint/pallas_call | solution.py:395
  62.0 0.0 copy-start.11
  62.0 0.8 copy-done.11
  62.8 0.7 copy-done.15
  63.5 0.1 collective-permute-start.8
  63.6 1.2 %collective-permute-done.8 = f32[48,256]{1,0:T(8,128)S(1)} collective-permute-done((f32[48,256]{1,0:T(8,128)S(1)}, f32[48,256]{1,0:T(8,128)S(1)}, u32[]{:S(2)}, u32[]{:S(2)}) %collective-permute-start.8) | collective-permute-done | bytes 49184 | tf_op jit(solution)/shard_map/ppermute | solution.py:418
  64.9 3.6 %collective-permute-start.11 = (f32[48,256]{1,0:T(8,128)S(1)}, f32[48,256]{1,0:T(8,128)S(1)}, u32[]{:S(2)}, u32[]{:S(2)}) collective-permute-start(f32[48,256]{1,0:T(8,128)S(1)} %pad_maximum_fusion.1), channel_id=1, source_target_pairs={{0,24},{4,28},{8,16},{12,20},{16,8},{20,12},{24,0},{28,4},{1,25},{... | collective-permute-start | bytes 147464 | tf_op jit(solution)/shard_map/ppermute | solution.py:426
  68.5 0.0 collective-permute-start.10
  68.5 0.8 %collective-permute-start.9 = (f32[48,256]{1,0:T(8,128)S(1)}, f32[48,256]{1,0:T(8,128)S(1)}, u32[]{:S(2)}, u32[]{:S(2)}) collective-permute-start(f32[48,256]{1,0:T(8,128)S(1)} %pad_maximum_fusion.1), channel_id=1, source_target_pairs={{0,8},{4,12},{8,0},{12,4},{16,24},{20,28},{24,16},{28,20},{1,9},{5... | collective-permute-start | bytes 147464 | tf_op jit(solution)/shard_map/ppermute | solution.py:426
  69.3 1.8 %pad_maximum_fusion = bf16[1024,256]{1,0:T(8,128)(2,1)} fusion(bf16[512,256]{1,0:T(8,128)(2,1)S(1)} %get-tuple-element.34, bf16[512,256]{1,0:T(8,128)(2,1)} %copy-done.15), kind=kLoop, calls=%fused_computation.6 | loop fusion | flops 1048576 | bytes 1048576 | tf_op jit(solution)/shard_map/concatenate | solution.py:445
  71.1 0.0 collective-permute-done.11
  71.1 2.4 %collective-permute-done.10 = f32[48,256]{1,0:T(8,128)S(1)} collective-permute-done((f32[48,256]{1,0:T(8,128)S(1)}, f32[48,256]{1,0:T(8,128)S(1)}, u32[]{:S(2)}, u32[]{:S(2)}) %collective-permute-start.10) | collective-permute-done | bytes 49184 | tf_op jit(solution)/shard_map/ppermute | solution.py:426
  73.5 0.1 collective-permute-done.9
  73.7 0.0 copy-start.12
  73.7 1.0 %copy-done.12 = f32[2,512,128]{2,1,0:T(8,128)S(1)} copy-done((f32[2,512,128]{2,1,0:T(8,128)S(1)}, f32[2,512,128]{2,1,0:T(8,128)}, u32[]{:S(2)}) %copy-start.12) | copy-done | bytes 524312
  74.7 3.5 %finish.1 = (bf16[1024,256]{1,0:T(8,128)(2,1)}, bf16[1024,256]{1,0:T(8,128)(2,1)}, f32[32,16]{1,0:T(8,128)S(1)}, f32[32,16]{1,0:T(8,128)S(1)}) custom-call(s32[1]{0:T(128)} %bitcast.2.index_ref, f32[2,512,128]{2,1,0:T(8,128)S(1)} %copy-done.12, f32[2,512,128]{2,1,0:T(8,128)S(1)} %get-tuple-element.36.refs_1_, ...), custom_call_target="tpu_custom_call" | custom-call | flops 8388608 | bytes 3145728 | tf_op jit(solution)/shard_map/finish/pallas_call | solution.py:433
  78.2 0.7 copy.14
  78.9 0.7 copy.15
  (25 shorter events, 0.2 us)
Async XLA Ops:
  1.4 2.2 %copy-start = (bf16[1024,2048]{1,0:T(8,128)(2,1)S(1)}, bf16[1024,2048]{1,0:T(8,128)(2,1)}, u32[]{:S(2)}) copy-start(bf16[1024,2048]{1,0:T(8,128)(2,1)} %g_ref.7) | copy-start | bytes 12582916
  8.7 36.0 %collective-permute-start.6 = (bf16[512,512]{1,0:T(8,128)(2,1)}, bf16[512,512]{1,0:T(8,128)(2,1)}, u32[]{:S(2)}, u32[]{:S(2)}) collective-permute-start(bf16[512,512]{1,0:T(8,128)(2,1)} %project.7), channel_id=1, source_target_pairs={{0,2},{1,3},{2,0},{3,1},{4,6},{5,7},{6,4},{7,5},{8,10},{9,11},{10,... | collective-permute-start | bytes 1572872 | tf_op jit(solution)/shard_map/ppermute | solution.py:325
  11.8 7.0 %copy-start.16 = (f32[256,16]{0,1:T(8,128)S(1)}, f32[256,16]{0,1:T(8,128)}, u32[]{:S(2)}) copy-start(f32[256,16]{0,1:T(8,128)} %param.14) | copy-start | bytes 49156
  11.8 7.0 %copy-start.8 = (f32[256,16]{0,1:T(8,128)S(1)}, f32[256,16]{0,1:T(8,128)}, u32[]{:S(2)}) copy-start(f32[256,16]{0,1:T(8,128)} %param.15) | copy-start | bytes 49156
  11.8 7.0 %copy-start.4 = (bf16[1024,256]{1,0:T(8,128)(2,1)S(1)}, bf16[1024,256]{1,0:T(8,128)(2,1)}, u32[]{:S(2)}) copy-start(bf16[1024,256]{1,0:T(8,128)(2,1)} %refs_9_.1) | copy-start | bytes 1572868
  11.8 7.0 %copy-start.6 = (bf16[1024,256]{1,0:T(8,128)(2,1)S(1)}, bf16[1024,256]{1,0:T(8,128)(2,1)}, u32[]{:S(2)}) copy-start(bf16[1024,256]{1,0:T(8,128)(2,1)} %refs_10_.1) | copy-start | bytes 1572868
  11.8 13.9 %copy-start.1 = (bf16[1024,2048]{1,0:T(8,128)(2,1)S(1)}, bf16[1024,2048]{1,0:T(8,128)(2,1)}, u32[]{:S(2)}) copy-start(bf16[1024,2048]{1,0:T(8,128)(2,1)} %g_ref.7) | copy-start | bytes 12582916
  17.3 25.7 %collective-permute-start = (bf16[512,512]{1,0:T(8,128)(2,1)}, bf16[512,512]{1,0:T(8,128)(2,1)}, u32[]{:S(2)}, u32[]{:S(2)}) collective-permute-start(bf16[512,512]{1,0:T(8,128)(2,1)} %project.5), channel_id=1, source_target_pairs={{0,1},{1,0},{2,3},{3,2},{4,5},{5,4},{6,7},{7,6},{8,9},{9,8},{10,11... | collective-permute-start | bytes 1572872 | tf_op jit(solution)/shard_map/ppermute | solution.py:325
  24.0 1.0 %copy-start.9 = (f32[2,1024,128]{2,1,0:T(8,128)}, f32[2,1024,128]{2,1,0:T(8,128)S(1)}, u32[]{:S(2)}) copy-start(f32[2,1024,128]{2,1,0:T(8,128)S(1)} %get-tuple-element.27.yloc_ref) | copy-start | bytes 3145732
  24.9 0.7 copy-start.13
  25.6 4.6 %collective-permute-start.2 = (f32[32,256]{1,0:T(8,128)S(1)}, f32[32,256]{1,0:T(8,128)S(1)}, u32[]{:S(2)}, u32[]{:S(2)}) collective-permute-start(f32[32,256]{1,0:T(8,128)S(1)} %get-tuple-element.28), channel_id=1, source_target_pairs={{0,4},{4,0},{8,12},{12,8},{16,20},{20,16},{24,28},{28,24},{1,5},{5... | collective-permute-start | bytes 98312 | tf_op jit(solution)/shard_map/ppermute | solution.py:355
  30.9 11.2 %collective-permute-start.5 = (f32[32,256]{1,0:T(8,128)}, f32[32,256]{1,0:T(8,128)S(1)}, u32[]{:S(2)}, u32[]{:S(2)}) collective-permute-start(f32[32,256]{1,0:T(8,128)} %pad_maximum_fusion.2), channel_id=1, source_target_pairs={{0,24},{4,28},{8,16},{12,20},{16,8},{20,12},{24,0},{28,4},{1,25},{... | collective-permute-start | bytes 98312 | tf_op jit(solution)/shard_map/ppermute | solution.py:365
  34.5 7.6 %collective-permute-start.4 = (f32[32,256]{1,0:T(8,128)}, f32[32,256]{1,0:T(8,128)}, u32[]{:S(2)}, u32[]{:S(2)}) collective-permute-start(f32[32,256]{1,0:T(8,128)} %pad_maximum_fusion.2), channel_id=1, source_target_pairs={{0,16},{4,20},{8,24},{12,28},{16,0},{20,4},{24,8},{28,12},{1,17},{... | collective-permute-start | bytes 98312 | tf_op jit(solution)/shard_map/ppermute | solution.py:365
  34.5 7.6 %collective-permute-start.3 = (f32[32,256]{1,0:T(8,128)}, f32[32,256]{1,0:T(8,128)}, u32[]{:S(2)}, u32[]{:S(2)}) collective-permute-start(f32[32,256]{1,0:T(8,128)} %pad_maximum_fusion.2), channel_id=1, source_target_pairs={{0,8},{4,12},{8,0},{12,4},{16,24},{20,28},{24,16},{28,20},{1,9},{5... | collective-permute-start | bytes 98312 | tf_op jit(solution)/shard_map/ppermute | solution.py:365
  35.3 2.2 %copy-start.2 = (bf16[1024,2048]{1,0:T(8,128)(2,1)S(1)}, bf16[1024,2048]{1,0:T(8,128)(2,1)}, u32[]{:S(2)}) copy-start(bf16[1024,2048]{1,0:T(8,128)(2,1)} %g_ref.7) | copy-start | bytes 12582916
  42.0 5.0 %copy-start.10 = (f32[2,1024,128]{2,1,0:T(8,128)S(1)}, f32[2,1024,128]{2,1,0:T(8,128)}, u32[]{:S(2)}) copy-start(f32[2,1024,128]{2,1,0:T(8,128)} %copy-done.9) | copy-start | bytes 3145732
  42.0 5.0 %copy-start.14 = (f32[2,2,128,128]{3,2,1,0:T(8,128)S(1)}, f32[2,2,128,128]{3,2,1,0:T(8,128)}, u32[]{:S(2)}) copy-start(f32[2,2,128,128]{3,2,1,0:T(8,128)} %copy-done.13) | copy-start | bytes 786436
  42.0 11.6 %copy-start.3 = (bf16[1024,256]{1,0:T(8,128)(2,1)S(1)}, bf16[1024,256]{1,0:T(8,128)(2,1)}, u32[]{:S(2)}) copy-start(bf16[1024,256]{1,0:T(8,128)(2,1)} %x1_ref.3) | copy-start | bytes 1572868
  44.2 13.6 %collective-permute-start.1 = (bf16[512,256]{1,0:T(8,128)(2,1)S(1)}, bf16[512,256]{1,0:T(8,128)(2,1)S(1)}, u32[]{:S(2)}, u32[]{:S(2)}) collective-permute-start(bf16[512,256]{1,0:T(8,128)(2,1)S(1)} %get-tuple-element.50), channel_id=1, source_target_pairs={{0,2},{1,3},{2,0},{3,1},{4,6},{5,7},{6,4},{7,5},{8,10},{9,11},{10,... | collective-permute-start | bytes 786440 | tf_op jit(solution)/shard_map/ppermute | solution.py:389
  45.9 7.7 %collective-permute-start.7 = (bf16[512,256]{1,0:T(8,128)(2,1)S(1)}, bf16[512,256]{1,0:T(8,128)(2,1)S(1)}, u32[]{:S(2)}, u32[]{:S(2)}) collective-permute-start(bf16[512,256]{1,0:T(8,128)(2,1)S(1)} %get-tuple-element.52), channel_id=1, source_target_pairs={{0,1},{1,0},{2,3},{3,2},{4,5},{5,4},{6,7},{7,6},{8,9},{9,8},{10,11... | collective-permute-start | bytes 786440 | tf_op jit(solution)/shard_map/ppermute | solution.py:389
  53.6 20.1 %copy-start.5 = (bf16[1024,256]{1,0:T(8,128)(2,1)S(1)}, bf16[1024,256]{1,0:T(8,128)(2,1)}, u32[]{:S(2)}) copy-start(bf16[1024,256]{1,0:T(8,128)(2,1)} %refs_9_.1) | copy-start | bytes 1572868
  53.6 20.1 %copy-start.7 = (bf16[1024,256]{1,0:T(8,128)(2,1)S(1)}, bf16[1024,256]{1,0:T(8,128)(2,1)}, u32[]{:S(2)}) copy-start(bf16[1024,256]{1,0:T(8,128)(2,1)} %refs_10_.1) | copy-start | bytes 1572868
  62.0 0.8 %copy-start.11 = (f32[2,512,128]{2,1,0:T(8,128)}, f32[2,512,128]{2,1,0:T(8,128)S(1)}, u32[]{:S(2)}) copy-start(f32[2,512,128]{2,1,0:T(8,128)S(1)} %get-tuple-element.35.refs_0_) | copy-start | bytes 1572868
  62.8 0.7 copy-start.15
  63.5 1.3 %collective-permute-start.8 = (f32[48,256]{1,0:T(8,128)S(1)}, f32[48,256]{1,0:T(8,128)S(1)}, u32[]{:S(2)}, u32[]{:S(2)}) collective-permute-start(f32[48,256]{1,0:T(8,128)S(1)} %totals.1), channel_id=1, source_target_pairs={{0,4},{4,0},{8,12},{12,8},{16,20},{20,16},{24,28},{28,24},{1,5},{5... | collective-permute-start | bytes 147464 | tf_op jit(solution)/shard_map/ppermute | solution.py:418
  64.9 6.2 %collective-permute-start.11 = (f32[48,256]{1,0:T(8,128)S(1)}, f32[48,256]{1,0:T(8,128)S(1)}, u32[]{:S(2)}, u32[]{:S(2)}) collective-permute-start(f32[48,256]{1,0:T(8,128)S(1)} %pad_maximum_fusion.1), channel_id=1, source_target_pairs={{0,24},{4,28},{8,16},{12,20},{16,8},{20,12},{24,0},{28,4},{1,25},{... | collective-permute-start | bytes 147464 | tf_op jit(solution)/shard_map/ppermute | solution.py:426
  68.5 5.0 %collective-permute-start.10 = (f32[48,256]{1,0:T(8,128)S(1)}, f32[48,256]{1,0:T(8,128)S(1)}, u32[]{:S(2)}, u32[]{:S(2)}) collective-permute-start(f32[48,256]{1,0:T(8,128)S(1)} %pad_maximum_fusion.1), channel_id=1, source_target_pairs={{0,16},{4,20},{8,24},{12,28},{16,0},{20,4},{24,8},{28,12},{1,17},{... | collective-permute-start | bytes 147464 | tf_op jit(solution)/shard_map/ppermute | solution.py:426
  68.5 5.1 %collective-permute-start.9 = (f32[48,256]{1,0:T(8,128)S(1)}, f32[48,256]{1,0:T(8,128)S(1)}, u32[]{:S(2)}, u32[]{:S(2)}) collective-permute-start(f32[48,256]{1,0:T(8,128)S(1)} %pad_maximum_fusion.1), channel_id=1, source_target_pairs={{0,8},{4,12},{8,0},{12,4},{16,24},{20,28},{24,16},{28,20},{1,9},{5... | collective-permute-start | bytes 147464 | tf_op jit(solution)/shard_map/ppermute | solution.py:426
  73.7 1.0 %copy-start.12 = (f32[2,512,128]{2,1,0:T(8,128)S(1)}, f32[2,512,128]{2,1,0:T(8,128)}, u32[]{:S(2)}) copy-start(f32[2,512,128]{2,1,0:T(8,128)} %copy-done.11) | copy-start | bytes 1572868
where the time goes:
time: 80.2 us; the launch traced here: 79.5 us
  Pallas kernels  38.9 us (49%)
  starting transfers between devices  14.3 us (18%)
  local copies, waits for them, and re-layouts  10.1 us (13%)
  waiting for transfers between devices  8.09 us (10%)
  other arithmetic  7.13 us (9%)
  between operations  1.04 us (1%)
    pallas_call x4, Pallas kernels, project(): pl.pallas_call(project_body, grid_spec=spec, out_shape=jax.ShapeDtypeStru...  19.7 us
    unnamed x36, local copies, waits for them, and re-layouts  9.95 us
    ppermute x6, starting transfers between devices, on_device(): got = lax.ppermute(both, 'ctx', xor_pairs(context_size, 2 * step))  8.84 us
    pallas_call x2, Pallas kernels, on_device(): pl.pallas_call(functools.partial(adjoint_body, (seg, start, rows), modes)...  8.35 us
    pallas_call x1, Pallas kernels, on_device(): pl.pallas_call(functools.partial(forward_body, segments, modes), out_shap...  5.14 us
    ppermute x2, starting transfers between devices, on_device(): sending.append(lax.ppermute(sent, 'ch', xor_pairs(ch_size, order[0])))  4.46 us
    ppermute x2, waiting for transfers between devices, on_device(): moved = lax.ppermute(away, 'ch', xor_pairs(ch_size, order[level]))  4.37 us
    pallas_call x1, Pallas kernels, on_device(): pl.pallas_call(functools.partial(finish_body, segments, modes, length), i...  3.46 us
  transfers between devices with their start and end apart: 12, of which 4 were waited for; matrix products, arithmetic and copies ran while one was open for 8% of the time, Pallas kernels for 33%

commit v1 on v0

--- a/solution.py
+++ b/solution.py
@@ -8,6 +8,7 @@
 from jax.sharding import PartitionSpec as P
 
 LANES = 128
+PIECES = 2
 BLOCKS = 8
 F32 = jnp.float32
 BF16 = jnp.bfloat16
@@ -24,43 +25,89 @@
     return [(index, index ^ step) for index in range(count)]
 
 
-def params(vmem=48 * 2**20):
-    return pltpu.CompilerParams(vmem_limit_bytes=vmem)
-
-
-def project_body(which_ref, g_ref, w_ref, out_ref):
-    out_ref[...] = lax.dot_general(
-        g_ref[...], w_ref[...], (((1,), (1,)), ((), ())), preferred_element_type=F32
-    ).astype(out_ref.dtype)
-
-
-def project(which, g_out, w_out, start, rows, width, dtype):
-    depth = g_out.shape[1]
-    count = which.shape[0]
-    tile = min(rows, 256)
-    tiles = rows // tile
-    first = start // tile
-    spec = pltpu.PrefetchScalarGridSpec(
-        num_scalar_prefetch=1,
-        grid=(count, tiles),
-        in_specs=[
-            pl.BlockSpec((tile, depth), lambda j, i, s: (first + i, 0)),
-            pl.BlockSpec((width, depth), lambda j, i, s: (s[j], 0)),
+HBM = pltpu.MemorySpace.HBM
+VMEM = pltpu.MemorySpace.VMEM
+CONTRACT_LAST = (((1,), (1,)), ((), ()))
+
+
+def params(mebibytes=24):
+    return pltpu.CompilerParams(vmem_limit_bytes=mebibytes * 2**20)
+
+
+def in_vmem(count):
+    return [pl.BlockSpec(memory_space=VMEM)] * count
+
+
+def block_rows(offset, width):
+    block = lax.axis_index("ch") ^ offset
+    return pl.ds(pl.multiple_of(block * width, width), width)
+
+
+def project_body(work, width, pieces, g_ref, w_ref, *refs):
+    count = len(work)
+    out_refs = refs[:count]
+    g_here, w_here, total, g_sems, w_sems = refs[count:]
+    depth = g_ref.shape[1] // pieces
+    pending = {}
+
+    def g_copy(rows, piece):
+        columns = pl.ds(piece * depth, depth)
+        return pltpu.make_async_copy(
+            g_ref.at[rows, columns], g_here.at[rows, columns], g_sems.at[rows.start // rows.size, piece])
+
+    def w_copy(offset, piece):
+        columns = pl.ds(piece * depth, depth)
+        here = block_rows(offset, width)
+        return pltpu.make_async_copy(
+            w_ref.at[here, columns], w_here.at[here, columns], w_sems.at[offset, piece])
+
+    for start, rows, offsets in work:
+        for piece in range(pieces):
+            for key, copy in [((start, piece), lambda: g_copy(pl.ds(start, rows), piece))] + [
+                    ((-1 - offset, piece), functools.partial(w_copy, offset, piece)) for offset in offsets]:
+                if key not in pending:
+                    pending[key] = copy()
+                    pending[key].start()
+    for (start, rows, offsets), out_ref in zip(work, out_refs):
+        for piece in range(pieces):
+            columns = pl.ds(piece * depth, depth)
+            for key in [(start, piece)] + [(-1 - offset, piece) for offset in offsets]:
+                copy = pending.pop(key, None)
+                if copy is not None:
+                    copy.wait()
+            for j, offset in enumerate(offsets):
+                here = pl.ds(j * width, width)
+                product = lax.dot_general(
+                    g_here[pl.ds(start, rows), columns], w_here[block_rows(offset, width), columns],
+                    CONTRACT_LAST, preferred_element_type=F32)
+                if piece > 0:
+                    product = product + total[:, here]
+                if piece < pieces - 1:
+                    total[:, here] = product
+                else:
+                    out_ref[:, here] = product.astype(out_ref.dtype)
+
+
+def project(g_out, w_out, work, width):
+    blocks = w_out.shape[0] // width
+    pieces = PIECES
+    shapes = [jax.ShapeDtypeStruct((rows, len(offsets) * width), BF16) for _, rows, offsets in work]
+    groups = g_out.shape[0] // work[0][1]
+    return pl.pallas_call(
+        functools.partial(project_body, work, width, pieces),
+        in_specs=[pl.BlockSpec(memory_space=HBM)] * 2,
+        out_specs=in_vmem(len(work)),
+        out_shape=shapes,
+        scratch_shapes=[
+            pltpu.VMEM(g_out.shape, BF16),
+            pltpu.VMEM(w_out.shape, BF16),
+            pltpu.VMEM(shapes[0].shape, F32),
+            pltpu.SemaphoreType.DMA((groups, pieces)),
+            pltpu.SemaphoreType.DMA((blocks, pieces)),
         ],
-        out_specs=pl.BlockSpec((tile, width), lambda j, i, s: (i, j)),
-    )
-    return pl.pallas_call(
-        project_body,
-        grid_spec=spec,
-        out_shape=jax.ShapeDtypeStruct((rows, count * width), dtype),
-        compiler_params=params(),
-        cost_estimate=pl.CostEstimate(
-            flops=2 * rows * depth * count * width,
-            bytes_accessed=2 * depth * (rows + count * width),
-            transcendentals=0,
-        ),
+        compiler_params=params(60),
         name="project",
-    )(which, g_out, w_out)
+    )(g_out, w_out)
 
 
 def spread(ref, row, lanes):
@@ -123,15 +170,41 @@
         total_ref[pl.ds(modes, modes), lanes] = moment
 
 
-def respond_body(segments, modes, hb_ref, eb_ref, yloc_ref, a_ref, r_ref, decay_ref, carry_ref,
-                 resp_ref, hin_ref, kin_ref):
+def place():
+    index = lax.axis_index("ctx")
+    return index // 2, index % 2
+
+
+def forward_pair_body(modes, tokens, total_ref, partner_ref, decay_ref, both_ref):
+    _, core = place()
+    state, moment = pl.ds(0, modes), pl.ds(modes, modes)
+    power = jnp.exp(-decay_ref[...] * tokens)
+    later = core == 1
+    first_h = jnp.where(later, partner_ref[state, :], total_ref[state, :])
+    first_k = jnp.where(later, partner_ref[moment, :], total_ref[moment, :])
+    second_h = jnp.where(later, total_ref[state, :], partner_ref[state, :])
+    second_k = jnp.where(later, total_ref[moment, :], partner_ref[moment, :])
+    both_ref[state, :] = second_h + power * first_h
+    both_ref[moment, :] = second_k + power * (first_k + tokens * first_h)
+
+
+def respond_body(segments, modes, tokens, hb_ref, eb_ref, yloc_ref, a_ref, r_ref, decay_ref, partner_ref, *refs):
+    got_refs, (resp_ref, hin_ref, kin_ref) = refs[:-3], refs[-3:]
+    pair, core = place()
     channels = a_ref.shape[1]
     unroll = 4
     for lane in range(channels // LANES):
         lanes = pl.ds(lane * LANES, LANES)
         a = a_ref[:, lanes]
-        state = carry_ref[pl.ds(0, modes), lanes]
-        moment = carry_ref[pl.ds(modes, modes), lanes]
+        state = jnp.where(core == 1, partner_ref[pl.ds(0, modes), lanes], 0.0)
+        moment = jnp.where(core == 1, partner_ref[pl.ds(modes, modes), lanes], 0.0)
+        for step, got_ref in enumerate(got_refs, 1):
+            other = pair ^ step
+            gap = jnp.maximum((2 * (pair - other - 1) + core) * tokens, 0).astype(F32)
+            weight = jnp.where(other < pair, jnp.exp(-decay_ref[:, lanes] * gap), 0.0)
+            got = got_ref[pl.ds(0, modes), lanes]
+            state = state + weight * got
+            moment = moment + weight * (got_ref[pl.ds(modes, modes), lanes] + gap * got)
         for seg, (start, rows) in enumerate(segments):
             steps = rows // BLOCKS
             power = jnp.exp(-decay_ref[:, lanes] * steps)
@@ -165,19 +238,32 @@
             lax.fori_loop(0, steps // unroll, body, edge)
 
 
-def adjoint_body(segment, modes, own_ref, recv_ref, x1_ref, resp_ref, xperm_ref, hin_ref, kin_ref,
-                 a_ref, r_ref, grad_ref, aloc_ref, gb_ref, sums_ref, nat, uperm, db, rb, mb):
+def adjoint_body(segment, modes, received, has_previous, kept_ref, *refs):
     seg, start, rows = segment
+    recv_refs = refs[:received]
+    refs = refs[received + has_previous:]
+    (x1_ref, resp_ref, xperm_ref, hin_ref, kin_ref, a_ref, r_ref,
+     grad_ref, aloc_ref, gb_ref, sums_ref, nat, uperm, db, rb, mb, grad_here, sem) = refs
     steps = rows // BLOCKS
-    channels = own_ref.shape[1]
+    channels = x1_ref.shape[1]
     unroll = 4
     half = modes // 2
+    window = pl.ds(start, rows)
     for lane in range(channels // LANES):
         lanes = pl.ds(lane * LANES, LANES)
-        grad_in = own_ref[:, lanes] + recv_ref[:, lanes].astype(F32)
-        window = pl.ds(start, rows)
-        grad_ref[:, lanes] = (grad_in * resp_ref[lane, window, :]).astype(BF16)
+
+        def own(ref):
+            return ref[:, pl.ds(ref.shape[1] - channels + lane * LANES, LANES)]
+
+        grad_in = own(kept_ref).astype(F32)
+        for recv_ref in recv_refs:
+            grad_in = grad_in + own(recv_ref).astype(F32)
+        grad_here[:, lanes] = (grad_in * resp_ref[lane, window, :]).astype(BF16)
         nat[lane] = (grad_in * x1_ref[window, lanes].astype(F32)).astype(BF16).astype(F32)
+    copy = pltpu.make_async_copy(grad_here, grad_ref.at[window, :], sem)
+    copy.start()
+    for lane in range(channels // LANES):
+        lanes = pl.ds(lane * LANES, LANES)
         for part in range(2):
             decays = [spread(a_ref, part * half + m, lanes) for m in range(half)]
             weights = [spread(r_ref, part * half + m, lanes) for m in range(half)]
@@ -226,6 +312,7 @@
             moment = moment + ag * kin_ref[lane, seg, rowsb, :]
         sums_ref[pl.ds(0, modes), lanes] = total
         sums_ref[pl.ds(modes, modes), lanes] = moment
+    copy.wait()
 
 
 def gather_body(segments, modes, *refs):
@@ -244,25 +331,49 @@
     out_ref[pl.ds(modes, 2 * modes), :] = sum(ref[...] for ref in sums_refs)
 
 
-def finish_body(segments, modes, length, index_ref, *refs):
+def backward_pair_body(modes, tokens, message_ref, partner_ref, decay_ref, both_ref):
+    _, core = place()
+    state, sums = pl.ds(0, modes), pl.ds(modes, 2 * modes)
+    first = jnp.where(core == 0, message_ref[state, :], partner_ref[state, :])
+    second = jnp.where(core == 0, partner_ref[state, :], message_ref[state, :])
+    both_ref[state, :] = first + jnp.exp(-decay_ref[...] * tokens) * second
+    both_ref[sums, :] = message_ref[sums, :] + partner_ref[sums, :]
+
+
+def finish_body(segments, modes, tokens, length, pairs, *refs):
     count = len(segments)
     aloc_refs, gb_refs = refs[:count], refs[count:2 * count]
-    (a_ref, r_ref, decay_ref, carry_ref, sums_ref, x2_ref, v_ref,
-     gx2_ref, gv_ref, rgrad_ref, dgrad_ref, gin, nat) = refs[2 * count:]
+    a_ref, r_ref, decay_ref, x2_ref, v_ref, partner_ref, both_ref = refs[2 * count:2 * count + 7]
+    got_refs = refs[2 * count + 7:2 * count + 6 + pairs]
+    (gx2_ref, gv_ref, rgrad_ref, dgrad_ref, gin, nat, gx2_here, gv_here, sems) = refs[2 * count + 6 + pairs:]
     channels = a_ref.shape[1]
     unroll = 4
+    pair, core = place()
+    states = []
     for lane in range(channels // LANES):
         lanes = pl.ds(lane * LANES, LANES)
-        decays = [spread(a_ref, m, lanes) for m in range(modes)]
-        state = carry_ref[:, lanes]
-        for seg in reversed(range(count)):
-            start, rows = segments[seg]
-            steps = rows // BLOCKS
+        state = jnp.where(core == 0, partner_ref[pl.ds(0, modes), lanes], 0.0)
+        for step, got_ref in enumerate(got_refs, 1):
+            other = pair ^ step
+            gap = jnp.maximum((2 * (other - pair - 1) + 1 - core) * tokens, 0).astype(F32)
+            weight = jnp.where(other > pair, jnp.exp(-decay_ref[:, lanes] * gap), 0.0)
+            state = state + weight * got_ref[pl.ds(0, modes), lanes]
+        states.append(state)
+    copies = []
+    for seg in reversed(range(count)):
+        start, rows = segments[seg]
+        steps = rows // BLOCKS
+        window = pl.ds(start, rows)
+        for lane in range(channels // LANES):
+            lanes = pl.ds(lane * LANES, LANES)
+            decays = [spread(a_ref, m, lanes) for m in range(modes)]
+            state = states[lane]
             power = jnp.exp(-decay_ref[:, lanes] * steps)
             for b in reversed(range(BLOCKS)):
                 rowsb = pl.ds(b * modes, modes)
                 gin[rowsb, :] = state
                 state = power * state + gb_refs[seg][lane, rowsb, :]
+            states[lane] = state
             edge = tuple(
                 spread(r_ref, m, lanes) * decays[m] * gin[pl.ds(m, BLOCKS, stride=modes), :]
                 for m in range(modes)
@@ -281,10 +392,18 @@
                 return tuple(edge)
 
             lax.fori_loop(0, steps // unroll, body, edge)
-        gx2_ref[:, lanes] = (nat[lane] * v_ref[:, lanes].astype(F32)).astype(BF16)
-        gv_ref[:, lanes] = (nat[lane] * x2_ref[:, lanes].astype(F32)).astype(BF16)
+            adjoint = nat[lane, window, :]
+            gx2_here[window, lanes] = (adjoint * v_ref[window, lanes].astype(F32)).astype(BF16)
+            gv_here[window, lanes] = (adjoint * x2_ref[window, lanes].astype(F32)).astype(BF16)
+        for j, (here, there) in enumerate(((gx2_here, gx2_ref), (gv_here, gv_ref))):
+            copy = pltpu.make_async_copy(here.at[window, :], there.at[window, :], sems.at[seg, j])
+            copy.start()
+            copies.append(copy)
+    sums = both_ref[pl.ds(modes, 2 * modes), :]
+    for got_ref in got_refs:
+        sums = sums + got_ref[pl.ds(modes, 2 * modes), :]
     owned = rgrad_ref.shape[0]
-    row = lax.broadcasted_iota(jnp.int32, (owned, channels), 0) + index_ref[0] * owned
+    row = lax.broadcasted_iota(jnp.int32, (owned, channels), 0) + lax.axis_index("ctx") * owned
     column = lax.broadcasted_iota(jnp.int32, (owned, channels), 1)
     pick = (row == column).astype(F32)
 
@@ -294,9 +413,11 @@
             precision=lax.Precision.HIGHEST, preferred_element_type=F32,
         )
 
-    rgrad_ref[...] = choose(sums_ref[pl.ds(0, modes), :]) / length
+    rgrad_ref[...] = choose(sums[:modes]) / length
     scale = r_ref[...] * decay_ref[...] * (float(length) ** 0.5)
-    dgrad_ref[...] = -choose(scale * sums_ref[pl.ds(modes, modes), :]) / length
+    dgrad_ref[...] = -choose(scale * sums[modes:]) / length
+    for copy in copies:
+        copy.wait()
 
 
 def on_device(g_out, w_out, gate_x1, gate_x2, value_v, residue, decay):
@@ -306,8 +427,6 @@
     length = tokens * context_size
     modes = residue.shape[1]
     lane_tiles = channels // LANES
-    context_index = lax.axis_index("ctx")
-    ch_index = lax.axis_index("ch")
     owned = channels // context_size
 
     bits = [1 << bit for bit in range(ch_size.bit_length() - 1)]
@@ -315,19 +434,17 @@
     chunks = [(0, half_rows, bits), (half_rows, half_rows, bits[::-1])]
     segments = [(start, rows) for start, rows, _ in chunks]
     count = len(chunks)
-
-    sending, keeping = [], []
-    for start, rows, order in chunks:
-        offsets = halving_layout(order)
-        cut = len(offsets) // 2
-        which = jnp.array(offsets, jnp.int32) ^ ch_index
-        sent = project(which[:cut], g_out, w_out, start, rows, channels, BF16)
-        sending.append(lax.ppermute(sent, "ch", xor_pairs(ch_size, order[0])))
-        keeping.append((which[cut:], start, rows, order))
-    keeping = [
-        (project(which, g_out, w_out, start, rows, channels, F32), order)
-        for which, start, rows, order in keeping
-    ]
+    layouts = [halving_layout(order) for _, _, order in chunks]
+    cut = ch_size // 2
+
+    rows_of = [(start, rows) for start, rows, _ in chunks]
+    projected = project(
+        g_out, w_out,
+        [(*where, layout[:cut]) for where, layout in zip(rows_of, layouts)]
+        + [(*where, layout[cut:]) for where, layout in zip(rows_of, layouts)], channels)
+    sent = [lax.ppermute(piece, "ch", xor_pairs(ch_size, order[0]))
+            for piece, (_, _, order) in zip(projected, chunks)]
+    kept = projected[count:]
 
     decay_t = decay.T
     residue_t = residue.T
@@ -347,64 +464,59 @@
         name="forward",
     )(gate_x2, value_v, a, r, decay_t)
 
-    pair = context_index // 2
-    core = context_index % 2
     pairs = context_size // 2
-    whole_power = jnp.exp(-decay_t * tokens)
-
     partner = lax.ppermute(total, "ctx", xor_pairs(context_size, 1))
-    first = jnp.where(core == 0, total, partner)
-    second = jnp.where(core == 0, partner, total)
-    pair_h = second[:modes] + whole_power * first[:modes]
-    pair_k = second[modes:] + whole_power * (first[modes:] + tokens * first[:modes])
-    both = jnp.concatenate([pair_h, pair_k], 0)
-    carry_h = jnp.where(core == 1, first[:modes], 0.0)
-    carry_k = jnp.where(core == 1, first[modes:], 0.0)
-    for step in range(1, pairs):
-        other = pair ^ step
-        got = lax.ppermute(both, "ctx", xor_pairs(context_size, 2 * step))
-        gap = ((2 * (pair - other - 1) + core) * tokens).astype(F32)
-        weight = jnp.where(other < pair, jnp.exp(-decay_t * jnp.maximum(gap, 0.0)), 0.0)
-        carry_h = carry_h + weight * got[:modes]
-        carry_k = carry_k + weight * (got[modes:] + gap * got[:modes])
-    carry = jnp.concatenate([carry_h, carry_k], 0)
+    both = pl.pallas_call(
+        functools.partial(forward_pair_body, modes, tokens),
+        out_shape=jax.ShapeDtypeStruct((2 * modes, channels), F32),
+        compiler_params=params(),
+        name="forward_pair",
+    )(total, partner, decay_t)
+    got = [lax.ppermute(both, "ctx", xor_pairs(context_size, 2 * step)) for step in range(1, pairs)]
 
     resp, hin, kin = pl.pallas_call(
-        functools.partial(respond_body, segments, modes),
+        functools.partial(respond_body, segments, modes, tokens),
         out_shape=[perm_shape, state_shape, state_shape],
         compiler_params=params(),
         cost_estimate=pl.CostEstimate(flops=work * 2, bytes_accessed=tokens * channels * 8, transcendentals=0),
         name="respond",
-    )(hb, eb, yloc, a, r, decay_t, carry)
-
-    grads, alocs, gbs, sums = [], [], [], []
-    arrived = []
-    stages = [(sent, kept, order) for sent, (kept, order) in zip(sending, keeping)]
+    )(hb, eb, yloc, a, r, decay_t, partner, *got)
+
+    alocs, gbs, sums = [], [], []
+    *sent, _ = lax.optimization_barrier((*sent, got))
+    arrived = [[piece] for piece in sent]
     for level in range(1, len(bits)):
-        following = []
-        for sent, kept, order in stages:
-            cut = kept.shape[1] // 2
-            away = (kept[:, :cut] + sent[:, :cut].astype(F32)).astype(BF16)
-            stay = kept[:, cut:] + sent[:, cut:].astype(F32)
-            moved = lax.ppermute(away, "ch", xor_pairs(ch_size, order[level]))
-            following.append((moved, stay, order))
-        stages = following
-    for seg, (moved, stay, _) in enumerate(stages):
-        start, rows = segments[seg]
+        for which, (_, _, order) in enumerate(chunks):
+            stop = cut >> level
+            width = kept[which].shape[1]
+            left = width - 2 * stop * channels
+            away = kept[which][:, left:left + stop * channels].astype(F32)
+            for piece in arrived[which]:
+                left = piece.shape[1] - 2 * stop * channels
+                away = away + piece[:, left:left + stop * channels].astype(F32)
+            arrived[which].append(
+                lax.ppermute(away.astype(BF16), "ch", xor_pairs(ch_size, order[level])))
+    previous = []
+    for seg, (start, rows) in enumerate(segments):
         block_shape = jax.ShapeDtypeStruct((lane_tiles, BLOCKS * modes, LANES), F32)
+        pieces = arrived[seg]
         grad_x1, aloc, gb, partial_sums = pl.pallas_call(
-            functools.partial(adjoint_body, (seg, start, rows), modes),
-            out_shape=[jax.ShapeDtypeStruct((rows, channels), BF16),
+            functools.partial(adjoint_body, (seg, start, rows), modes, len(pieces), len(previous)),
+            in_specs=in_vmem(1 + len(pieces)) + [pl.BlockSpec(memory_space=HBM)] * len(previous) + in_vmem(7),
+            out_specs=[pl.BlockSpec(memory_space=HBM)] + in_vmem(3),
+            out_shape=[jax.ShapeDtypeStruct((tokens, channels), BF16),
                        jax.ShapeDtypeStruct((lane_tiles, rows, LANES), F32),
                        block_shape,
                        jax.ShapeDtypeStruct((2 * modes, channels), F32)],
             scratch_shapes=[pltpu.VMEM((lane_tiles, rows, LANES), F32)] * 2
-            + [pltpu.VMEM((BLOCKS * modes, LANES), F32)] * 3,
+            + [pltpu.VMEM((BLOCKS * modes, LANES), F32)] * 3
+            + [pltpu.VMEM((rows, channels), BF16), pltpu.SemaphoreType.DMA(())],
+            input_output_aliases={1 + len(pieces): 0} if previous else {},
             compiler_params=params(),
             cost_estimate=pl.CostEstimate(flops=rows * channels * modes * 10, bytes_accessed=rows * channels * 16, transcendentals=0),
             name="adjoint",
-        )(stay, moved, gate_x1, resp, xperm, hin, kin, a, r)
-        grads.append(grad_x1)
+        )(kept[seg], *pieces, *previous, gate_x1, resp, xperm, hin, kin, a, r)
+        previous = [grad_x1]
         alocs.append(aloc)
         gbs.append(gb)
         sums.append(partial_sums)
@@ -416,33 +528,30 @@
         name="totals",
     )(*gbs, *sums, decay_t)
     partner = lax.ppermute(message, "ctx", xor_pairs(context_size, 1))
-    first = jnp.where(core == 0, message[:modes], partner[:modes])
-    second = jnp.where(core == 0, partner[:modes], message[:modes])
-    both = jnp.concatenate([first + whole_power * second, message[modes:] + partner[modes:]], 0)
-    carry_g = jnp.where(core == 0, second, 0.0)
-    param_sums = both[modes:]
-    for step in range(1, pairs):
-        other = pair ^ step
-        got = lax.ppermute(both, "ctx", xor_pairs(context_size, 2 * step))
-        gap = ((2 * (other - pair - 1) + 1 - core) * tokens).astype(F32)
-        weight = jnp.where(other > pair, jnp.exp(-decay_t * jnp.maximum(gap, 0.0)), 0.0)
-        carry_g = carry_g + weight * got[:modes]
-        param_sums = param_sums + got[modes:]
-
-    vmem = pl.BlockSpec(memory_space=pltpu.VMEM)
+    both = pl.pallas_call(
+        functools.partial(backward_pair_body, modes, tokens),
+        out_shape=jax.ShapeDtypeStruct((3 * modes, channels), F32),
+        compiler_params=params(),
+        name="backward_pair",
+    )(message, partner, decay_t)
+    got = [lax.ppermute(both, "ctx", xor_pairs(context_size, 2 * step)) for step in range(1, pairs)]
+
     grad_x2, grad_v, residue_grad, decay_grad = pl.pallas_call(
-        functools.partial(finish_body, segments, modes, length),
-        in_specs=[pl.BlockSpec(memory_space=pltpu.SMEM)] + [vmem] * (2 * count + 7),
-        out_specs=[vmem] * 4,
+        functools.partial(finish_body, segments, modes, tokens, length, pairs),
+        in_specs=in_vmem(2 * count + 6 + pairs),
+        out_specs=[pl.BlockSpec(memory_space=HBM)] * 2 + in_vmem(2),
         out_shape=[jax.ShapeDtypeStruct((tokens, channels), BF16)] * 2
         + [jax.ShapeDtypeStruct((owned, modes), F32)] * 2,
         scratch_shapes=[pltpu.VMEM((BLOCKS * modes, LANES), F32),
-                        pltpu.VMEM((lane_tiles, tokens, LANES), F32)],
+                        pltpu.VMEM((lane_tiles, tokens, LANES), F32),
+                        pltpu.VMEM((tokens, channels), BF16),
+                        pltpu.VMEM((tokens, channels), BF16),
+                        pltpu.SemaphoreType.DMA((count, 2))],
         compiler_params=params(),
         cost_estimate=pl.CostEstimate(flops=work * 2, bytes_accessed=tokens * channels * 12, transcendentals=0),
         name="finish",
-    )(context_index.reshape(1), *alocs, *gbs, a, r, decay_t, carry_g, param_sums, gate_x2, value_v)
-    return jnp.concatenate(grads, 0), grad_x2, grad_v, residue_grad, decay_grad
+    )(*alocs, *gbs, a, r, decay_t, gate_x2, value_v, partner, both, *got)
+    return grad_x1, grad_x2, grad_v, residue_grad, decay_grad
 
 
 def solution(mesh):

time: 80.2 us -> 59.2 us (0.74)
  Pallas kernels: 38.9 us -> 27.3 us
  local copies, waits for them, and re-layouts: 10.1 us -> 1.37 us
  waiting for transfers between devices: 8.09 us -> 13.5 us
  other arithmetic: 7.13 us -> 2.04 us
    pallas_call x8 -> x7, Pallas kernels: 33.7 us -> 22.2 us  [the longest x2 8.29 us: on_device(): pl.pallas_call(functools.partial(adjoint_body, (seg, start, rows), modes,...]
    unnamed x36 -> x16, local copies, waits for them, and re-layouts: 9.95 us -> 1.37 us
    ppermute x10, waiting for transfers between devices: 6.9 us -> 11.1 us  [the longest x6 8.8 us: on_device(): lax.ppermute(both, 'ctx', xor_pairs(context_size, 2 * step))]
    concatenate x4 -> x0, other arithmetic: 2.41 us -> none  [the longest x1 1.78 us: on_device(): jnp.concatenate(grads, 0)]
    add x7 -> x0, other arithmetic: 1.74 us -> none  [the longest x1 0.92 us: on_device(): carry_k = carry_k + weight * (got[modes:] + gap * got[:modes])]
    ppermute x1, waiting for transfers between devices: 0.01 us -> 1.19 us  [on_device(): partner = lax.ppermute(total, 'ctx', xor_pairs(context_size, 1))]
  transfers between devices with their start and end apart: 12 -> 12, of which waited for: 4 -> 7; matrix products, arithmetic and copies ran while one was open for 8% -> 2% of each run, Pallas kernels for 33% -> 20%
where the time goes in v1:
time: 59.2 us; the launch traced here: 59 us
  Pallas kernels  27.3 us (46%)
  starting transfers between devices  13.8 us (23%)
  waiting for transfers between devices  13.5 us (23%)
  other arithmetic  2.04 us (3%)
  local copies, waits for them, and re-layouts  1.37 us (2%)
  between operations  0.84 us (1%)
    ppermute x6, waiting for transfers between devices, on_device(): lax.ppermute(both, 'ctx', xor_pairs(context_size, 2 * step))  8.8 us
    pallas_call x2, Pallas kernels, on_device(): pl.pallas_call(functools.partial(adjoint_body, (seg, start, rows), modes,...  8.29 us
    pallas_call x1, Pallas kernels, project(): pl.pallas_call(functools.partial(project_body, work, width, pieces), in_s...  8.22 us
    ppermute x6, starting transfers between devices, on_device(): lax.ppermute(both, 'ctx', xor_pairs(context_size, 2 * step))  8 us
    pallas_call x1, Pallas kernels, on_device(): pl.pallas_call(functools.partial(forward_body, segments, modes), out_shap...  5.14 us
    ppermute x2, starting transfers between devices, on_device(): lax.ppermute(piece, 'ch', xor_pairs(ch_size, order[0]))  4.52 us
    pallas_call x1, Pallas kernels, on_device(): pl.pallas_call(functools.partial(finish_body, segments, modes, tokens, le...  3.4 us
    ppermute x2, waiting for transfers between devices, on_device(): lax.ppermute(away.astype(BF16), 'ch', xor_pairs(ch_size, order[level]))  2.32 us
  transfers between devices with their start and end apart: 12, of which 7 were waited for; matrix products, arithmetic and copies ran while one was open for 2% of the time, Pallas kernels for 20%

profile of v1, /device:TPU:0, one launch (start us, length us, event | category | flops | bytes accessed | tf_op | source)
XLA Modules:
  0.0 59.0 jit_solution(8238724437488533494)
XLA Ops:
  0.6 0.0 copy-start.6
  0.6 0.0 copy-start.5
  0.7 0.0 copy-start.1
  0.7 0.0 copy-start.2
  0.7 8.2 %project.1 = (bf16[512,512]{1,0:T(8,128)(2,1)}, bf16[512,512]{1,0:T(8,128)(2,1)}, bf16[512,512]{1,0:T(8,128)(2,1)}, bf16[512,512]{1,0:T(8,128)(2,1)}) custom-call(bf16[1024,2048]{1,0:T(8,128)(2,1)} %g_ref.1, bf16[1024,2048]{1,0:T(8,128)(2,1)} %w_ref.1), custom_call_target="tpu_custom_call" | custom-call | tf_op jit(solution)/shard_map/project/pallas_call | solution.py:96
  8.9 0.0 copy-start
  8.9 0.0 copy-start.4
  8.9 3.0 %collective-permute-start = (bf16[512,512]{1,0:T(8,128)(2,1)}, bf16[512,512]{1,0:T(8,128)(2,1)S(1)}, u32[]{:S(2)}, u32[]{:S(2)}) collective-permute-start(bf16[512,512]{1,0:T(8,128)(2,1)} %get-tuple-element.32), channel_id=1, source_target_pairs={{0,1},{1,0},{2,3},{3,2},{4,5},{5,4},{6,7},{7,6},{8,9},{9,8},{10,11... | collective-permute-start | bytes 1572872 | tf_op jit(solution)/shard_map/ppermute | solution.py:445
  11.9 1.5 %collective-permute-start.1 = (bf16[512,512]{1,0:T(8,128)(2,1)}, bf16[512,512]{1,0:T(8,128)(2,1)S(1)}, u32[]{:S(2)}, u32[]{:S(2)}) collective-permute-start(bf16[512,512]{1,0:T(8,128)(2,1)} %get-tuple-element.33), channel_id=1, source_target_pairs={{0,2},{1,3},{2,0},{3,1},{4,6},{5,7},{6,4},{7,5},{8,10},{9,11},{10,... | collective-permute-start | bytes 1572872 | tf_op jit(solution)/shard_map/ppermute | solution.py:445
  13.4 0.0 copy-done.6
  13.5 0.0 copy-done.5
  13.5 0.0 copy-done.1
  13.5 0.0 copy-done.2
  13.5 5.1 %forward.1 = (f32[2,1024,128]{2,1,0:T(8,128)S(1)}, f32[2,1024,128]{2,1,0:T(8,128)S(1)}, f32[2,2,128,128]{3,2,1,0:T(8,128)S(1)}, f32[2,2,128,128]{3,2,1,0:T(8,128)S(1)}, f32[32,256]{1,0:T(8,128)S(1)}) custom-call(bf16[1024,256]{1,0:T(8,128)(2,1)S(1)} %copy-done.1, bf16[1024,256]{1,0:T(8,128)(2,1)S(1)} %copy-done.2, ...), custom_call_target="tpu_custom_call" | custom-call | flops 25165824 | bytes 3145728 | tf_op jit(solution)/shard_map/forward/pallas_call | solution.py:457
  18.6 0.0 copy-start.3
  18.6 0.1 collective-permute-start.2
  18.7 1.2 %collective-permute-done.2.partner_ref = f32[32,256]{1,0:T(8,128)S(1)} collective-permute-done((f32[32,256]{1,0:T(8,128)S(1)}, f32[32,256]{1,0:T(8,128)S(1)}, u32[]{:S(2)}, u32[]{:S(2)}) %collective-permute-start.2) | collective-permute-done | bytes 32800 | tf_op jit(solution)/shard_map/ppermute | solution.py:468
  19.9 1.6 %collective-permute-start.3 = (f32[32,256]{1,0:T(8,128)S(1)}, f32[32,256]{1,0:T(8,128)S(1)}, u32[]{:S(2)}, u32[]{:S(2)}) collective-permute-start(f32[32,256]{1,0:T(8,128)S(1)} %forward_pair.1), channel_id=1, source_target_pairs={{0,8},{4,12},{8,0},{12,4},{16,24},{20,28},{24,16},{28,20},{1,9},{5... | collective-permute-start | bytes 98312 | tf_op jit(solution)/shard_map/ppermute | solution.py:475
  21.6 2.6 %collective-permute-start.4 = (f32[32,256]{1,0:T(8,128)S(1)}, f32[32,256]{1,0:T(8,128)S(1)}, u32[]{:S(2)}, u32[]{:S(2)}) collective-permute-start(f32[32,256]{1,0:T(8,128)S(1)} %forward_pair.1), channel_id=1, source_target_pairs={{0,16},{4,20},{8,24},{12,28},{16,0},{20,4},{24,8},{28,12},{1,17},{... | collective-permute-start | bytes 98312 | tf_op jit(solution)/shard_map/ppermute | solution.py:475
  24.2 0.2 collective-permute-start.5
  24.4 0.0 collective-permute-done.3.refs_0_
  24.4 2.6 %collective-permute-done.4.refs_1_ = f32[32,256]{1,0:T(8,128)S(1)} collective-permute-done((f32[32,256]{1,0:T(8,128)S(1)}, f32[32,256]{1,0:T(8,128)S(1)}, u32[]{:S(2)}, u32[]{:S(2)}) %collective-permute-start.4) | collective-permute-done | bytes 32800 | tf_op jit(solution)/shard_map/ppermute | solution.py:475
  27.0 2.9 %collective-permute-done.5.refs_2_ = f32[32,256]{1,0:T(8,128)S(1)} collective-permute-done((f32[32,256]{1,0:T(8,128)S(1)}, f32[32,256]{1,0:T(8,128)S(1)}, u32[]{:S(2)}, u32[]{:S(2)}) %collective-permute-start.5) | collective-permute-done | bytes 32800 | tf_op jit(solution)/shard_map/ppermute | solution.py:475
  29.9 0.0 collective-permute-done.refs_0_
  29.9 0.0 collective-permute-done.1.refs_0_
  29.9 1.0 %add_convert_fusion = bf16[512,256]{1,0:T(8,128)(2,1)S(1)} fusion(bf16[512,512]{1,0:T(8,128)(2,1)S(1)} %collective-permute-done.refs_0_, bf16[512,512]{1,0:T(8,128)(2,1)} %get-tuple-element.36.kept_ref), kind=kLoop, calls=%fused_computation | loop fusion | flops 524288 | bytes 786432 | tf_op jit(solution)/shard_map/convert_element_type | solution.py:498
  30.9 0.6 collective-permute-start.7
  31.5 1.0 %add_convert_fusion.1 = bf16[512,256]{1,0:T(8,128)(2,1)S(1)} fusion(bf16[512,512]{1,0:T(8,128)(2,1)S(1)} %collective-permute-done.1.refs_0_, bf16[512,512]{1,0:T(8,128)(2,1)} %get-tuple-element.31.kept_ref), kind=kLoop, calls=%fused_computation.1 | loop fusion | flops 524288 | bytes 786432 | tf_op jit(solution)/shard_map/convert_element_type | solution.py:498
  32.5 0.6 %collective-permute-start.6 = (bf16[512,256]{1,0:T(8,128)(2,1)S(1)}, bf16[512,256]{1,0:T(8,128)(2,1)S(1)}, u32[]{:S(2)}, u32[]{:S(2)}) collective-permute-start(bf16[512,256]{1,0:T(8,128)(2,1)S(1)} %add_convert_fusion.1), channel_id=1, source_target_pairs={{0,1},{1,0},{2,3},{3,2},{4,5},{5,4},{6,7},{7,6},{8,9},{9,8},{10,11... | collective-permute-start | bytes 786440 | tf_op jit(solution)/shard_map/ppermute | solution.py:498
  33.1 2.2 %respond.1 = (f32[2,1024,128]{2,1,0:T(8,128)S(1)}, f32[2,2,128,128]{3,2,1,0:T(8,128)S(1)}, f32[2,2,128,128]{3,2,1,0:T(8,128)S(1)}) custom-call(f32[2,2,128,128]{3,2,1,0:T(8,128)S(1)} %get-tuple-element.38.hb_ref, f32[2,2,128,128]{3,2,1,0:T(8,128)S(1)} %get-tuple-element.39.eb_ref, f32[2,1024,128]{2,1,0:T(8,128)S(1)} %get-tuple-element.40.yloc_ref, ...), custom_call_target="tpu_custom_call" | custom-call | flops 8388608 | bytes 2097152 | tf_op jit(solution)/shard_map/respond/pallas_call | solution.py:477
  35.3 2.3 %collective-permute-done.7.refs_1_ = bf16[512,256]{1,0:T(8,128)(2,1)S(1)} collective-permute-done((bf16[512,256]{1,0:T(8,128)(2,1)S(1)}, bf16[512,256]{1,0:T(8,128)(2,1)S(1)}, u32[]{:S(2)}, u32[]{:S(2)}) %collective-permute-start.7) | collective-permute-done | bytes 262176 | tf_op jit(solution)/shard_map/ppermute | solution.py:498
  37.6 0.0 copy-done
  37.6 0.0 copy-done.4
  37.6 4.1 %adjoint.2 = (bf16[1024,256]{1,0:T(8,128)(2,1)}, f32[2,512,128]{2,1,0:T(8,128)S(1)}, f32[2,128,128]{2,1,0:T(8,128)S(1)}, f32[32,256]{1,0:T(8,128)S(1)}) custom-call(bf16[512,512]{1,0:T(8,128)(2,1)S(1)} %copy-done.4, bf16[512,512]{1,0:T(8,128)(2,1)S(1)} %collective-permute-done.refs_0_, bf16[512,256]{1,0:T(8,128)(2,1)S(1)} %collective-permute-done.7.refs_1_, ...), custom_call_target="tpu_custom_call" | custom-call | flops 20971520 | bytes 2097152 | tf_op jit(solution)/shard_map/adjoint/pallas_call | solution.py:503
  41.8 0.0 collective-permute-done.6.refs_1_
  41.8 0.0 copy-done.3
  41.8 4.2 %adjoint.3 = (bf16[1024,256]{1,0:T(8,128)(2,1)}, f32[2,512,128]{2,1,0:T(8,128)S(1)}, f32[2,128,128]{2,1,0:T(8,128)S(1)}, f32[32,256]{1,0:T(8,128)S(1)}) custom-call(bf16[512,512]{1,0:T(8,128)(2,1)S(1)} %copy-done.3, bf16[512,512]{1,0:T(8,128)(2,1)S(1)} %collective-permute-done.1.refs_0_, ...), custom_call_target="tpu_custom_call", output_to_operand_aliasing={{0}: (3, {})} | custom-call | flops 20971520 | bytes 2097152 | tf_op jit(solution)/shard_map/adjoint/pallas_call | solution.py:503
  46.0 0.1 totals.1.message_ref
  46.0 0.1 collective-permute-start.8
  46.1 1.2 %collective-permute-done.8.partner_ref.refs_9_ = f32[48,256]{1,0:T(8,128)S(1)} collective-permute-done((f32[48,256]{1,0:T(8,128)S(1)}, f32[48,256]{1,0:T(8,128)S(1)}, u32[]{:S(2)}, u32[]{:S(2)}) %collective-permute-start.8) | collective-permute-done | bytes 49184 | tf_op jit(solution)/shard_map/ppermute | solution.py:530
  47.4 0.1 collective-permute-start.10
  47.4 1.4 %collective-permute-start.11 = (f32[48,256]{1,0:T(8,128)S(1)}, f32[48,256]{1,0:T(8,128)S(1)}, u32[]{:S(2)}, u32[]{:S(2)}) collective-permute-start(f32[48,256]{1,0:T(8,128)S(1)} %backward_pair.1.refs_10_), channel_id=1, source_target_pairs={{0,24},{4,28},{8,16},{12,20},{16,8},{20,12},{24,0},{28,4},{1,25},{... | collective-permute-start | bytes 147464 | tf_op jit(solution)/shard_map/ppermute | solution.py:537
  48.8 2.1 %collective-permute-start.9 = (f32[48,256]{1,0:T(8,128)S(1)}, f32[48,256]{1,0:T(8,128)S(1)}, u32[]{:S(2)}, u32[]{:S(2)}) collective-permute-start(f32[48,256]{1,0:T(8,128)S(1)} %backward_pair.1.refs_10_), channel_id=1, source_target_pairs={{0,8},{4,12},{8,0},{12,4},{16,24},{20,28},{24,16},{28,20},{1,9},{5... | collective-permute-start | bytes 147464 | tf_op jit(solution)/shard_map/ppermute | solution.py:537
  50.9 2.9 %collective-permute-done.10.refs_12_ = f32[48,256]{1,0:T(8,128)S(1)} collective-permute-done((f32[48,256]{1,0:T(8,128)S(1)}, f32[48,256]{1,0:T(8,128)S(1)}, u32[]{:S(2)}, u32[]{:S(2)}) %collective-permute-start.10) | collective-permute-done | bytes 49184 | tf_op jit(solution)/shard_map/ppermute | solution.py:537
  53.8 0.0 collective-permute-done.11.refs_13_
  53.8 0.5 collective-permute-done.9.refs_11_
  54.2 3.4 %finish.1 = (bf16[1024,256]{1,0:T(8,128)(2,1)}, bf16[1024,256]{1,0:T(8,128)(2,1)}, f32[32,16]{1,0:T(8,128)S(1)}, f32[32,16]{1,0:T(8,128)S(1)}) custom-call(f32[2,512,128]{2,1,0:T(8,128)S(1)} %get-tuple-element.47.refs_0_, f32[2,512,128]{2,1,0:T(8,128)S(1)} %get-tuple-element.48.refs_1_, f32[2,128,128]{2,1,0:T(8,128)S(1)} %get-tuple-element.49.refs_0_.refs_2_, ...), custom_call_target="tpu_custom_call" | custom-call | flops 8388608 | bytes 3145728 | tf_op jit(solution)/shard_map/finish/pallas_call | solution.py:539
  57.6 0.7 %copy.13 = f32[32,16]{0,1:T(8,128)} copy(f32[32,16]{1,0:T(8,128)S(1)} %get-tuple-element.60) | data formatting | bytes 4096
  58.3 0.7 %copy.14 = f32[32,16]{0,1:T(8,128)} copy(f32[32,16]{1,0:T(8,128)S(1)} %get-tuple-element.61) | data formatting | bytes 4096
  (4 shorter events, 0.0 us)
Async XLA Ops:
  0.6 12.8 %copy-start.6 = (f32[256,16]{0,1:T(8,128)S(1)}, f32[256,16]{0,1:T(8,128)}, u32[]{:S(2)}) copy-start(f32[256,16]{0,1:T(8,128)} %param.12) | copy-start | bytes 49156
  0.6 12.8 %copy-start.5 = (f32[256,16]{0,1:T(8,128)S(1)}, f32[256,16]{0,1:T(8,128)}, u32[]{:S(2)}) copy-start(f32[256,16]{0,1:T(8,128)} %param.13) | copy-start | bytes 49156
  0.7 12.8 %copy-start.1 = (bf16[1024,256]{1,0:T(8,128)(2,1)S(1)}, bf16[1024,256]{1,0:T(8,128)(2,1)}, u32[]{:S(2)}) copy-start(bf16[1024,256]{1,0:T(8,128)(2,1)} %refs_7_.1) | copy-start | bytes 1572868
  0.7 12.8 %copy-start.2 = (bf16[1024,256]{1,0:T(8,128)(2,1)S(1)}, bf16[1024,256]{1,0:T(8,128)(2,1)}, u32[]{:S(2)}) copy-start(bf16[1024,256]{1,0:T(8,128)(2,1)} %refs_8_.1) | copy-start | bytes 1572868
  8.9 28.7 %copy-start = (bf16[1024,256]{1,0:T(8,128)(2,1)S(1)}, bf16[1024,256]{1,0:T(8,128)(2,1)}, u32[]{:S(2)}) copy-start(bf16[1024,256]{1,0:T(8,128)(2,1)} %refs_3_.1) | copy-start | bytes 1572868
  8.9 28.7 %copy-start.4 = (bf16[512,512]{1,0:T(8,128)(2,1)S(1)}, bf16[512,512]{1,0:T(8,128)(2,1)}, u32[]{:S(2)}) copy-start(bf16[512,512]{1,0:T(8,128)(2,1)} %get-tuple-element.36.kept_ref) | copy-start | bytes 1572868
  8.9 21.0 %collective-permute-start = (bf16[512,512]{1,0:T(8,128)(2,1)}, bf16[512,512]{1,0:T(8,128)(2,1)S(1)}, u32[]{:S(2)}, u32[]{:S(2)}) collective-permute-start(bf16[512,512]{1,0:T(8,128)(2,1)} %get-tuple-element.32), channel_id=1, source_target_pairs={{0,1},{1,0},{2,3},{3,2},{4,5},{5,4},{6,7},{7,6},{8,9},{9,8},{10,11... | collective-permute-start | bytes 1572872 | tf_op jit(solution)/shard_map/ppermute | solution.py:445
  11.9 18.0 %collective-permute-start.1 = (bf16[512,512]{1,0:T(8,128)(2,1)}, bf16[512,512]{1,0:T(8,128)(2,1)S(1)}, u32[]{:S(2)}, u32[]{:S(2)}) collective-permute-start(bf16[512,512]{1,0:T(8,128)(2,1)} %get-tuple-element.33), channel_id=1, source_target_pairs={{0,2},{1,3},{2,0},{3,1},{4,6},{5,7},{6,4},{7,5},{8,10},{9,11},{10,... | collective-permute-start | bytes 1572872 | tf_op jit(solution)/shard_map/ppermute | solution.py:445
  18.6 23.2 %copy-start.3 = (bf16[512,512]{1,0:T(8,128)(2,1)S(1)}, bf16[512,512]{1,0:T(8,128)(2,1)}, u32[]{:S(2)}) copy-start(bf16[512,512]{1,0:T(8,128)(2,1)} %get-tuple-element.31.kept_ref) | copy-start | bytes 1572868
  18.6 1.3 %collective-permute-start.2 = (f32[32,256]{1,0:T(8,128)S(1)}, f32[32,256]{1,0:T(8,128)S(1)}, u32[]{:S(2)}, u32[]{:S(2)}) collective-permute-start(f32[32,256]{1,0:T(8,128)S(1)} %get-tuple-element.34.total_ref), channel_id=1, source_target_pairs={{0,4},{4,0},{8,12},{12,8},{16,20},{20,16},{24,28},{28,24},{1,5},{5... | collective-permute-start | bytes 98312 | tf_op jit(solution)/shard_map/ppermute | solution.py:468
  19.9 4.5 %collective-permute-start.3 = (f32[32,256]{1,0:T(8,128)S(1)}, f32[32,256]{1,0:T(8,128)S(1)}, u32[]{:S(2)}, u32[]{:S(2)}) collective-permute-start(f32[32,256]{1,0:T(8,128)S(1)} %forward_pair.1), channel_id=1, source_target_pairs={{0,8},{4,12},{8,0},{12,4},{16,24},{20,28},{24,16},{28,20},{1,9},{5... | collective-permute-start | bytes 98312 | tf_op jit(solution)/shard_map/ppermute | solution.py:475
  21.6 5.4 %collective-permute-start.4 = (f32[32,256]{1,0:T(8,128)S(1)}, f32[32,256]{1,0:T(8,128)S(1)}, u32[]{:S(2)}, u32[]{:S(2)}) collective-permute-start(f32[32,256]{1,0:T(8,128)S(1)} %forward_pair.1), channel_id=1, source_target_pairs={{0,16},{4,20},{8,24},{12,28},{16,0},{20,4},{24,8},{28,12},{1,17},{... | collective-permute-start | bytes 98312 | tf_op jit(solution)/shard_map/ppermute | solution.py:475
  24.2 5.7 %collective-permute-start.5 = (f32[32,256]{1,0:T(8,128)S(1)}, f32[32,256]{1,0:T(8,128)S(1)}, u32[]{:S(2)}, u32[]{:S(2)}) collective-permute-start(f32[32,256]{1,0:T(8,128)S(1)} %forward_pair.1), channel_id=1, source_target_pairs={{0,24},{4,28},{8,16},{12,20},{16,8},{20,12},{24,0},{28,4},{1,25},{... | collective-permute-start | bytes 98312 | tf_op jit(solution)/shard_map/ppermute | solution.py:475
  30.9 6.7 %collective-permute-start.7 = (bf16[512,256]{1,0:T(8,128)(2,1)S(1)}, bf16[512,256]{1,0:T(8,128)(2,1)S(1)}, u32[]{:S(2)}, u32[]{:S(2)}) collective-permute-start(bf16[512,256]{1,0:T(8,128)(2,1)S(1)} %add_convert_fusion), channel_id=1, source_target_pairs={{0,2},{1,3},{2,0},{3,1},{4,6},{5,7},{6,4},{7,5},{8,10},{9,11},{10,... | collective-permute-start | bytes 786440 | tf_op jit(solution)/shard_map/ppermute | solution.py:498
  32.5 9.3 %collective-permute-start.6 = (bf16[512,256]{1,0:T(8,128)(2,1)S(1)}, bf16[512,256]{1,0:T(8,128)(2,1)S(1)}, u32[]{:S(2)}, u32[]{:S(2)}) collective-permute-start(bf16[512,256]{1,0:T(8,128)(2,1)S(1)} %add_convert_fusion.1), channel_id=1, source_target_pairs={{0,1},{1,0},{2,3},{3,2},{4,5},{5,4},{6,7},{7,6},{8,9},{9,8},{10,11... | collective-permute-start | bytes 786440 | tf_op jit(solution)/shard_map/ppermute | solution.py:498
  46.0 1.3 %collective-permute-start.8 = (f32[48,256]{1,0:T(8,128)S(1)}, f32[48,256]{1,0:T(8,128)S(1)}, u32[]{:S(2)}, u32[]{:S(2)}) collective-permute-start(f32[48,256]{1,0:T(8,128)S(1)} %totals.1.message_ref), channel_id=1, source_target_pairs={{0,4},{4,0},{8,12},{12,8},{16,20},{20,16},{24,28},{28,24},{1,5},{5... | collective-permute-start | bytes 147464 | tf_op jit(solution)/shard_map/ppermute | solution.py:530
  47.4 6.4 %collective-permute-start.10 = (f32[48,256]{1,0:T(8,128)S(1)}, f32[48,256]{1,0:T(8,128)S(1)}, u32[]{:S(2)}, u32[]{:S(2)}) collective-permute-start(f32[48,256]{1,0:T(8,128)S(1)} %backward_pair.1.refs_10_), channel_id=1, source_target_pairs={{0,16},{4,20},{8,24},{12,28},{16,0},{20,4},{24,8},{28,12},{1,17},{... | collective-permute-start | bytes 147464 | tf_op jit(solution)/shard_map/ppermute | solution.py:537
  47.4 6.3 %collective-permute-start.11 = (f32[48,256]{1,0:T(8,128)S(1)}, f32[48,256]{1,0:T(8,128)S(1)}, u32[]{:S(2)}, u32[]{:S(2)}) collective-permute-start(f32[48,256]{1,0:T(8,128)S(1)} %backward_pair.1.refs_10_), channel_id=1, source_target_pairs={{0,24},{4,28},{8,16},{12,20},{16,8},{20,12},{24,0},{28,4},{1,25},{... | collective-permute-start | bytes 147464 | tf_op jit(solution)/shard_map/ppermute | solution.py:537
  48.8 5.4 %collective-permute-start.9 = (f32[48,256]{1,0:T(8,128)S(1)}, f32[48,256]{1,0:T(8,128)S(1)}, u32[]{:S(2)}, u32[]{:S(2)}) collective-permute-start(f32[48,256]{1,0:T(8,128)S(1)} %backward_pair.1.refs_10_), channel_id=1, source_target_pairs={{0,8},{4,12},{8,0},{12,4},{16,24},{20,28},{24,16},{28,20},{1,9},{5... | collective-permute-start | bytes 147464 | tf_op jit(solution)/shard_map/ppermute | solution.py:537

commit v2 on v1

--- a/solution.py
+++ b/solution.py
@@ -9,6 +9,7 @@
 
 LANES = 128
 PIECES = 2
+FPARTS = 1
 BLOCKS = 8
 F32 = jnp.float32
 BF16 = jnp.bfloat16
@@ -43,11 +44,27 @@
     return pl.ds(pl.multiple_of(block * width, width), width)
 
 
+def arrange(count):
+    return [1, 3, 2, 0] if count == 4 else list(range(count))
+
+
+def block_runs(offsets, arranged):
+    places = sorted((arranged.index(offset), spot) for spot, offset in enumerate(offsets))
+    runs = []
+    for where, spot in places:
+        if runs and runs[-1][1] + len(runs[-1][0]) == where:
+            runs[-1][0].append(spot)
+        else:
+            runs.append(([spot], where))
+    return runs
+
+
 def project_body(work, width, pieces, g_ref, w_ref, *refs):
     count = len(work)
     out_refs = refs[:count]
     g_here, w_here, total, g_sems, w_sems = refs[count:]
     depth = g_ref.shape[1] // pieces
+    arranged = arrange(w_ref.shape[0] // width)
     pending = {}
 
     def g_copy(rows, piece):
@@ -57,9 +74,10 @@
 
     def w_copy(offset, piece):
         columns = pl.ds(piece * depth, depth)
-        here = block_rows(offset, width)
+        there = pl.ds(arranged.index(offset) * width, width)
         return pltpu.make_async_copy(
-            w_ref.at[here, columns], w_here.at[here, columns], w_sems.at[offset, piece])
+            w_ref.at[block_rows(offset, width), columns], w_here.at[there, columns],
+            w_sems.at[offset, piece])
 
     for start, rows, offsets in work:
         for piece in range(pieces):
@@ -75,17 +93,20 @@
                 copy = pending.pop(key, None)
                 if copy is not None:
                     copy.wait()
-            for j, offset in enumerate(offsets):
-                here = pl.ds(j * width, width)
+            for spots, where in block_runs(offsets, arranged):
                 product = lax.dot_general(
-                    g_here[pl.ds(start, rows), columns], w_here[block_rows(offset, width), columns],
+                    g_here[pl.ds(start, rows), columns],
+                    w_here[pl.ds(where * width, len(spots) * width), columns],
                     CONTRACT_LAST, preferred_element_type=F32)
-                if piece > 0:
-                    product = product + total[:, here]
-                if piece < pieces - 1:
-                    total[:, here] = product
-                else:
-                    out_ref[:, here] = product.astype(out_ref.dtype)
+                for k, spot in enumerate(spots):
+                    here = pl.ds(spot * width, width)
+                    value = product[:, k * width:(k + 1) * width]
+                    if piece > 0:
+                        value = value + total[:, here]
+                    if piece < pieces - 1:
+                        total[:, here] = value
+                    else:
+                        out_ref[:, here] = value.astype(out_ref.dtype)
 
 
 def project(g_out, w_out, work, width):
@@ -114,20 +135,19 @@
     return jnp.broadcast_to(ref[pl.ds(row, 1), lanes], (BLOCKS, LANES))
 
 
-def forward_body(segments, modes, x2_ref, v_ref, a_ref, r_ref, decay_ref,
-                 xperm_ref, yloc_ref, hb_ref, eb_ref, total_ref, nat):
+def forward_body(segments, modes, x2_ref, v_ref, a_ref, decay_ref,
+                 xperm_ref, hb_ref, eb_ref, total_ref, nat):
     channels = x2_ref.shape[1]
     unroll = 4
-    half = modes // 2
+    group = modes // FPARTS
     for lane in range(channels // LANES):
         lanes = pl.ds(lane * LANES, LANES)
         mixed = (x2_ref[:, lanes].astype(F32) * v_ref[:, lanes].astype(F32)).astype(BF16)
         nat[lane] = mixed.astype(F32)
         for seg, (start, rows) in enumerate(segments):
             steps = rows // BLOCKS
-            for part in range(2):
-                decays = [spread(a_ref, part * half + m, lanes) for m in range(half)]
-                weights = [spread(r_ref, part * half + m, lanes) for m in range(half)]
+            for part in range(FPARTS):
+                decays = [spread(a_ref, part * group + m, lanes) for m in range(group)]
 
                 def body(outer, carry):
                     h, e = list(carry[0]), list(carry[1])
@@ -139,21 +159,15 @@
                             xperm_ref[lane, here, :] = x
                         else:
                             x = xperm_ref[lane, here, :]
-                        y = None
-                        for m in range(half):
+                        for m in range(group):
                             e[m] = decays[m] * e[m] + h[m]
                             h[m] = decays[m] * h[m] + x
-                            term = weights[m] * h[m]
-                            y = term if y is None else y + term
-                        if part == 1:
-                            y = y + yloc_ref[lane, here, :]
-                        yloc_ref[lane, here, :] = y
                     return tuple(h), tuple(e)
 
-                zero = (jnp.zeros((BLOCKS, LANES), F32),) * half
+                zero = (jnp.zeros((BLOCKS, LANES), F32),) * group
                 h, e = lax.fori_loop(0, steps // unroll, body, (zero, zero))
-                for m in range(half):
-                    row = pl.ds(part * half + m, BLOCKS, stride=modes)
+                for m in range(group):
+                    row = pl.ds(part * group + m, BLOCKS, stride=modes)
                     hb_ref[lane, seg, row, :] = h[m]
                     eb_ref[lane, seg, row, :] = e[m]
         a = a_ref[:, lanes]
@@ -188,8 +202,9 @@
     both_ref[moment, :] = second_k + power * (first_k + tokens * first_h)
 
 
-def respond_body(segments, modes, tokens, hb_ref, eb_ref, yloc_ref, a_ref, r_ref, decay_ref, partner_ref, *refs):
-    got_refs, (resp_ref, hin_ref, kin_ref) = refs[:-3], refs[-3:]
+def respond_body(segments, modes, tokens, hb_ref, eb_ref, xperm_ref, a_ref, r_ref, decay_ref, partner_ref, *refs):
+    got_refs, (resp_ref, store_ref, hin_ref, kin_ref, yloc) = refs[:-5], refs[-5:]
+    half = modes // 2
     pair, core = place()
     channels = a_ref.shape[1]
     unroll = 4
@@ -214,36 +229,43 @@
                 kin_ref[lane, seg, rowsb, :] = moment
                 moment = power * (moment + steps * state) + a * eb_ref[lane, seg, rowsb, :]
                 state = power * state + hb_ref[lane, seg, rowsb, :]
-        decays = [spread(a_ref, m, lanes) for m in range(modes)]
         for seg, (start, rows) in enumerate(segments):
             steps = rows // BLOCKS
-            edge = tuple(
-                spread(r_ref, m, lanes) * decays[m]
-                * hin_ref[lane, seg, pl.ds(m, BLOCKS, stride=modes), :]
-                for m in range(modes)
-            )
-
-            def body(outer, edge):
-                edge = list(edge)
-                for q in range(unroll):
-                    i = outer * unroll + q
-                    here = pl.ds(pl.multiple_of(start + i * BLOCKS, BLOCKS), BLOCKS)
-                    y = yloc_ref[lane, here, :]
-                    for m in range(modes):
-                        y = y + edge[m]
-                        edge[m] = edge[m] * decays[m]
-                    resp_ref[lane, pl.ds(start + i, BLOCKS, stride=steps), :] = y
-                return tuple(edge)
-
-            lax.fori_loop(0, steps // unroll, body, edge)
+            for part in range(2):
+                decays = [spread(a_ref, part * half + m, lanes) for m in range(half)]
+                weights = [spread(r_ref, part * half + m, lanes) for m in range(half)]
+
+                def body(outer, h):
+                    h = list(h)
+                    for q in range(unroll):
+                        i = outer * unroll + q
+                        here = pl.ds(pl.multiple_of(start + i * BLOCKS, BLOCKS), BLOCKS)
+                        x = xperm_ref[lane, here, :]
+                        y = None
+                        for m in range(half):
+                            h[m] = decays[m] * h[m] + x
+                            store_ref[lane, part * half + m, here, :] = h[m]
+                            term = weights[m] * h[m]
+                            y = term if y is None else y + term
+                        if part == 0:
+                            yloc[here, :] = y
+                        else:
+                            y = y + yloc[here, :]
+                            resp_ref[lane, pl.ds(start + i, BLOCKS, stride=steps), :] = y
+                    return tuple(h)
+
+                begin = tuple(
+                    hin_ref[lane, seg, pl.ds(part * half + m, BLOCKS, stride=modes), :]
+                    for m in range(half))
+                lax.fori_loop(0, steps // unroll, body, begin)
 
 
 def adjoint_body(segment, modes, received, has_previous, kept_ref, *refs):
     seg, start, rows = segment
     recv_refs = refs[:received]
     refs = refs[received + has_previous:]
-    (x1_ref, resp_ref, xperm_ref, hin_ref, kin_ref, a_ref, r_ref,
-     grad_ref, aloc_ref, gb_ref, sums_ref, nat, uperm, db, rb, mb, grad_here, sem) = refs
+    x1_ref, resp_ref, store_ref, hin_ref, kin_ref, a_ref, r_ref, grad_ref = refs[:8]
+    aloc_ref, gb_ref, sums_ref, nat, uperm, rb, qb, grad_here, sem = refs[-9:]
     steps = rows // BLOCKS
     channels = x1_ref.shape[1]
     unroll = 4
@@ -269,7 +291,7 @@
             weights = [spread(r_ref, part * half + m, lanes) for m in range(half)]
 
             def body(outer, carry):
-                g, d, racc, macc = (list(item) for item in carry)
+                g, racc, qacc = (list(item) for item in carry)
                 for q in range(unroll):
                     i = steps - 1 - (outer * unroll + q)
                     here = pl.ds(pl.multiple_of(i * BLOCKS, BLOCKS), BLOCKS)
@@ -278,38 +300,35 @@
                         uperm[lane, here, :] = u
                     else:
                         u = uperm[lane, here, :]
-                    x = xperm_ref[lane, pl.ds(pl.multiple_of(start + i * BLOCKS, BLOCKS), BLOCKS), :]
+                    there = pl.ds(pl.multiple_of(start + i * BLOCKS, BLOCKS), BLOCKS)
                     y = None
                     for m in range(half):
-                        d[m] = decays[m] * d[m] + g[m]
+                        h = store_ref[lane, part * half + m, there, :]
                         g[m] = decays[m] * g[m] + u
-                        racc[m] = racc[m] + x * g[m]
-                        macc[m] = macc[m] + x * d[m]
+                        racc[m] = racc[m] + u * h
+                        qacc[m] = qacc[m] + g[m] * h
                         term = weights[m] * g[m]
                         y = term if y is None else y + term
                     if part == 1:
                         y = y + aloc_ref[lane, here, :]
                     aloc_ref[lane, here, :] = y
-                return tuple(g), tuple(d), tuple(racc), tuple(macc)
+                return tuple(g), tuple(racc), tuple(qacc)
 
             zero = (jnp.zeros((BLOCKS, LANES), F32),) * half
-            g, d, racc, macc = lax.fori_loop(0, steps // unroll, body, (zero,) * 4)
+            g, racc, qacc = lax.fori_loop(0, steps // unroll, body, (zero,) * 3)
             for m in range(half):
                 row = pl.ds(part * half + m, BLOCKS, stride=modes)
                 gb_ref[lane, row, :] = g[m]
-                db[row, :] = d[m]
                 rb[row, :] = racc[m]
-                mb[row, :] = macc[m]
+                qb[row, :] = qacc[m]
         a = a_ref[:, lanes]
         total = jnp.zeros((modes, LANES), F32)
         moment = jnp.zeros((modes, LANES), F32)
         for b in range(BLOCKS):
             rowsb = pl.ds(b * modes, modes)
-            hin = hin_ref[lane, seg, rowsb, :]
-            ag = a * gb_ref[lane, rowsb, :]
-            total = total + rb[rowsb, :] + ag * hin
-            moment = moment + a * mb[rowsb, :] + (ag + a * a * db[rowsb, :]) * hin
-            moment = moment + ag * kin_ref[lane, seg, rowsb, :]
+            before = hin_ref[lane, seg, rowsb, :] + kin_ref[lane, seg, rowsb, :]
+            total = total + rb[rowsb, :]
+            moment = moment + qb[rowsb, :] - rb[rowsb, :] + a * gb_ref[lane, rowsb, :] * before
         sums_ref[pl.ds(0, modes), lanes] = total
         sums_ref[pl.ds(modes, modes), lanes] = moment
     copy.wait()
@@ -318,7 +337,7 @@
 def gather_body(segments, modes, *refs):
     count = len(segments)
     gb_refs, sums_refs = refs[:count], refs[count:2 * count]
-    decay_ref, out_ref = refs[2 * count:]
+    scale_ref, decay_ref, out_ref = refs[2 * count:]
     channels = decay_ref.shape[1]
     for lane in range(channels // LANES):
         lanes = pl.ds(lane * LANES, LANES)
@@ -328,16 +347,42 @@
             for b in reversed(range(BLOCKS)):
                 state = power * state + gb_refs[seg][lane, pl.ds(b * modes, modes), :]
         out_ref[pl.ds(0, modes), lanes] = state
-    out_ref[pl.ds(modes, 2 * modes), :] = sum(ref[...] for ref in sums_refs)
-
-
-def backward_pair_body(modes, tokens, message_ref, partner_ref, decay_ref, both_ref):
+    sums = sum(ref[...] for ref in sums_refs)
+    out_ref[pl.ds(modes, modes), :] = sums[:modes]
+    out_ref[pl.ds(2 * modes, modes), :] = sums[modes:] * scale_ref[...]
+
+
+def three_parts(values):
+    parts = []
+    for _ in range(3):
+        parts.append(values.astype(BF16))
+        values = values - parts[-1].astype(F32)
+    return parts
+
+
+def pick(values, chosen, dims):
+    return sum(
+        lax.dot_general(part, chosen, dims, preferred_element_type=F32)
+        for part in three_parts(values)
+    )
+
+
+def backward_pair_body(modes, tokens, owned, message_ref, partner_ref, decay_ref, both_ref):
     _, core = place()
+    channels = decay_ref.shape[1]
     state, sums = pl.ds(0, modes), pl.ds(modes, 2 * modes)
     first = jnp.where(core == 0, message_ref[state, :], partner_ref[state, :])
     second = jnp.where(core == 0, partner_ref[state, :], message_ref[state, :])
     both_ref[state, :] = first + jnp.exp(-decay_ref[...] * tokens) * second
-    both_ref[sums, :] = message_ref[sums, :] + partner_ref[sums, :]
+    channel = lax.broadcasted_iota(jnp.int32, (channels, LANES), 0)
+    lane = lax.broadcasted_iota(jnp.int32, (channels, LANES), 1)
+    wanted = (2 * (lane // owned) + core) * owned + lane % owned
+    picked = pick(message_ref[sums, :] + partner_ref[sums, :], (channel == wanted).astype(BF16),
+                  (((1,), (0,)), ((), ())))
+    tiles = channels // LANES
+    rows = 2 * modes // tiles
+    for tile in range(tiles):
+        both_ref[pl.ds(modes, rows), pl.ds(tile * LANES, LANES)] = picked[tile * rows:(tile + 1) * rows]
 
 
 def finish_body(segments, modes, tokens, length, pairs, *refs):
@@ -345,7 +390,7 @@
     aloc_refs, gb_refs = refs[:count], refs[count:2 * count]
     a_ref, r_ref, decay_ref, x2_ref, v_ref, partner_ref, both_ref = refs[2 * count:2 * count + 7]
     got_refs = refs[2 * count + 7:2 * count + 6 + pairs]
-    (gx2_ref, gv_ref, rgrad_ref, dgrad_ref, gin, nat, gx2_here, gv_here, sems) = refs[2 * count + 6 + pairs:]
+    gx2_ref, gv_ref, rgrad_ref, dgrad_ref, gin, nat, gx2_here, gv_here, sems = refs[-9:]
     channels = a_ref.shape[1]
     unroll = 4
     pair, core = place()
@@ -399,23 +444,28 @@
             copy = pltpu.make_async_copy(here.at[window, :], there.at[window, :], sems.at[seg, j])
             copy.start()
             copies.append(copy)
-    sums = both_ref[pl.ds(modes, 2 * modes), :]
+    owned = rgrad_ref.shape[0]
+    tiles = channels // LANES
+    lower = pl.ds(modes, 2 * modes // tiles)
+    sums = both_ref[lower, :]
     for got_ref in got_refs:
-        sums = sums + got_ref[pl.ds(modes, 2 * modes), :]
-    owned = rgrad_ref.shape[0]
-    row = lax.broadcasted_iota(jnp.int32, (owned, channels), 0) + lax.axis_index("ctx") * owned
-    column = lax.broadcasted_iota(jnp.int32, (owned, channels), 1)
-    pick = (row == column).astype(F32)
+        sums = sums + got_ref[lower, :]
+    row = lax.broadcasted_iota(jnp.int32, (owned, LANES), 0)
+    column = lax.broadcasted_iota(jnp.int32, (owned, LANES), 1)
+    chosen = (column == pair * owned + row).astype(BF16)
 
     def choose(values):
-        return lax.dot_general(
-            pick, values, (((1,), (1,)), ((), ())),
-            precision=lax.Precision.HIGHEST, preferred_element_type=F32,
+        return sum(
+            lax.dot_general(chosen, part, CONTRACT_LAST, preferred_element_type=F32)
+            for part in three_parts(values)
         )
 
-    rgrad_ref[...] = choose(sums[:modes]) / length
-    scale = r_ref[...] * decay_ref[...] * (float(length) ** 0.5)
-    dgrad_ref[...] = -choose(scale * sums[modes:]) / length
+    if tiles == 1:
+        residue_sums, decay_sums = sums[:modes], sums[modes:]
+    else:
+        residue_sums, decay_sums = sums[:, :LANES], sums[:, LANES:]
+    rgrad_ref[...] = choose(residue_sums) / length
+    dgrad_ref[...] = choose(decay_sums) / length
     for copy in copies:
         copy.wait()
 
@@ -450,19 +500,20 @@
     residue_t = residue.T
     a = jnp.exp(-decay_t)
     r = residue_t * length ** (-0.5)
+    scale = -residue_t * decay_t
 
     state_shape = jax.ShapeDtypeStruct((lane_tiles, count, BLOCKS * modes, LANES), F32)
     perm_shape = jax.ShapeDtypeStruct((lane_tiles, tokens, LANES), F32)
     work = tokens * channels * modes
-    xperm, yloc, hb, eb, total = pl.pallas_call(
+    xperm, hb, eb, total = pl.pallas_call(
         functools.partial(forward_body, segments, modes),
-        out_shape=[perm_shape, perm_shape, state_shape, state_shape,
+        out_shape=[perm_shape, state_shape, state_shape,
                    jax.ShapeDtypeStruct((2 * modes, channels), F32)],
         scratch_shapes=[pltpu.VMEM((lane_tiles, tokens, LANES), F32)],
         compiler_params=params(),
         cost_estimate=pl.CostEstimate(flops=work * 6, bytes_accessed=tokens * channels * 12, transcendentals=0),
         name="forward",
-    )(gate_x2, value_v, a, r, decay_t)
+    )(gate_x2, value_v, a, decay_t)
 
     pairs = context_size // 2
     partner = lax.ppermute(total, "ctx", xor_pairs(context_size, 1))
@@ -474,13 +525,15 @@
     )(total, partner, decay_t)
     got = [lax.ppermute(both, "ctx", xor_pairs(context_size, 2 * step)) for step in range(1, pairs)]
 
-    resp, hin, kin = pl.pallas_call(
+    store_shape = jax.ShapeDtypeStruct((lane_tiles, modes, tokens, LANES), F32)
+    resp, store, hin, kin = pl.pallas_call(
         functools.partial(respond_body, segments, modes, tokens),
-        out_shape=[perm_shape, state_shape, state_shape],
+        out_shape=[perm_shape, store_shape, state_shape, state_shape],
+        scratch_shapes=[pltpu.VMEM((tokens, LANES), F32)],
         compiler_params=params(),
-        cost_estimate=pl.CostEstimate(flops=work * 2, bytes_accessed=tokens * channels * 8, transcendentals=0),
+        cost_estimate=pl.CostEstimate(flops=work * 4, bytes_accessed=tokens * channels * 8, transcendentals=0),
         name="respond",
-    )(hb, eb, yloc, a, r, decay_t, partner, *got)
+    )(hb, eb, xperm, a, r, decay_t, partner, *got)
 
     alocs, gbs, sums = [], [], []
     *sent, _ = lax.optimization_barrier((*sent, got))
@@ -500,23 +553,24 @@
     for seg, (start, rows) in enumerate(segments):
         block_shape = jax.ShapeDtypeStruct((lane_tiles, BLOCKS * modes, LANES), F32)
         pieces = arrived[seg]
-        grad_x1, aloc, gb, partial_sums = pl.pallas_call(
+        *buffers, aloc, gb, partial_sums = pl.pallas_call(
             functools.partial(adjoint_body, (seg, start, rows), modes, len(pieces), len(previous)),
             in_specs=in_vmem(1 + len(pieces)) + [pl.BlockSpec(memory_space=HBM)] * len(previous) + in_vmem(7),
-            out_specs=[pl.BlockSpec(memory_space=HBM)] + in_vmem(3),
-            out_shape=[jax.ShapeDtypeStruct((tokens, channels), BF16),
+            out_specs=[pl.BlockSpec(memory_space=HBM)] * 3 + in_vmem(3),
+            out_shape=[jax.ShapeDtypeStruct((tokens, channels), BF16)] * 3
+            + [
                        jax.ShapeDtypeStruct((lane_tiles, rows, LANES), F32),
                        block_shape,
                        jax.ShapeDtypeStruct((2 * modes, channels), F32)],
             scratch_shapes=[pltpu.VMEM((lane_tiles, rows, LANES), F32)] * 2
-            + [pltpu.VMEM((BLOCKS * modes, LANES), F32)] * 3
+            + [pltpu.VMEM((BLOCKS * modes, LANES), F32)] * 2
             + [pltpu.VMEM((rows, channels), BF16), pltpu.SemaphoreType.DMA(())],
-            input_output_aliases={1 + len(pieces): 0} if previous else {},
+            input_output_aliases={1 + len(pieces) + j: j for j in range(len(previous))},
             compiler_params=params(),
-            cost_estimate=pl.CostEstimate(flops=rows * channels * modes * 10, bytes_accessed=rows * channels * 16, transcendentals=0),
+            cost_estimate=pl.CostEstimate(flops=rows * channels * modes * 8, bytes_accessed=rows * channels * 16, transcendentals=0),
             name="adjoint",
-        )(kept[seg], *pieces, *previous, gate_x1, resp, xperm, hin, kin, a, r)
-        previous = [grad_x1]
+        )(kept[seg], *pieces, *previous, gate_x1, resp, store, hin, kin, a, r)
+        previous = buffers
         alocs.append(aloc)
         gbs.append(gb)
         sums.append(partial_sums)
@@ -526,11 +580,11 @@
         out_shape=jax.ShapeDtypeStruct((3 * modes, channels), F32),
         compiler_params=params(),
         name="totals",
-    )(*gbs, *sums, decay_t)
+    )(*gbs, *sums, scale, decay_t)
     partner = lax.ppermute(message, "ctx", xor_pairs(context_size, 1))
     both = pl.pallas_call(
-        functools.partial(backward_pair_body, modes, tokens),
-        out_shape=jax.ShapeDtypeStruct((3 * modes, channels), F32),
+        functools.partial(backward_pair_body, modes, tokens, owned),
+        out_shape=jax.ShapeDtypeStruct((modes + 2 * modes // lane_tiles, channels), F32),
         compiler_params=params(),
         name="backward_pair",
     )(message, partner, decay_t)
@@ -538,7 +592,7 @@
 
     grad_x2, grad_v, residue_grad, decay_grad = pl.pallas_call(
         functools.partial(finish_body, segments, modes, tokens, length, pairs),
-        in_specs=in_vmem(2 * count + 6 + pairs),
+        in_specs=in_vmem(2 * count + 6 + pairs) + [pl.BlockSpec(memory_space=HBM)] * 2,
         out_specs=[pl.BlockSpec(memory_space=HBM)] * 2 + in_vmem(2),
         out_shape=[jax.ShapeDtypeStruct((tokens, channels), BF16)] * 2
         + [jax.ShapeDtypeStruct((owned, modes), F32)] * 2,
@@ -547,11 +601,12 @@
                         pltpu.VMEM((tokens, channels), BF16),
                         pltpu.VMEM((tokens, channels), BF16),
                         pltpu.SemaphoreType.DMA((count, 2))],
+        input_output_aliases={2 * count + 6 + pairs: 0, 2 * count + 7 + pairs: 1},
         compiler_params=params(),
         cost_estimate=pl.CostEstimate(flops=work * 2, bytes_accessed=tokens * channels * 12, transcendentals=0),
         name="finish",
-    )(*alocs, *gbs, a, r, decay_t, gate_x2, value_v, partner, both, *got)
-    return grad_x1, grad_x2, grad_v, residue_grad, decay_grad
+    )(*alocs, *gbs, a, r, decay_t, gate_x2, value_v, partner, both, *got, *previous[1:])
+    return previous[0], grad_x2, grad_v, residue_grad, decay_grad
 
 
 def solution(mesh):

time: 59.2 us -> 55.5 us (0.938)
  waiting for transfers between devices: 13.5 us -> 10.4 us
  Pallas kernels: 27.3 us -> 25.9 us
  starting transfers between devices: 13.8 us -> 14.7 us
    ppermute x6, waiting for transfers between devices: 8.8 us -> 6.37 us  [on_device(): lax.ppermute(both, 'ctx', xor_pairs(context_size, 2 * step))]
    pallas_call x1, Pallas kernels: 5.14 us -> 3.76 us  [on_device(): pl.pallas_call(functools.partial(forward_body, segments, modes), out_shap...]
    pallas_call x1, Pallas kernels: 2.21 us -> 3.58 us  [on_device(): pl.pallas_call(functools.partial(respond_body, segments, modes, tokens),...]
    pallas_call x2, Pallas kernels: 8.29 us -> 7.09 us  [on_device(): pl.pallas_call(functools.partial(adjoint_body, (seg, start, rows), modes,...]
    ppermute x6, starting transfers between devices: 8 us -> 8.9 us  [on_device(): lax.ppermute(both, 'ctx', xor_pairs(context_size, 2 * step))]
    ppermute x2, waiting for transfers between devices: 2.32 us -> 1.6 us  [on_device(): lax.ppermute(away.astype(BF16), 'ch', xor_pairs(ch_size, order[level]))]
where the time goes in v2:
time: 55.5 us; the launch traced here: 55.3 us
  Pallas kernels  25.9 us (47%)
  starting transfers between devices  14.7 us (26%)
  waiting for transfers between devices  10.4 us (19%)
  other arithmetic  2.04 us (4%)
  local copies, waits for them, and re-layouts  1.37 us (2%)
  between operations  0.82 us (1%)
    ppermute x6, starting transfers between devices, on_device(): lax.ppermute(both, 'ctx', xor_pairs(context_size, 2 * step))  8.9 us
    pallas_call x1, Pallas kernels, project(): pl.pallas_call(functools.partial(project_body, work, width, pieces), in_s...  7.91 us
    pallas_call x2, Pallas kernels, on_device(): pl.pallas_call(functools.partial(adjoint_body, (seg, start, rows), modes,...  7.09 us
    ppermute x6, waiting for transfers between devices, on_device(): lax.ppermute(both, 'ctx', xor_pairs(context_size, 2 * step))  6.37 us
    ppermute x2, starting transfers between devices, on_device(): lax.ppermute(piece, 'ch', xor_pairs(ch_size, order[0]))  4.52 us
    pallas_call x1, Pallas kernels, on_device(): pl.pallas_call(functools.partial(forward_body, segments, modes), out_shap...  3.76 us
    pallas_call x1, Pallas kernels, on_device(): pl.pallas_call(functools.partial(respond_body, segments, modes, tokens),...  3.58 us
    pallas_call x1, Pallas kernels, on_device(): pl.pallas_call(functools.partial(finish_body, segments, modes, tokens, le...  3.36 us
  transfers between devices with their start and end apart: 12, of which 7 were waited for; matrix products, arithmetic and copies ran while one was open for 2% of the time, Pallas kernels for 20%

profile of v2, /device:TPU:0, one launch (start us, length us, event | category | flops | bytes accessed | tf_op | source)
XLA Modules:
  0.0 55.3 jit_solution(1003222991446225451)
XLA Ops:
  0.6 0.0 copy-start.5
  0.6 0.0 copy-start.6
  0.7 0.0 copy-start.2
  0.7 0.0 copy-start.1
  0.7 7.9 %project.1 = (bf16[512,512]{1,0:T(8,128)(2,1)}, bf16[512,512]{1,0:T(8,128)(2,1)}, bf16[512,512]{1,0:T(8,128)(2,1)}, bf16[512,512]{1,0:T(8,128)(2,1)}) custom-call(bf16[1024,2048]{1,0:T(8,128)(2,1)} %g_ref.1, bf16[1024,2048]{1,0:T(8,128)(2,1)} %w_ref.1), custom_call_target="tpu_custom_call" | custom-call | tf_op jit(solution)/shard_map/project/pallas_call | solution.py:117
  8.6 0.0 copy-start
  8.6 0.0 copy-start.4
  8.6 3.0 %collective-permute-start = (bf16[512,512]{1,0:T(8,128)(2,1)}, bf16[512,512]{1,0:T(8,128)(2,1)S(1)}, u32[]{:S(2)}, u32[]{:S(2)}) collective-permute-start(bf16[512,512]{1,0:T(8,128)(2,1)} %get-tuple-element.36), channel_id=1, source_target_pairs={{0,1},{1,0},{2,3},{3,2},{4,5},{5,4},{6,7},{7,6},{8,9},{9,8},{10,11... | collective-permute-start | bytes 1572872 | tf_op jit(solution)/shard_map/ppermute | solution.py:495
  11.6 1.5 %collective-permute-start.1 = (bf16[512,512]{1,0:T(8,128)(2,1)}, bf16[512,512]{1,0:T(8,128)(2,1)S(1)}, u32[]{:S(2)}, u32[]{:S(2)}) collective-permute-start(bf16[512,512]{1,0:T(8,128)(2,1)} %get-tuple-element.37), channel_id=1, source_target_pairs={{0,2},{1,3},{2,0},{3,1},{4,6},{5,7},{6,4},{7,5},{8,10},{9,11},{10,... | collective-permute-start | bytes 1572872 | tf_op jit(solution)/shard_map/ppermute | solution.py:495
  13.1 0.0 copy-done.5
  13.1 0.0 copy-done.6
  13.2 0.0 copy-done.2
  13.2 0.0 copy-done.1
  13.2 3.8 %forward.1 = (f32[2,1024,128]{2,1,0:T(8,128)S(1)}, f32[2,2,128,128]{3,2,1,0:T(8,128)S(1)}, f32[2,2,128,128]{3,2,1,0:T(8,128)S(1)}, f32[32,256]{1,0:T(8,128)S(1)}) custom-call(bf16[1024,256]{1,0:T(8,128)(2,1)S(1)} %copy-done.1, bf16[1024,256]{1,0:T(8,128)(2,1)S(1)} %copy-done.2, f32[16,256]{1,0:T(8,128)S(1)} %get-tuple-element.71.a_ref.refs_7_.refs_10_.refs_4_, ...), custom_call_target="tpu_custom_call" | custom-call | flops 25165824 | bytes 3145728 | tf_op jit(solution)/shard_map/forward/pallas_call | solution.py:508
  16.9 0.1 collective-permute-start.2
  17.0 1.2 %collective-permute-done.2.partner_ref = f32[32,256]{1,0:T(8,128)S(1)} collective-permute-done((f32[32,256]{1,0:T(8,128)S(1)}, f32[32,256]{1,0:T(8,128)S(1)}, u32[]{:S(2)}, u32[]{:S(2)}) %collective-permute-start.2) | collective-permute-done | bytes 32800 | tf_op jit(solution)/shard_map/ppermute | solution.py:519
  18.2 3.7 %collective-permute-start.5 = (f32[32,256]{1,0:T(8,128)S(1)}, f32[32,256]{1,0:T(8,128)S(1)}, u32[]{:S(2)}, u32[]{:S(2)}) collective-permute-start(f32[32,256]{1,0:T(8,128)S(1)} %forward_pair.1), channel_id=1, source_target_pairs={{0,24},{4,28},{8,16},{12,20},{16,8},{20,12},{24,0},{28,4},{1,25},{... | collective-permute-start | bytes 98312 | tf_op jit(solution)/shard_map/ppermute | solution.py:526
  21.9 0.0 collective-permute-start.4
  21.9 0.8 %collective-permute-start.3 = (f32[32,256]{1,0:T(8,128)S(1)}, f32[32,256]{1,0:T(8,128)S(1)}, u32[]{:S(2)}, u32[]{:S(2)}) collective-permute-start(f32[32,256]{1,0:T(8,128)S(1)} %forward_pair.1), channel_id=1, source_target_pairs={{0,8},{4,12},{8,0},{12,4},{16,24},{20,28},{24,16},{28,20},{1,9},{5... | collective-permute-start | bytes 98312 | tf_op jit(solution)/shard_map/ppermute | solution.py:526
  22.7 1.3 %collective-permute-done.5.refs_2_ = f32[32,256]{1,0:T(8,128)S(1)} collective-permute-done((f32[32,256]{1,0:T(8,128)S(1)}, f32[32,256]{1,0:T(8,128)S(1)}, u32[]{:S(2)}, u32[]{:S(2)}) %collective-permute-start.5) | collective-permute-done | bytes 32800 | tf_op jit(solution)/shard_map/ppermute | solution.py:526
  24.0 2.7 %collective-permute-done.4.refs_1_ = f32[32,256]{1,0:T(8,128)S(1)} collective-permute-done((f32[32,256]{1,0:T(8,128)S(1)}, f32[32,256]{1,0:T(8,128)S(1)}, u32[]{:S(2)}, u32[]{:S(2)}) %collective-permute-start.4) | collective-permute-done | bytes 32800 | tf_op jit(solution)/shard_map/ppermute | solution.py:526
  26.7 0.0 collective-permute-done.3.refs_0_
  26.7 0.0 collective-permute-done.refs_0_
  26.7 0.0 collective-permute-done.1.refs_0_
  26.7 1.0 %add_convert_fusion = bf16[512,256]{1,0:T(8,128)(2,1)S(1)} fusion(bf16[512,512]{1,0:T(8,128)(2,1)S(1)} %collective-permute-done.refs_0_, bf16[512,512]{1,0:T(8,128)(2,1)} %get-tuple-element.40.kept_ref), kind=kLoop, calls=%fused_computation | loop fusion | flops 524288 | bytes 786432 | tf_op jit(solution)/shard_map/convert_element_type | solution.py:551
  27.8 0.6 %collective-permute-start.7 = (bf16[512,256]{1,0:T(8,128)(2,1)S(1)}, bf16[512,256]{1,0:T(8,128)(2,1)S(1)}, u32[]{:S(2)}, u32[]{:S(2)}) collective-permute-start(bf16[512,256]{1,0:T(8,128)(2,1)S(1)} %add_convert_fusion), channel_id=1, source_target_pairs={{0,2},{1,3},{2,0},{3,1},{4,6},{5,7},{6,4},{7,5},{8,10},{9,11},{10,... | collective-permute-start | bytes 786440 | tf_op jit(solution)/shard_map/ppermute | solution.py:551
  28.3 1.0 %add_convert_fusion.1 = bf16[512,256]{1,0:T(8,128)(2,1)S(1)} fusion(bf16[512,512]{1,0:T(8,128)(2,1)S(1)} %collective-permute-done.1.refs_0_, bf16[512,512]{1,0:T(8,128)(2,1)} %get-tuple-element.35.kept_ref), kind=kLoop, calls=%fused_computation.1 | loop fusion | flops 524288 | bytes 786432 | tf_op jit(solution)/shard_map/convert_element_type | solution.py:551
  29.3 0.6 %collective-permute-start.6 = (bf16[512,256]{1,0:T(8,128)(2,1)S(1)}, bf16[512,256]{1,0:T(8,128)(2,1)S(1)}, u32[]{:S(2)}, u32[]{:S(2)}) collective-permute-start(bf16[512,256]{1,0:T(8,128)(2,1)S(1)} %add_convert_fusion.1), channel_id=1, source_target_pairs={{0,1},{1,0},{2,3},{3,2},{4,5},{5,4},{6,7},{7,6},{8,9},{9,8},{10,11... | collective-permute-start | bytes 786440 | tf_op jit(solution)/shard_map/ppermute | solution.py:551
  29.9 3.6 %respond.1 = (f32[2,1024,128]{2,1,0:T(8,128)S(1)}, f32[2,16,1024,128]{3,2,1,0:T(8,128)S(1)}, f32[2,2,128,128]{3,2,1,0:T(8,128)S(1)}, f32[2,2,128,128]{3,2,1,0:T(8,128)S(1)}) custom-call(f32[2,2,128,128]{3,2,1,0:T(8,128)S(1)} %get-tuple-element.42.hb_ref, f32[2,2,128,128]{3,2,1,0:T(8,128)S(1)} %get-tuple-element.43.eb_ref, ...), custom_call_target="tpu_custom_call" | custom-call | flops 16777216 | bytes 2097152 | tf_op jit(solution)/shard_map/respond/pallas_call | solution.py:529
  33.5 1.6 %collective-permute-done.7.refs_1_ = bf16[512,256]{1,0:T(8,128)(2,1)S(1)} collective-permute-done((bf16[512,256]{1,0:T(8,128)(2,1)S(1)}, bf16[512,256]{1,0:T(8,128)(2,1)S(1)}, u32[]{:S(2)}, u32[]{:S(2)}) %collective-permute-start.7) | collective-permute-done | bytes 262176 | tf_op jit(solution)/shard_map/ppermute | solution.py:551
  35.1 0.0 copy-done
  35.1 0.0 copy-done.4
  35.1 0.0 copy-start.3
  35.1 3.5 %adjoint.2 = (bf16[1024,256]{1,0:T(8,128)(2,1)}, bf16[1024,256]{1,0:T(8,128)(2,1)}, bf16[1024,256]{1,0:T(8,128)(2,1)}, f32[2,512,128]{2,1,0:T(8,128)S(1)}, f32[2...) custom-call(bf16[512,512]{1,0:T(8,128)(2,1)S(1)} %copy-done.4, bf16[512,512]{1,0:T(8,128)(2,1)S(1)} %collective-permute-done.refs_0_, ...), custom_call_target="tpu_custom_call" | custom-call | flops 16777216 | bytes 2097152 | tf_op jit(solution)/shard_map/adjoint/pallas_call | solution.py:556
  38.7 0.0 collective-permute-done.6.refs_1_
  38.7 0.0 copy-done.3
  38.7 3.5 %adjoint.3 = (bf16[1024,256]{1,0:T(8,128)(2,1)}, bf16[1024,256]{1,0:T(8,128)(2,1)}, bf16[1024,256]{1,0:T(8,128)(2,1)}, f32[2,512,128]{2,1,0:T(8,128)S(1)}, f32[2...) custom-call(bf16[512,512]{1,0:T(8,128)(2,1)S(1)} %copy-done.3, ...), custom_call_target="tpu_custom_call", output_to_operand_aliasing={{0}: (3, {}), {1}: (4, {}), {2}: (5, {})} | custom-call | flops 16777216 | bytes 2097152 | tf_op jit(solution)/shard_map/adjoint/pallas_call | solution.py:556
  42.3 0.1 totals.1.message_ref
  42.3 0.1 collective-permute-start.8
  42.4 1.2 %collective-permute-done.8.partner_ref.refs_9_ = f32[48,256]{1,0:T(8,128)S(1)} collective-permute-done((f32[48,256]{1,0:T(8,128)S(1)}, f32[48,256]{1,0:T(8,128)S(1)}, u32[]{:S(2)}, u32[]{:S(2)}) %collective-permute-start.8) | collective-permute-done | bytes 49184 | tf_op jit(solution)/shard_map/ppermute | solution.py:584
  43.6 0.2 backward_pair.1.refs_10_
  43.8 1.7 %collective-permute-start.11 = (f32[32,256]{1,0:T(8,128)S(1)}, f32[32,256]{1,0:T(8,128)S(1)}, u32[]{:S(2)}, u32[]{:S(2)}) collective-permute-start(f32[32,256]{1,0:T(8,128)S(1)} %backward_pair.1.refs_10_), channel_id=1, source_target_pairs={{0,24},{4,28},{8,16},{12,20},{16,8},{20,12},{24,0},{28,4},{1,25},{... | collective-permute-start | bytes 98312 | tf_op jit(solution)/shard_map/ppermute | solution.py:591
  45.4 0.1 collective-permute-start.10
  45.6 2.6 %collective-permute-start.9 = (f32[32,256]{1,0:T(8,128)S(1)}, f32[32,256]{1,0:T(8,128)S(1)}, u32[]{:S(2)}, u32[]{:S(2)}) collective-permute-start(f32[32,256]{1,0:T(8,128)S(1)} %backward_pair.1.refs_10_), channel_id=1, source_target_pairs={{0,8},{4,12},{8,0},{12,4},{16,24},{20,28},{24,16},{28,20},{1,9},{5... | collective-permute-start | bytes 98312 | tf_op jit(solution)/shard_map/ppermute | solution.py:591
  48.2 1.5 %collective-permute-done.11.refs_13_ = f32[32,256]{1,0:T(8,128)S(1)} collective-permute-done((f32[32,256]{1,0:T(8,128)S(1)}, f32[32,256]{1,0:T(8,128)S(1)}, u32[]{:S(2)}, u32[]{:S(2)}) %collective-permute-start.11) | collective-permute-done | bytes 32800 | tf_op jit(solution)/shard_map/ppermute | solution.py:591
  49.7 0.9 %collective-permute-done.10.refs_12_ = f32[32,256]{1,0:T(8,128)S(1)} collective-permute-done((f32[32,256]{1,0:T(8,128)S(1)}, f32[32,256]{1,0:T(8,128)S(1)}, u32[]{:S(2)}, u32[]{:S(2)}) %collective-permute-start.10) | collective-permute-done | bytes 32800 | tf_op jit(solution)/shard_map/ppermute | solution.py:591
  50.6 0.0 collective-permute-done.9.refs_11_
  50.6 3.4 %finish.1 = (bf16[1024,256]{1,0:T(8,128)(2,1)}, bf16[1024,256]{1,0:T(8,128)(2,1)}, f32[32,16]{1,0:T(8,128)S(1)}, f32[32,16]{1,0:T(8,128)S(1)}) custom-call(f32[2,512,128]{2,1,0:T(8,128)S(1)} %get-tuple-element.53.refs_0_, f32[2,512,128]{2,1,0:T(8,128)S(1)} %get-tuple-element.54.refs_1_, ...), custom_call_target="tpu_custom_call", output_to_operand_aliasing={{0}: (14, {}), {1}: (15, {})} | custom-call | flops 8388608 | bytes 3145728 | tf_op jit(solution)/shard_map/finish/pallas_call | solution.py:593
  53.9 0.7 %copy.17 = f32[32,16]{0,1:T(8,128)} copy(f32[32,16]{1,0:T(8,128)S(1)} %get-tuple-element.68) | data formatting | bytes 4096
  54.6 0.7 %copy.18 = f32[32,16]{0,1:T(8,128)} copy(f32[32,16]{1,0:T(8,128)S(1)} %get-tuple-element.69) | data formatting | bytes 4096
  (3 shorter events, 0.0 us)
Async XLA Ops:
  0.6 12.5 %copy-start.5 = (f32[256,16]{0,1:T(8,128)S(1)}, f32[256,16]{0,1:T(8,128)}, u32[]{:S(2)}) copy-start(f32[256,16]{0,1:T(8,128)} %param.13) | copy-start | bytes 49156
  0.6 12.5 %copy-start.6 = (f32[256,16]{0,1:T(8,128)S(1)}, f32[256,16]{0,1:T(8,128)}, u32[]{:S(2)}) copy-start(f32[256,16]{0,1:T(8,128)} %param.12) | copy-start | bytes 49156
  0.7 12.5 %copy-start.2 = (bf16[1024,256]{1,0:T(8,128)(2,1)S(1)}, bf16[1024,256]{1,0:T(8,128)(2,1)}, u32[]{:S(2)}) copy-start(bf16[1024,256]{1,0:T(8,128)(2,1)} %refs_8_.1) | copy-start | bytes 1572868
  0.7 12.5 %copy-start.1 = (bf16[1024,256]{1,0:T(8,128)(2,1)S(1)}, bf16[1024,256]{1,0:T(8,128)(2,1)}, u32[]{:S(2)}) copy-start(bf16[1024,256]{1,0:T(8,128)(2,1)} %refs_7_.1) | copy-start | bytes 1572868
  8.6 26.5 %copy-start = (bf16[1024,256]{1,0:T(8,128)(2,1)S(1)}, bf16[1024,256]{1,0:T(8,128)(2,1)}, u32[]{:S(2)}) copy-start(bf16[1024,256]{1,0:T(8,128)(2,1)} %refs_5_.1) | copy-start | bytes 1572868
  8.6 26.5 %copy-start.4 = (bf16[512,512]{1,0:T(8,128)(2,1)S(1)}, bf16[512,512]{1,0:T(8,128)(2,1)}, u32[]{:S(2)}) copy-start(bf16[512,512]{1,0:T(8,128)(2,1)} %get-tuple-element.40.kept_ref) | copy-start | bytes 1572868
  8.6 18.1 %collective-permute-start = (bf16[512,512]{1,0:T(8,128)(2,1)}, bf16[512,512]{1,0:T(8,128)(2,1)S(1)}, u32[]{:S(2)}, u32[]{:S(2)}) collective-permute-start(bf16[512,512]{1,0:T(8,128)(2,1)} %get-tuple-element.36), channel_id=1, source_target_pairs={{0,1},{1,0},{2,3},{3,2},{4,5},{5,4},{6,7},{7,6},{8,9},{9,8},{10,11... | collective-permute-start | bytes 1572872 | tf_op jit(solution)/shard_map/ppermute | solution.py:495
  11.6 15.1 %collective-permute-start.1 = (bf16[512,512]{1,0:T(8,128)(2,1)}, bf16[512,512]{1,0:T(8,128)(2,1)S(1)}, u32[]{:S(2)}, u32[]{:S(2)}) collective-permute-start(bf16[512,512]{1,0:T(8,128)(2,1)} %get-tuple-element.37), channel_id=1, source_target_pairs={{0,2},{1,3},{2,0},{3,1},{4,6},{5,7},{6,4},{7,5},{8,10},{9,11},{10,... | collective-permute-start | bytes 1572872 | tf_op jit(solution)/shard_map/ppermute | solution.py:495
  16.9 1.3 %collective-permute-start.2 = (f32[32,256]{1,0:T(8,128)S(1)}, f32[32,256]{1,0:T(8,128)S(1)}, u32[]{:S(2)}, u32[]{:S(2)}) collective-permute-start(f32[32,256]{1,0:T(8,128)S(1)} %get-tuple-element.38.total_ref), channel_id=1, source_target_pairs={{0,4},{4,0},{8,12},{12,8},{16,20},{20,16},{24,28},{28,24},{1,5},{5... | collective-permute-start | bytes 98312 | tf_op jit(solution)/shard_map/ppermute | solution.py:519
  18.2 5.8 %collective-permute-start.5 = (f32[32,256]{1,0:T(8,128)S(1)}, f32[32,256]{1,0:T(8,128)S(1)}, u32[]{:S(2)}, u32[]{:S(2)}) collective-permute-start(f32[32,256]{1,0:T(8,128)S(1)} %forward_pair.1), channel_id=1, source_target_pairs={{0,24},{4,28},{8,16},{12,20},{16,8},{20,12},{24,0},{28,4},{1,25},{... | collective-permute-start | bytes 98312 | tf_op jit(solution)/shard_map/ppermute | solution.py:526
  21.9 4.8 %collective-permute-start.4 = (f32[32,256]{1,0:T(8,128)S(1)}, f32[32,256]{1,0:T(8,128)S(1)}, u32[]{:S(2)}, u32[]{:S(2)}) collective-permute-start(f32[32,256]{1,0:T(8,128)S(1)} %forward_pair.1), channel_id=1, source_target_pairs={{0,16},{4,20},{8,24},{12,28},{16,0},{20,4},{24,8},{28,12},{1,17},{... | collective-permute-start | bytes 98312 | tf_op jit(solution)/shard_map/ppermute | solution.py:526
  21.9 4.8 %collective-permute-start.3 = (f32[32,256]{1,0:T(8,128)S(1)}, f32[32,256]{1,0:T(8,128)S(1)}, u32[]{:S(2)}, u32[]{:S(2)}) collective-permute-start(f32[32,256]{1,0:T(8,128)S(1)} %forward_pair.1), channel_id=1, source_target_pairs={{0,8},{4,12},{8,0},{12,4},{16,24},{20,28},{24,16},{28,20},{1,9},{5... | collective-permute-start | bytes 98312 | tf_op jit(solution)/shard_map/ppermute | solution.py:526
  27.8 7.4 %collective-permute-start.7 = (bf16[512,256]{1,0:T(8,128)(2,1)S(1)}, bf16[512,256]{1,0:T(8,128)(2,1)S(1)}, u32[]{:S(2)}, u32[]{:S(2)}) collective-permute-start(bf16[512,256]{1,0:T(8,128)(2,1)S(1)} %add_convert_fusion), channel_id=1, source_target_pairs={{0,2},{1,3},{2,0},{3,1},{4,6},{5,7},{6,4},{7,5},{8,10},{9,11},{10,... | collective-permute-start | bytes 786440 | tf_op jit(solution)/shard_map/ppermute | solution.py:551
  29.3 9.3 %collective-permute-start.6 = (bf16[512,256]{1,0:T(8,128)(2,1)S(1)}, bf16[512,256]{1,0:T(8,128)(2,1)S(1)}, u32[]{:S(2)}, u32[]{:S(2)}) collective-permute-start(bf16[512,256]{1,0:T(8,128)(2,1)S(1)} %add_convert_fusion.1), channel_id=1, source_target_pairs={{0,1},{1,0},{2,3},{3,2},{4,5},{5,4},{6,7},{7,6},{8,9},{9,8},{10,11... | collective-permute-start | bytes 786440 | tf_op jit(solution)/shard_map/ppermute | solution.py:551
  35.1 3.6 %copy-start.3 = (bf16[512,512]{1,0:T(8,128)(2,1)S(1)}, bf16[512,512]{1,0:T(8,128)(2,1)}, u32[]{:S(2)}) copy-start(bf16[512,512]{1,0:T(8,128)(2,1)} %get-tuple-element.35.kept_ref) | copy-start | bytes 1572868
  42.3 1.3 %collective-permute-start.8 = (f32[48,256]{1,0:T(8,128)S(1)}, f32[48,256]{1,0:T(8,128)S(1)}, u32[]{:S(2)}, u32[]{:S(2)}) collective-permute-start(f32[48,256]{1,0:T(8,128)S(1)} %totals.1.message_ref), channel_id=1, source_target_pairs={{0,4},{4,0},{8,12},{12,8},{16,20},{20,16},{24,28},{28,24},{1,5},{5... | collective-permute-start | bytes 147464 | tf_op jit(solution)/shard_map/ppermute | solution.py:584
  43.8 5.9 %collective-permute-start.11 = (f32[32,256]{1,0:T(8,128)S(1)}, f32[32,256]{1,0:T(8,128)S(1)}, u32[]{:S(2)}, u32[]{:S(2)}) collective-permute-start(f32[32,256]{1,0:T(8,128)S(1)} %backward_pair.1.refs_10_), channel_id=1, source_target_pairs={{0,24},{4,28},{8,16},{12,20},{16,8},{20,12},{24,0},{28,4},{1,25},{... | collective-permute-start | bytes 98312 | tf_op jit(solution)/shard_map/ppermute | solution.py:591
  45.4 5.1 %collective-permute-start.10 = (f32[32,256]{1,0:T(8,128)S(1)}, f32[32,256]{1,0:T(8,128)S(1)}, u32[]{:S(2)}, u32[]{:S(2)}) collective-permute-start(f32[32,256]{1,0:T(8,128)S(1)} %backward_pair.1.refs_10_), channel_id=1, source_target_pairs={{0,16},{4,20},{8,24},{12,28},{16,0},{20,4},{24,8},{28,12},{1,17},{... | collective-permute-start | bytes 98312 | tf_op jit(solution)/shard_map/ppermute | solution.py:591
  45.6 5.0 %collective-permute-start.9 = (f32[32,256]{1,0:T(8,128)S(1)}, f32[32,256]{1,0:T(8,128)S(1)}, u32[]{:S(2)}, u32[]{:S(2)}) collective-permute-start(f32[32,256]{1,0:T(8,128)S(1)} %backward_pair.1.refs_10_), channel_id=1, source_target_pairs={{0,8},{4,12},{8,0},{12,4},{16,24},{20,28},{24,16},{28,20},{1,9},{5... | collective-permute-start | bytes 98312 | tf_op jit(solution)/shard_map/ppermute | solution.py:591

commit v3 on v2

--- a/solution.py
+++ b/solution.py
@@ -9,7 +9,8 @@
 
 LANES = 128
 PIECES = 2
-FPARTS = 1
+FPARTS = 2
+KEPT = jnp.bfloat16
 BLOCKS = 8
 F32 = jnp.float32
 BF16 = jnp.bfloat16
@@ -33,6 +34,10 @@
 
 def params(mebibytes=24):
     return pltpu.CompilerParams(vmem_limit_bytes=mebibytes * 2**20)
+
+
+def cost(microseconds):
+    return pl.CostEstimate(flops=int(microseconds * 1.1e9), bytes_accessed=0, transcendentals=0)
 
 
 def in_vmem(count):
@@ -62,7 +67,8 @@
 def project_body(work, width, pieces, g_ref, w_ref, *refs):
     count = len(work)
     out_refs = refs[:count]
-    g_here, w_here, total, g_sems, w_sems = refs[count:]
+    out_here = refs[count:2 * count]
+    g_here, w_here, total, g_sems, w_sems, out_sems = refs[2 * count:]
     depth = g_ref.shape[1] // pieces
     arranged = arrange(w_ref.shape[0] // width)
     pending = {}
@@ -86,7 +92,9 @@
                 if key not in pending:
                     pending[key] = copy()
                     pending[key].start()
-    for (start, rows, offsets), out_ref in zip(work, out_refs):
+    leaving = []
+    for which, (start, rows, offsets) in enumerate(work):
+        out_ref = out_here[which]
         for piece in range(pieces):
             columns = pl.ds(piece * depth, depth)
             for key in [(start, piece)] + [(-1 - offset, piece) for offset in offsets]:
@@ -107,6 +115,10 @@
                         total[:, here] = value
                     else:
                         out_ref[:, here] = value.astype(out_ref.dtype)
+        leaving.append(pltpu.make_async_copy(out_ref, out_refs[which], out_sems.at[which]))
+        leaving[-1].start()
+    for copy in leaving:
+        copy.wait()
 
 
 def project(g_out, w_out, work, width):
@@ -117,17 +129,40 @@
     return pl.pallas_call(
         functools.partial(project_body, work, width, pieces),
         in_specs=[pl.BlockSpec(memory_space=HBM)] * 2,
-        out_specs=in_vmem(len(work)),
+        out_specs=[pl.BlockSpec(memory_space=HBM)] * len(work),
         out_shape=shapes,
-        scratch_shapes=[
+        scratch_shapes=[pltpu.VMEM(shape.shape, BF16) for shape in shapes] + [
             pltpu.VMEM(g_out.shape, BF16),
             pltpu.VMEM(w_out.shape, BF16),
             pltpu.VMEM(shapes[0].shape, F32),
             pltpu.SemaphoreType.DMA((groups, pieces)),
             pltpu.SemaphoreType.DMA((blocks, pieces)),
+            pltpu.SemaphoreType.DMA((len(work),)),
         ],
         compiler_params=params(60),
+        cost_estimate=cost(5),
         name="project",
+    )(g_out, w_out)
+
+
+def project_kept_body(work, width, g_ref, w_ref, *out_refs):
+    for (start, rows, offsets), out_ref in zip(work, out_refs):
+        for spot, offset in enumerate(offsets):
+            out_ref[:, pl.ds(spot * width, width)] = lax.dot_general(
+                g_ref[pl.ds(start, rows), :], w_ref[block_rows(offset, width), :],
+                CONTRACT_LAST, preferred_element_type=F32).astype(out_ref.dtype)
+
+
+def project_kept(g_out, w_out, work, width):
+    return pl.pallas_call(
+        functools.partial(project_kept_body, work, width),
+        in_specs=in_vmem(2),
+        out_specs=in_vmem(len(work)),
+        out_shape=[jax.ShapeDtypeStruct((rows, len(offsets) * width), KEPT)
+                   for _, rows, offsets in work],
+        compiler_params=params(),
+        cost_estimate=cost(3),
+        name="project_kept",
     )(g_out, w_out)
 
 
@@ -264,8 +299,8 @@
     seg, start, rows = segment
     recv_refs = refs[:received]
     refs = refs[received + has_previous:]
-    x1_ref, resp_ref, store_ref, hin_ref, kin_ref, a_ref, r_ref, grad_ref = refs[:8]
-    aloc_ref, gb_ref, sums_ref, nat, uperm, rb, qb, grad_here, sem = refs[-9:]
+    x1_ref, resp_ref, store_ref, hin_ref, kin_ref, a_ref, grad_ref = refs[:7]
+    uperm, gb_ref, sums_ref, nat, rb, qb, grad_here, sem = refs[-8:]
     steps = rows // BLOCKS
     channels = x1_ref.shape[1]
     unroll = 4
@@ -288,7 +323,6 @@
         lanes = pl.ds(lane * LANES, LANES)
         for part in range(2):
             decays = [spread(a_ref, part * half + m, lanes) for m in range(half)]
-            weights = [spread(r_ref, part * half + m, lanes) for m in range(half)]
 
             def body(outer, carry):
                 g, racc, qacc = (list(item) for item in carry)
@@ -301,17 +335,11 @@
                     else:
                         u = uperm[lane, here, :]
                     there = pl.ds(pl.multiple_of(start + i * BLOCKS, BLOCKS), BLOCKS)
-                    y = None
                     for m in range(half):
                         h = store_ref[lane, part * half + m, there, :]
                         g[m] = decays[m] * g[m] + u
                         racc[m] = racc[m] + u * h
                         qacc[m] = qacc[m] + g[m] * h
-                        term = weights[m] * g[m]
-                        y = term if y is None else y + term
-                    if part == 1:
-                        y = y + aloc_ref[lane, here, :]
-                    aloc_ref[lane, here, :] = y
                 return tuple(g), tuple(racc), tuple(qacc)
 
             zero = (jnp.zeros((BLOCKS, LANES), F32),) * half
@@ -334,6 +362,46 @@
     copy.wait()
 
 
+def local_body(segments, modes, seg, uperm_ref, *refs):
+    count = len(segments)
+    gb_refs = refs[:count - seg]
+    a_ref, r_ref, decay_ref, aloc_ref, gin = refs[count - seg:]
+    channels = a_ref.shape[1]
+    unroll = 4
+    half = modes // 2
+    for lane in range(channels // LANES):
+        lanes = pl.ds(lane * LANES, LANES)
+        state = jnp.zeros((modes, LANES), F32)
+        for other in reversed(range(seg, count)):
+            steps = segments[other][1] // BLOCKS
+            power = jnp.exp(-decay_ref[:, lanes] * steps)
+            for b in reversed(range(BLOCKS)):
+                rowsb = pl.ds(b * modes, modes)
+                if other == seg:
+                    gin[rowsb, :] = state
+                state = power * state + gb_refs[other - seg][lane, rowsb, :]
+        for part in range(2):
+            decays = [spread(a_ref, part * half + m, lanes) for m in range(half)]
+            weights = [spread(r_ref, part * half + m, lanes) for m in range(half)]
+
+            def body(outer, g):
+                g = list(g)
+                for q in range(unroll):
+                    i = steps - 1 - (outer * unroll + q)
+                    here = pl.ds(pl.multiple_of(i * BLOCKS, BLOCKS), BLOCKS)
+                    u = uperm_ref[lane, here, :]
+                    y = None if part == 0 else aloc_ref[lane, here, :]
+                    for m in range(half):
+                        g[m] = decays[m] * g[m] + u
+                        term = weights[m] * g[m]
+                        y = term if y is None else y + term
+                    aloc_ref[lane, here, :] = y
+                return tuple(g)
+
+            begin = tuple(gin[pl.ds(part * half + m, BLOCKS, stride=modes), :] for m in range(half))
+            lax.fori_loop(0, steps // unroll, body, begin)
+
+
 def gather_body(segments, modes, *refs):
     count = len(segments)
     gb_refs, sums_refs = refs[:count], refs[count:2 * count]
@@ -387,10 +455,10 @@
 
 def finish_body(segments, modes, tokens, length, pairs, *refs):
     count = len(segments)
-    aloc_refs, gb_refs = refs[:count], refs[count:2 * count]
-    a_ref, r_ref, decay_ref, x2_ref, v_ref, partner_ref, both_ref = refs[2 * count:2 * count + 7]
-    got_refs = refs[2 * count + 7:2 * count + 6 + pairs]
-    gx2_ref, gv_ref, rgrad_ref, dgrad_ref, gin, nat, gx2_here, gv_here, sems = refs[-9:]
+    aloc_refs = refs[:count]
+    a_ref, r_ref, decay_ref, x2_ref, v_ref, partner_ref, both_ref = refs[count:count + 7]
+    got_refs = refs[count + 7:count + 6 + pairs]
+    gx2_ref, gv_ref, rgrad_ref, dgrad_ref, gin, nat, gx2_here, gv_here, r_here, d_here, sems = refs[-11:]
     channels = a_ref.shape[1]
     unroll = 4
     pair, core = place()
@@ -405,6 +473,32 @@
             state = state + weight * got_ref[pl.ds(0, modes), lanes]
         states.append(state)
     copies = []
+    owned = rgrad_ref.shape[1]
+    tiles = channels // LANES
+    lower = pl.ds(modes, 2 * modes // tiles)
+    sums = both_ref[lower, :]
+    for got_ref in got_refs:
+        sums = sums + got_ref[lower, :]
+    row = lax.broadcasted_iota(jnp.int32, (owned, LANES), 0)
+    column = lax.broadcasted_iota(jnp.int32, (owned, LANES), 1)
+    chosen = (column == pair * owned + row).astype(BF16)
+
+    def choose(values):
+        return sum(
+            lax.dot_general(part, chosen, CONTRACT_LAST, preferred_element_type=F32)
+            for part in three_parts(values)
+        )
+
+    if tiles == 1:
+        residue_sums, decay_sums = sums[:modes], sums[modes:]
+    else:
+        residue_sums, decay_sums = sums[:, :LANES], sums[:, LANES:]
+    r_here[...] = choose(residue_sums) / length
+    d_here[...] = choose(decay_sums) / length
+    for j, (here, there) in enumerate(((r_here, rgrad_ref), (d_here, dgrad_ref))):
+        copy = pltpu.make_async_copy(here, there, sems.at[count, j])
+        copy.start()
+        copies.append(copy)
     for seg in reversed(range(count)):
         start, rows = segments[seg]
         steps = rows // BLOCKS
@@ -417,7 +511,7 @@
             for b in reversed(range(BLOCKS)):
                 rowsb = pl.ds(b * modes, modes)
                 gin[rowsb, :] = state
-                state = power * state + gb_refs[seg][lane, rowsb, :]
+                state = power * state
             states[lane] = state
             edge = tuple(
                 spread(r_ref, m, lanes) * decays[m] * gin[pl.ds(m, BLOCKS, stride=modes), :]
@@ -444,28 +538,6 @@
             copy = pltpu.make_async_copy(here.at[window, :], there.at[window, :], sems.at[seg, j])
             copy.start()
             copies.append(copy)
-    owned = rgrad_ref.shape[0]
-    tiles = channels // LANES
-    lower = pl.ds(modes, 2 * modes // tiles)
-    sums = both_ref[lower, :]
-    for got_ref in got_refs:
-        sums = sums + got_ref[lower, :]
-    row = lax.broadcasted_iota(jnp.int32, (owned, LANES), 0)
-    column = lax.broadcasted_iota(jnp.int32, (owned, LANES), 1)
-    chosen = (column == pair * owned + row).astype(BF16)
-
-    def choose(values):
-        return sum(
-            lax.dot_general(chosen, part, CONTRACT_LAST, preferred_element_type=F32)
-            for part in three_parts(values)
-        )
-
-    if tiles == 1:
-        residue_sums, decay_sums = sums[:modes], sums[modes:]
-    else:
-        residue_sums, decay_sums = sums[:, :LANES], sums[:, LANES:]
-    rgrad_ref[...] = choose(residue_sums) / length
-    dgrad_ref[...] = choose(decay_sums) / length
     for copy in copies:
         copy.wait()
 
@@ -489,12 +561,11 @@
 
     rows_of = [(start, rows) for start, rows, _ in chunks]
     projected = project(
-        g_out, w_out,
-        [(*where, layout[:cut]) for where, layout in zip(rows_of, layouts)]
-        + [(*where, layout[cut:]) for where, layout in zip(rows_of, layouts)], channels)
+        g_out, w_out, [(*where, layout[:cut]) for where, layout in zip(rows_of, layouts)], channels)
     sent = [lax.ppermute(piece, "ch", xor_pairs(ch_size, order[0]))
             for piece, (_, _, order) in zip(projected, chunks)]
-    kept = projected[count:]
+    kept = project_kept(
+        g_out, w_out, [(*where, layout[cut:]) for where, layout in zip(rows_of, layouts)], channels)
 
     decay_t = decay.T
     residue_t = residue.T
@@ -511,7 +582,7 @@
                    jax.ShapeDtypeStruct((2 * modes, channels), F32)],
         scratch_shapes=[pltpu.VMEM((lane_tiles, tokens, LANES), F32)],
         compiler_params=params(),
-        cost_estimate=pl.CostEstimate(flops=work * 6, bytes_accessed=tokens * channels * 12, transcendentals=0),
+        cost_estimate=cost(3.7),
         name="forward",
     )(gate_x2, value_v, a, decay_t)
 
@@ -525,21 +596,12 @@
     )(total, partner, decay_t)
     got = [lax.ppermute(both, "ctx", xor_pairs(context_size, 2 * step)) for step in range(1, pairs)]
 
-    store_shape = jax.ShapeDtypeStruct((lane_tiles, modes, tokens, LANES), F32)
-    resp, store, hin, kin = pl.pallas_call(
-        functools.partial(respond_body, segments, modes, tokens),
-        out_shape=[perm_shape, store_shape, state_shape, state_shape],
-        scratch_shapes=[pltpu.VMEM((tokens, LANES), F32)],
-        compiler_params=params(),
-        cost_estimate=pl.CostEstimate(flops=work * 4, bytes_accessed=tokens * channels * 8, transcendentals=0),
-        name="respond",
-    )(hb, eb, xperm, a, r, decay_t, partner, *got)
-
-    alocs, gbs, sums = [], [], []
-    *sent, _ = lax.optimization_barrier((*sent, got))
+    uperms, gbs, sums = [], [], []
     arrived = [[piece] for piece in sent]
+    away = both
     for level in range(1, len(bits)):
         for which, (_, _, order) in enumerate(chunks):
+            arrived[which][-1], _ = lax.optimization_barrier((arrived[which][-1], away))
             stop = cut >> level
             width = kept[which].shape[1]
             left = width - 2 * stop * channels
@@ -547,31 +609,42 @@
             for piece in arrived[which]:
                 left = piece.shape[1] - 2 * stop * channels
                 away = away + piece[:, left:left + stop * channels].astype(F32)
-            arrived[which].append(
-                lax.ppermute(away.astype(BF16), "ch", xor_pairs(ch_size, order[level])))
+            away = away.astype(BF16)
+            hb, away = lax.optimization_barrier((hb, away))
+            arrived[which].append(lax.ppermute(away, "ch", xor_pairs(ch_size, order[level])))
+    store_shape = jax.ShapeDtypeStruct((lane_tiles, modes, tokens, LANES), F32)
+    resp, store, hin, kin = pl.pallas_call(
+        functools.partial(respond_body, segments, modes, tokens),
+        out_shape=[perm_shape, store_shape, state_shape, state_shape],
+        scratch_shapes=[pltpu.VMEM((tokens, LANES), F32)],
+        compiler_params=params(),
+        cost_estimate=cost(3.5),
+        name="respond",
+    )(hb, eb, xperm, a, r, decay_t, partner, *got)
+
     previous = []
     for seg, (start, rows) in enumerate(segments):
         block_shape = jax.ShapeDtypeStruct((lane_tiles, BLOCKS * modes, LANES), F32)
         pieces = arrived[seg]
-        *buffers, aloc, gb, partial_sums = pl.pallas_call(
+        *buffers, uperm, gb, partial_sums = pl.pallas_call(
             functools.partial(adjoint_body, (seg, start, rows), modes, len(pieces), len(previous)),
-            in_specs=in_vmem(1 + len(pieces)) + [pl.BlockSpec(memory_space=HBM)] * len(previous) + in_vmem(7),
+            in_specs=in_vmem(1 + len(pieces)) + [pl.BlockSpec(memory_space=HBM)] * len(previous) + in_vmem(6),
             out_specs=[pl.BlockSpec(memory_space=HBM)] * 3 + in_vmem(3),
             out_shape=[jax.ShapeDtypeStruct((tokens, channels), BF16)] * 3
             + [
                        jax.ShapeDtypeStruct((lane_tiles, rows, LANES), F32),
                        block_shape,
                        jax.ShapeDtypeStruct((2 * modes, channels), F32)],
-            scratch_shapes=[pltpu.VMEM((lane_tiles, rows, LANES), F32)] * 2
+            scratch_shapes=[pltpu.VMEM((lane_tiles, rows, LANES), F32)]
             + [pltpu.VMEM((BLOCKS * modes, LANES), F32)] * 2
             + [pltpu.VMEM((rows, channels), BF16), pltpu.SemaphoreType.DMA(())],
             input_output_aliases={1 + len(pieces) + j: j for j in range(len(previous))},
             compiler_params=params(),
-            cost_estimate=pl.CostEstimate(flops=rows * channels * modes * 8, bytes_accessed=rows * channels * 16, transcendentals=0),
+            cost_estimate=cost(2.7 * rows / 512),
             name="adjoint",
-        )(kept[seg], *pieces, *previous, gate_x1, resp, store, hin, kin, a, r)
+        )(kept[seg], *pieces, *previous, gate_x1, resp, store, hin, kin, a)
         previous = buffers
-        alocs.append(aloc)
+        uperms.append(uperm)
         gbs.append(gb)
         sums.append(partial_sums)
 
@@ -589,24 +662,38 @@
         name="backward_pair",
     )(message, partner, decay_t)
     got = [lax.ppermute(both, "ctx", xor_pairs(context_size, 2 * step)) for step in range(1, pairs)]
+    *uperms, _ = lax.optimization_barrier((*uperms, both))
+    alocs = [
+        pl.pallas_call(
+            functools.partial(local_body, segments, modes, seg),
+            out_shape=jax.ShapeDtypeStruct((lane_tiles, rows, LANES), F32),
+            scratch_shapes=[pltpu.VMEM((BLOCKS * modes, LANES), F32)],
+            compiler_params=params(),
+            cost_estimate=cost(1.8 * rows / 512),
+            name="local_adjoint",
+        )(uperms[seg], *gbs[seg:], a, r, decay_t)
+        for seg, (_, rows) in enumerate(segments)
+    ]
 
     grad_x2, grad_v, residue_grad, decay_grad = pl.pallas_call(
         functools.partial(finish_body, segments, modes, tokens, length, pairs),
-        in_specs=in_vmem(2 * count + 6 + pairs) + [pl.BlockSpec(memory_space=HBM)] * 2,
-        out_specs=[pl.BlockSpec(memory_space=HBM)] * 2 + in_vmem(2),
+        in_specs=in_vmem(count + 6 + pairs) + [pl.BlockSpec(memory_space=HBM)] * 2,
+        out_specs=[pl.BlockSpec(memory_space=HBM)] * 4,
         out_shape=[jax.ShapeDtypeStruct((tokens, channels), BF16)] * 2
-        + [jax.ShapeDtypeStruct((owned, modes), F32)] * 2,
+        + [jax.ShapeDtypeStruct((modes, owned), F32)] * 2,
         scratch_shapes=[pltpu.VMEM((BLOCKS * modes, LANES), F32),
                         pltpu.VMEM((lane_tiles, tokens, LANES), F32),
                         pltpu.VMEM((tokens, channels), BF16),
                         pltpu.VMEM((tokens, channels), BF16),
-                        pltpu.SemaphoreType.DMA((count, 2))],
-        input_output_aliases={2 * count + 6 + pairs: 0, 2 * count + 7 + pairs: 1},
+                        pltpu.VMEM((modes, owned), F32),
+                        pltpu.VMEM((modes, owned), F32),
+                        pltpu.SemaphoreType.DMA((count + 1, 2))],
+        input_output_aliases={count + 6 + pairs: 0, count + 7 + pairs: 1},
         compiler_params=params(),
-        cost_estimate=pl.CostEstimate(flops=work * 2, bytes_accessed=tokens * channels * 12, transcendentals=0),
+        cost_estimate=cost(3.4),
         name="finish",
-    )(*alocs, *gbs, a, r, decay_t, gate_x2, value_v, partner, both, *got, *previous[1:])
-    return previous[0], grad_x2, grad_v, residue_grad, decay_grad
+    )(*alocs, a, r, decay_t, gate_x2, value_v, partner, both, *got, *previous[1:])
+    return previous[0], grad_x2, grad_v, residue_grad.T, decay_grad.T
 
 
 def solution(mesh):

time: 55.5 us -> 49.5 us (0.89)
  waiting for transfers between devices: 10.4 us -> 3.86 us
  Pallas kernels: 25.9 us -> 28.7 us
  other arithmetic: 2.04 us -> 0.16 us
  local copies, waits for them, and re-layouts: 1.37 us -> 0.03 us
  starting transfers between devices: 14.7 us -> 15.7 us
    pallas_call x0 -> x3, Pallas kernels: none -> 6.78 us  [the longest x2 4.41 us: on_device(): pl.pallas_call(functools.partial(local_body, segments, modes, seg), out_s...]
    ppermute x6, waiting for transfers between devices: 6.37 us -> 0.26 us  [on_device(): lax.ppermute(both, 'ctx', xor_pairs(context_size, 2 * step))]
    pallas_call x1, Pallas kernels: 7.91 us -> 5.28 us  [project(): pl.pallas_call(functools.partial(project_body, work, width, pieces), in_s...]
    convert_element_type x2, other arithmetic: 2.03 us -> 0.14 us  [on_device(): away = away.astype(BF16)]
    ppermute x2, waiting for transfers between devices: 0.01 us -> 1.51 us  [on_device(): lax.ppermute(piece, 'ch', xor_pairs(ch_size, order[0]))]
    unnamed x16 -> x14, local copies, waits for them, and re-layouts: 1.37 us -> 0.03 us
    ppermute x1, waiting for transfers between devices: 1.19 us -> 0.01 us  [on_device(): partner = lax.ppermute(total, 'ctx', xor_pairs(context_size, 1))]
    pallas_call x2, Pallas kernels: 7.09 us -> 5.91 us  [on_device(): pl.pallas_call(functools.partial(adjoint_body, (seg, start, rows), modes,...]
  transfers between devices with their start and end apart: 12 -> 12, of which waited for: 7 -> 4; matrix products, arithmetic and copies ran while one was open for 2% -> 0% of each run, Pallas kernels for 20% -> 34%
where the time goes in v3:
time: 49.5 us; the launch traced here: 49.3 us
  Pallas kernels  28.7 us (58%)
  starting transfers between devices  15.7 us (32%)
  waiting for transfers between devices  3.86 us (8%)
  between operations  0.86 us (2%)
    ppermute x6, starting transfers between devices, on_device(): lax.ppermute(both, 'ctx', xor_pairs(context_size, 2 * step))  8.9 us
    pallas_call x2, Pallas kernels, on_device(): pl.pallas_call(functools.partial(adjoint_body, (seg, start, rows), modes,...  5.91 us
    pallas_call x1, Pallas kernels, project(): pl.pallas_call(functools.partial(project_body, work, width, pieces), in_s...  5.28 us
    ppermute x2, starting transfers between devices, on_device(): lax.ppermute(piece, 'ch', xor_pairs(ch_size, order[0]))  4.52 us
    pallas_call x2, Pallas kernels, on_device(): pl.pallas_call(functools.partial(local_body, segments, modes, seg), out_s...  4.41 us
    pallas_call x1, Pallas kernels, on_device(): pl.pallas_call(functools.partial(respond_body, segments, modes, tokens),...  3.58 us
    pallas_call x1, Pallas kernels, on_device(): pl.pallas_call(functools.partial(forward_body, segments, modes), out_shap...  3.55 us
    pallas_call x1, Pallas kernels, on_device(): pl.pallas_call(functools.partial(finish_body, segments, modes, tokens, le...  3.39 us
  transfers between devices with their start and end apart: 12, of which 4 were waited for; matrix products, arithmetic and copies ran while one was open for 0% of the time, Pallas kernels for 34%

profile of v3, /device:TPU:0, one launch (start us, length us, event | category | flops | bytes accessed | tf_op | source)
XLA Modules:
  0.0 49.3 jit_solution(15048677276754043473)
XLA Ops:
  0.6 0.0 copy-start.1
  0.6 0.0 copy-start.6
  0.7 0.0 copy-start.5
  0.7 0.0 copy-start.4
  0.7 5.3 %project.1 = (bf16[512,512]{1,0:T(8,128)(2,1)}, bf16[512,512]{1,0:T(8,128)(2,1)}) custom-call(bf16[1024,2048]{1,0:T(8,128)(2,1)} %g_ref.3, bf16[1024,2048]{1,0:T(8,128)(2,1)} %w_ref.3), custom_call_target="tpu_custom_call" | custom-call | flops 5500000256 | tf_op jit(solution)/shard_map/project/pallas_call | solution.py:129
  6.0 3.0 %collective-permute-start = (bf16[512,512]{1,0:T(8,128)(2,1)}, bf16[512,512]{1,0:T(8,128)(2,1)S(1)}, u32[]{:S(2)}, u32[]{:S(2)}) collective-permute-start(bf16[512,512]{1,0:T(8,128)(2,1)} %get-tuple-element.42), channel_id=1, source_target_pairs={{0,2},{1,3},{2,0},{3,1},{4,6},{5,7},{6,4},{7,5},{8,10},{9,11},{10,... | collective-permute-start | bytes 1572872 | tf_op jit(solution)/shard_map/ppermute | solution.py:565
  9.0 1.5 %collective-permute-start.1 = (bf16[512,512]{1,0:T(8,128)(2,1)}, bf16[512,512]{1,0:T(8,128)(2,1)S(1)}, u32[]{:S(2)}, u32[]{:S(2)}) collective-permute-start(bf16[512,512]{1,0:T(8,128)(2,1)} %get-tuple-element.45), channel_id=1, source_target_pairs={{0,1},{1,0},{2,3},{3,2},{4,5},{5,4},{6,7},{7,6},{8,9},{9,8},{10,11... | collective-permute-start | bytes 1572872 | tf_op jit(solution)/shard_map/ppermute | solution.py:565
  10.5 0.0 copy-done.1
  10.5 0.0 copy-done.6
  10.5 0.0 copy-done.5
  10.5 0.0 copy-done.4
  10.5 0.0 copy-start.2
  10.5 0.0 copy-start.3
  10.5 3.5 %forward.1 = (f32[2,1024,128]{2,1,0:T(8,128)S(1)}, f32[2,2,128,128]{3,2,1,0:T(8,128)S(1)}, f32[2,2,128,128]{3,2,1,0:T(8,128)S(1)}, f32[32,256]{1,0:T(8,128)S(1)}) custom-call(bf16[1024,256]{1,0:T(8,128)(2,1)S(1)} %copy-done.4, bf16[1024,256]{1,0:T(8,128)(2,1)S(1)} %copy-done.5, f32[16,256]{1,0:T(8,128)S(1)} %get-tuple-element.78.a_ref.refs_7_.refs_10_.refs_2_.refs_1_, ...), custom_call_target="tpu_custom_call" | custom-call | flops 4070000128 | tf_op jit(solution)/shard_map/forward/pallas_call | solution.py:579
  14.1 0.1 collective-permute-start.2
  14.2 0.0 copy-done.2
  14.2 0.0 copy-done.3
  14.2 2.4 %project_kept.1 = (bf16[512,512]{1,0:T(8,128)(2,1)S(1)}, bf16[512,512]{1,0:T(8,128)(2,1)S(1)}) custom-call(bf16[1024,2048]{1,0:T(8,128)(2,1)S(1)} %copy-done.2, bf16[1024,2048]{1,0:T(8,128)(2,1)S(1)} %copy-done.3), custom_call_target="tpu_custom_call" | custom-call | flops 3300000000 | tf_op jit(solution)/shard_map/project_kept/pallas_call | solution.py:157
  16.6 0.0 collective-permute-done.2.partner_ref
  16.6 3.7 %collective-permute-start.7 = (f32[32,256]{1,0:T(8,128)S(1)}, f32[32,256]{1,0:T(8,128)S(1)}, u32[]{:S(2)}, u32[]{:S(2)}) collective-permute-start(f32[32,256]{1,0:T(8,128)S(1)} %forward_pair.1), channel_id=1, source_target_pairs={{0,24},{4,28},{8,16},{12,20},{16,8},{20,12},{24,0},{28,4},{1,25},{... | collective-permute-start | bytes 98312 | tf_op jit(solution)/shard_map/ppermute | solution.py:597
  20.3 0.0 collective-permute-start.6
  20.3 0.8 %collective-permute-start.5 = (f32[32,256]{1,0:T(8,128)S(1)}, f32[32,256]{1,0:T(8,128)S(1)}, u32[]{:S(2)}, u32[]{:S(2)}) collective-permute-start(f32[32,256]{1,0:T(8,128)S(1)} %forward_pair.1), channel_id=1, source_target_pairs={{0,8},{4,12},{8,0},{12,4},{16,24},{20,28},{24,16},{28,20},{1,9},{5... | collective-permute-start | bytes 98312 | tf_op jit(solution)/shard_map/ppermute | solution.py:597
  21.1 1.5 %collective-permute-done.1.refs_0_ = bf16[512,512]{1,0:T(8,128)(2,1)S(1)} collective-permute-done((bf16[512,512]{1,0:T(8,128)(2,1)}, bf16[512,512]{1,0:T(8,128)(2,1)S(1)}, u32[]{:S(2)}, u32[]{:S(2)}) %collective-permute-start.1) | collective-permute-done | bytes 524320 | tf_op jit(solution)/shard_map/ppermute | solution.py:565
  22.6 0.1 add_convert_fusion.1
  22.7 0.4 collective-permute-start.4
  23.1 0.0 collective-permute-done.refs_0_
  23.1 0.1 add_convert_fusion
  23.2 1.7 %collective-permute-start.3 = (bf16[512,256]{1,0:T(8,128)(2,1)S(1)}, bf16[512,256]{1,0:T(8,128)(2,1)S(1)}, u32[]{:S(2)}, u32[]{:S(2)}) collective-permute-start(bf16[512,256]{1,0:T(8,128)(2,1)S(1)} %add_convert_fusion), channel_id=1, source_target_pairs={{0,1},{1,0},{2,3},{3,2},{4,5},{5,4},{6,7},{7,6},{8,9},{9,8},{10,11... | collective-permute-start | bytes 786440 | tf_op jit(solution)/shard_map/ppermute | solution.py:614
  24.9 0.0 collective-permute-done.7.refs_2_
  24.9 0.2 collective-permute-done.6.refs_1_
  25.1 0.0 collective-permute-done.5.refs_0_
  25.1 0.0 copy-start
  25.1 3.6 %respond.1 = (f32[2,1024,128]{2,1,0:T(8,128)S(1)}, f32[2,16,1024,128]{3,2,1,0:T(8,128)S(1)}, f32[2,2,128,128]{3,2,1,0:T(8,128)S(1)}, f32[2,2,128,128]{3,2,1,0:T(8,128)S(1)}) custom-call(f32[2,2,128,128]{3,2,1,0:T(8,128)S(1)} %get-tuple-element.52.hb_ref, f32[2,2,128,128]{3,2,1,0:T(8,128)S(1)} %get-tuple-element.53.eb_ref, ...), custom_call_target="tpu_custom_call" | custom-call | flops 3849999872 | tf_op jit(solution)/shard_map/respond/pallas_call | solution.py:616
  28.7 0.9 %collective-permute-done.4.refs_1_ = bf16[512,256]{1,0:T(8,128)(2,1)S(1)} collective-permute-done((bf16[512,256]{1,0:T(8,128)(2,1)S(1)}, bf16[512,256]{1,0:T(8,128)(2,1)S(1)}, u32[]{:S(2)}, u32[]{:S(2)}) %collective-permute-start.4) | collective-permute-done | bytes 262176 | tf_op jit(solution)/shard_map/ppermute | solution.py:614
  29.6 0.0 copy-done
  29.6 2.9 %adjoint.2 = (bf16[1024,256]{1,0:T(8,128)(2,1)}, bf16[1024,256]{1,0:T(8,128)(2,1)}, bf16[1024,256]{1,0:T(8,128)(2,1)}, f32[2,512,128]{2,1,0:T(8,128)S(1)}, f32[2...) custom-call(bf16[512,512]{1,0:T(8,128)(2,1)S(1)} %get-tuple-element.44.kept_ref, ...), custom_call_target="tpu_custom_call" | custom-call | flops 2969999872 | tf_op jit(solution)/shard_map/adjoint/pallas_call | solution.py:629
  32.5 0.0 collective-permute-done.3.refs_1_
  32.6 3.0 %adjoint.3 = (bf16[1024,256]{1,0:T(8,128)(2,1)}, bf16[1024,256]{1,0:T(8,128)(2,1)}, bf16[1024,256]{1,0:T(8,128)(2,1)}, f32[2,512,128]{2,1,0:T(8,128)S(1)}, f32[2...) custom-call(bf16[512,512]{1,0:T(8,128)(2,1)S(1)} %get-tuple-element.41.ke, ...), custom_call_target="tpu_custom_call", output_to_operand_aliasing={{0}: (3, {}), {1}: (4, {}), {2}: (5, {})} | custom-call | flops 2969999872 | tf_op jit(solution)/shard_map/adjoint/pallas_call | solution.py:629
  35.5 0.1 totals.1.message_ref
  35.6 0.1 collective-permute-start.8
  35.7 1.2 %collective-permute-done.8.partner_ref.refs_7_ = f32[48,256]{1,0:T(8,128)S(1)} collective-permute-done((f32[48,256]{1,0:T(8,128)S(1)}, f32[48,256]{1,0:T(8,128)S(1)}, u32[]{:S(2)}, u32[]{:S(2)}) %collective-permute-start.8) | collective-permute-done | bytes 49184 | tf_op jit(solution)/shard_map/ppermute | solution.py:657
  36.9 0.2 backward_pair.1.refs_8_
  37.0 3.7 %collective-permute-start.11 = (f32[32,256]{1,0:T(8,128)S(1)}, f32[32,256]{1,0:T(8,128)S(1)}, u32[]{:S(2)}, u32[]{:S(2)}) collective-permute-start(f32[32,256]{1,0:T(8,128)S(1)} %backward_pair.1.refs_8_), channel_id=1, source_target_pairs={{0,24},{4,28},{8,16},{12,20},{16,8},{20,12},{24,0},{28,4},{1,25},{... | collective-permute-start | bytes 98312 | tf_op jit(solution)/shard_map/ppermute | solution.py:664
  40.7 0.0 collective-permute-start.10
  40.7 0.8 %collective-permute-start.9 = (f32[32,256]{1,0:T(8,128)S(1)}, f32[32,256]{1,0:T(8,128)S(1)}, u32[]{:S(2)}, u32[]{:S(2)}) collective-permute-start(f32[32,256]{1,0:T(8,128)S(1)} %backward_pair.1.refs_8_), channel_id=1, source_target_pairs={{0,8},{4,12},{8,0},{12,4},{16,24},{20,28},{24,16},{28,20},{1,9},{5... | collective-permute-start | bytes 98312 | tf_op jit(solution)/shard_map/ppermute | solution.py:664
  41.5 2.2 %local_adjoint.2.refs_0_ = f32[2,512,128]{2,1,0:T(8,128)S(1)} custom-call(f32[2,512,128]{2,1,0:T(8,128)S(1)} %get-tuple-element.69.uperm_ref, f32[2,128,128]{2,1,0:T(8,128)S(1)} %get-tuple-element.65.refs_0_, f32[2,128,128]{2,1,0:T(8,128)S(1)} %get-tuple-element.66.refs_1_.refs_0_, f32[16,256]{1,0:T(8,128)S(1)} %get-tuple-element.78.a_ref.refs_7_.refs_10_.refs_2_.refs_1_, ...), custom_call_target="tpu_custom_call" | custom-call | flops 1980000000 | tf_op jit(solution)/shard_map/local_adjoint/pallas_call | solution.py:667
  43.7 2.2 %local_adjoint.3.refs_1_ = f32[2,512,128]{2,1,0:T(8,128)S(1)} custom-call(f32[2,512,128]{2,1,0:T(8,128)S(1)} %get-tuple-element.70.uperm_ref, f32[2,128,128]{2,1,0:T(8,128)S(1)} %get-tuple-element.66.refs_1_.refs_0_, f32[16,256]{1,0:T(8,128)S(1)} %get-tuple-element.78.a_ref.refs_7_.refs_10_.refs_2_.refs_1_, ...), custom_call_target="tpu_custom_call" | custom-call | flops 1980000000 | tf_op jit(solution)/shard_map/local_adjoint/pallas_call | solution.py:667
  45.9 0.0 collective-permute-done.11.refs_11_
  45.9 0.0 collective-permute-done.10.refs_10_
  45.9 0.0 collective-permute-done.9.refs_9_
  45.9 3.4 %finish.1 = (bf16[1024,256]{1,0:T(8,128)(2,1)}, bf16[1024,256]{1,0:T(8,128)(2,1)}, f32[16,32]{1,0:T(8,128)}, f32[16,32]{1,0:T(8,128)}) custom-call(f32[2,512,128]{2,1,0:T(8,128)S(1)} %local_adjoint.2.refs_0_, f32[2,512,128]{2,1,0:T(8,128)S(1)} %local_adjoint.3.refs_1_, ...), custom_call_target="tpu_custom_call", output_to_operand_aliasing={{0}: (12, {}), {1}: (13, {})} | custom-call | flops 3740000000 | tf_op jit(solution)/shard_map/finish/pallas_call | solution.py:678
  (3 shorter events, 0.0 us)
Async XLA Ops:
  0.6 9.9 %copy-start.1 = (f32[256,16]{0,1:T(8,128)S(1)}, f32[256,16]{0,1:T(8,128)}, u32[]{:S(2)}) copy-start(f32[256,16]{0,1:T(8,128)} %param.13) | copy-start | bytes 49156
  0.6 9.8 %copy-start.6 = (f32[256,16]{0,1:T(8,128)S(1)}, f32[256,16]{0,1:T(8,128)}, u32[]{:S(2)}) copy-start(f32[256,16]{0,1:T(8,128)} %param.12) | copy-start | bytes 49156
  0.7 9.8 %copy-start.5 = (bf16[1024,256]{1,0:T(8,128)(2,1)S(1)}, bf16[1024,256]{1,0:T(8,128)(2,1)}, u32[]{:S(2)}) copy-start(bf16[1024,256]{1,0:T(8,128)(2,1)} %refs_6_.1) | copy-start | bytes 1572868
  0.7 9.8 %copy-start.4 = (bf16[1024,256]{1,0:T(8,128)(2,1)S(1)}, bf16[1024,256]{1,0:T(8,128)(2,1)}, u32[]{:S(2)}) copy-start(bf16[1024,256]{1,0:T(8,128)(2,1)} %refs_5_.3) | copy-start | bytes 1572868
  6.0 17.1 %collective-permute-start = (bf16[512,512]{1,0:T(8,128)(2,1)}, bf16[512,512]{1,0:T(8,128)(2,1)S(1)}, u32[]{:S(2)}, u32[]{:S(2)}) collective-permute-start(bf16[512,512]{1,0:T(8,128)(2,1)} %get-tuple-element.42), channel_id=1, source_target_pairs={{0,2},{1,3},{2,0},{3,1},{4,6},{5,7},{6,4},{7,5},{8,10},{9,11},{10,... | collective-permute-start | bytes 1572872 | tf_op jit(solution)/shard_map/ppermute | solution.py:565
  9.0 13.6 %collective-permute-start.1 = (bf16[512,512]{1,0:T(8,128)(2,1)}, bf16[512,512]{1,0:T(8,128)(2,1)S(1)}, u32[]{:S(2)}, u32[]{:S(2)}) collective-permute-start(bf16[512,512]{1,0:T(8,128)(2,1)} %get-tuple-element.45), channel_id=1, source_target_pairs={{0,1},{1,0},{2,3},{3,2},{4,5},{5,4},{6,7},{7,6},{8,9},{9,8},{10,11... | collective-permute-start | bytes 1572872 | tf_op jit(solution)/shard_map/ppermute | solution.py:565
  10.5 3.7 %copy-start.2 = (bf16[1024,2048]{1,0:T(8,128)(2,1)S(1)}, bf16[1024,2048]{1,0:T(8,128)(2,1)}, u32[]{:S(2)}) copy-start(bf16[1024,2048]{1,0:T(8,128)(2,1)} %g_ref.3) | copy-start | bytes 12582916
  10.5 3.7 %copy-start.3 = (bf16[1024,2048]{1,0:T(8,128)(2,1)S(1)}, bf16[1024,2048]{1,0:T(8,128)(2,1)}, u32[]{:S(2)}) copy-start(bf16[1024,2048]{1,0:T(8,128)(2,1)} %w_ref.3) | copy-start | bytes 12582916
  14.1 2.5 %collective-permute-start.2 = (f32[32,256]{1,0:T(8,128)S(1)}, f32[32,256]{1,0:T(8,128)S(1)}, u32[]{:S(2)}, u32[]{:S(2)}) collective-permute-start(f32[32,256]{1,0:T(8,128)S(1)} %get-tuple-element.46.total_ref), channel_id=1, source_target_pairs={{0,4},{4,0},{8,12},{12,8},{16,20},{20,16},{24,28},{28,24},{1,5},{5... | collective-permute-start | bytes 98312 | tf_op jit(solution)/shard_map/ppermute | solution.py:590
  16.6 8.2 %collective-permute-start.7 = (f32[32,256]{1,0:T(8,128)S(1)}, f32[32,256]{1,0:T(8,128)S(1)}, u32[]{:S(2)}, u32[]{:S(2)}) collective-permute-start(f32[32,256]{1,0:T(8,128)S(1)} %forward_pair.1), channel_id=1, source_target_pairs={{0,24},{4,28},{8,16},{12,20},{16,8},{20,12},{24,0},{28,4},{1,25},{... | collective-permute-start | bytes 98312 | tf_op jit(solution)/shard_map/ppermute | solution.py:597
  20.3 4.8 %collective-permute-start.6 = (f32[32,256]{1,0:T(8,128)S(1)}, f32[32,256]{1,0:T(8,128)S(1)}, u32[]{:S(2)}, u32[]{:S(2)}) collective-permute-start(f32[32,256]{1,0:T(8,128)S(1)} %forward_pair.1), channel_id=1, source_target_pairs={{0,16},{4,20},{8,24},{12,28},{16,0},{20,4},{24,8},{28,12},{1,17},{... | collective-permute-start | bytes 98312 | tf_op jit(solution)/shard_map/ppermute | solution.py:597
  20.3 4.8 %collective-permute-start.5 = (f32[32,256]{1,0:T(8,128)S(1)}, f32[32,256]{1,0:T(8,128)S(1)}, u32[]{:S(2)}, u32[]{:S(2)}) collective-permute-start(f32[32,256]{1,0:T(8,128)S(1)} %forward_pair.1), channel_id=1, source_target_pairs={{0,8},{4,12},{8,0},{12,4},{16,24},{20,28},{24,16},{28,20},{1,9},{5... | collective-permute-start | bytes 98312 | tf_op jit(solution)/shard_map/ppermute | solution.py:597
  22.7 6.9 %collective-permute-start.4 = (bf16[512,256]{1,0:T(8,128)(2,1)S(1)}, bf16[512,256]{1,0:T(8,128)(2,1)S(1)}, u32[]{:S(2)}, u32[]{:S(2)}) collective-permute-start(bf16[512,256]{1,0:T(8,128)(2,1)S(1)} %add_convert_fusion.1), channel_id=1, source_target_pairs={{0,2},{1,3},{2,0},{3,1},{4,6},{5,7},{6,4},{7,5},{8,10},{9,11},{10,... | collective-permute-start | bytes 786440 | tf_op jit(solution)/shard_map/ppermute | solution.py:614
  23.2 9.4 %collective-permute-start.3 = (bf16[512,256]{1,0:T(8,128)(2,1)S(1)}, bf16[512,256]{1,0:T(8,128)(2,1)S(1)}, u32[]{:S(2)}, u32[]{:S(2)}) collective-permute-start(bf16[512,256]{1,0:T(8,128)(2,1)S(1)} %add_convert_fusion), channel_id=1, source_target_pairs={{0,1},{1,0},{2,3},{3,2},{4,5},{5,4},{6,7},{7,6},{8,9},{9,8},{10,11... | collective-permute-start | bytes 786440 | tf_op jit(solution)/shard_map/ppermute | solution.py:614
  25.1 4.5 %copy-start = (bf16[1024,256]{1,0:T(8,128)(2,1)S(1)}, bf16[1024,256]{1,0:T(8,128)(2,1)}, u32[]{:S(2)}) copy-start(bf16[1024,256]{1,0:T(8,128)(2,1)} %refs_5_.2) | copy-start | bytes 1572868
  35.6 1.3 %collective-permute-start.8 = (f32[48,256]{1,0:T(8,128)S(1)}, f32[48,256]{1,0:T(8,128)S(1)}, u32[]{:S(2)}, u32[]{:S(2)}) collective-permute-start(f32[48,256]{1,0:T(8,128)S(1)} %totals.1.message_ref), channel_id=1, source_target_pairs={{0,4},{4,0},{8,12},{12,8},{16,20},{20,16},{24,28},{28,24},{1,5},{5... | collective-permute-start | bytes 147464 | tf_op jit(solution)/shard_map/ppermute | solution.py:657
  37.0 8.9 %collective-permute-start.11 = (f32[32,256]{1,0:T(8,128)S(1)}, f32[32,256]{1,0:T(8,128)S(1)}, u32[]{:S(2)}, u32[]{:S(2)}) collective-permute-start(f32[32,256]{1,0:T(8,128)S(1)} %backward_pair.1.refs_8_), channel_id=1, source_target_pairs={{0,24},{4,28},{8,16},{12,20},{16,8},{20,12},{24,0},{28,4},{1,25},{... | collective-permute-start | bytes 98312 | tf_op jit(solution)/shard_map/ppermute | solution.py:664
  40.7 5.2 %collective-permute-start.10 = (f32[32,256]{1,0:T(8,128)S(1)}, f32[32,256]{1,0:T(8,128)S(1)}, u32[]{:S(2)}, u32[]{:S(2)}) collective-permute-start(f32[32,256]{1,0:T(8,128)S(1)} %backward_pair.1.refs_8_), channel_id=1, source_target_pairs={{0,16},{4,20},{8,24},{12,28},{16,0},{20,4},{24,8},{28,12},{1,17},{... | collective-permute-start | bytes 98312 | tf_op jit(solution)/shard_map/ppermute | solution.py:664
  40.7 5.2 %collective-permute-start.9 = (f32[32,256]{1,0:T(8,128)S(1)}, f32[32,256]{1,0:T(8,128)S(1)}, u32[]{:S(2)}, u32[]{:S(2)}) collective-permute-start(f32[32,256]{1,0:T(8,128)S(1)} %backward_pair.1.refs_8_), channel_id=1, source_target_pairs={{0,8},{4,12},{8,0},{12,4},{16,24},{20,28},{24,16},{28,20},{1,9},{5... | collective-permute-start | bytes 98312 | tf_op jit(solution)/shard_map/ppermute | solution.py:664

commit v4 on v3

--- a/solution.py
+++ b/solution.py
@@ -166,6 +166,13 @@
     )(g_out, w_out)
 
 
+def tree_sum(terms):
+    terms = list(terms)
+    while len(terms) > 1:
+        terms = [sum(terms[i:i + 2][1:], terms[i]) for i in range(0, len(terms), 2)]
+    return terms[0]
+
+
 def spread(ref, row, lanes):
     return jnp.broadcast_to(ref[pl.ds(row, 1), lanes], (BLOCKS, LANES))
 
@@ -173,7 +180,7 @@
 def forward_body(segments, modes, x2_ref, v_ref, a_ref, decay_ref,
                  xperm_ref, hb_ref, eb_ref, total_ref, nat):
     channels = x2_ref.shape[1]
-    unroll = 4
+    unroll = 16
     group = modes // FPARTS
     for lane in range(channels // LANES):
         lanes = pl.ds(lane * LANES, LANES)
@@ -242,7 +249,7 @@
     half = modes // 2
     pair, core = place()
     channels = a_ref.shape[1]
-    unroll = 4
+    unroll = 16
     for lane in range(channels // LANES):
         lanes = pl.ds(lane * LANES, LANES)
         a = a_ref[:, lanes]
@@ -276,12 +283,10 @@
                         i = outer * unroll + q
                         here = pl.ds(pl.multiple_of(start + i * BLOCKS, BLOCKS), BLOCKS)
                         x = xperm_ref[lane, here, :]
-                        y = None
                         for m in range(half):
                             h[m] = decays[m] * h[m] + x
                             store_ref[lane, part * half + m, here, :] = h[m]
-                            term = weights[m] * h[m]
-                            y = term if y is None else y + term
+                        y = tree_sum(weights[m] * h[m] for m in range(half))
                         if part == 0:
                             yloc[here, :] = y
                         else:
@@ -303,7 +308,7 @@
     uperm, gb_ref, sums_ref, nat, rb, qb, grad_here, sem = refs[-8:]
     steps = rows // BLOCKS
     channels = x1_ref.shape[1]
-    unroll = 4
+    unroll = 16
     half = modes // 2
     window = pl.ds(start, rows)
     for lane in range(channels // LANES):
@@ -367,7 +372,7 @@
     gb_refs = refs[:count - seg]
     a_ref, r_ref, decay_ref, aloc_ref, gin = refs[count - seg:]
     channels = a_ref.shape[1]
-    unroll = 4
+    unroll = 16
     half = modes // 2
     for lane in range(channels // LANES):
         lanes = pl.ds(lane * LANES, LANES)
@@ -390,11 +395,11 @@
                     i = steps - 1 - (outer * unroll + q)
                     here = pl.ds(pl.multiple_of(i * BLOCKS, BLOCKS), BLOCKS)
                     u = uperm_ref[lane, here, :]
-                    y = None if part == 0 else aloc_ref[lane, here, :]
                     for m in range(half):
                         g[m] = decays[m] * g[m] + u
-                        term = weights[m] * g[m]
-                        y = term if y is None else y + term
+                    y = tree_sum(weights[m] * g[m] for m in range(half))
+                    if part == 1:
+                        y = y + aloc_ref[lane, here, :]
                     aloc_ref[lane, here, :] = y
                 return tuple(g)
 
@@ -460,7 +465,7 @@
     got_refs = refs[count + 7:count + 6 + pairs]
     gx2_ref, gv_ref, rgrad_ref, dgrad_ref, gin, nat, gx2_here, gv_here, r_here, d_here, sems = refs[-11:]
     channels = a_ref.shape[1]
-    unroll = 4
+    unroll = 16
     pair, core = place()
     states = []
     for lane in range(channels // LANES):
@@ -523,9 +528,8 @@
                 for q in range(unroll):
                     i = steps - 1 - (outer * unroll + q)
                     here = pl.ds(pl.multiple_of(i * BLOCKS, BLOCKS), BLOCKS)
-                    y = aloc_refs[seg][lane, here, :]
+                    y = tree_sum(edge) + aloc_refs[seg][lane, here, :]
                     for m in range(modes):
-                        y = y + edge[m]
                         edge[m] = edge[m] * decays[m]
                     nat[lane, pl.ds(start + i, BLOCKS, stride=steps), :] = y
                 return tuple(edge)

time: 49.5 us -> 47.7 us (0.964)
  Pallas kernels: 28.7 us -> 24.6 us
  waiting for transfers between devices: 3.86 us -> 5.87 us
    pallas_call x2, Pallas kernels: 4.41 us -> 2.63 us  [on_device(): pl.pallas_call(functools.partial(local_body, segments, modes, seg), out_s...]
    ppermute x6, waiting for transfers between devices: 0.26 us -> 1.42 us  [on_device(): lax.ppermute(both, 'ctx', xor_pairs(context_size, 2 * step))]
    pallas_call x2, Pallas kernels: 5.91 us -> 4.91 us  [on_device(): pl.pallas_call(functools.partial(adjoint_body, (seg, start, rows), modes,...]
    ppermute x2, waiting for transfers between devices: 0.87 us -> 1.52 us  [on_device(): lax.ppermute(away, 'ch', xor_pairs(ch_size, order[level]))]
    pallas_call x1, Pallas kernels: 3.55 us -> 3.03 us  [on_device(): pl.pallas_call(functools.partial(forward_body, segments, modes), out_shap...]
  transfers between devices with their start and end apart: 12 -> 12, of which waited for: 4 -> 4; matrix products, arithmetic and copies ran while one was open for 0% -> 0% of each run, Pallas kernels for 34% -> 29%
where the time goes in v4:
time: 47.7 us; the launch traced here: 47.5 us
  Pallas kernels  24.6 us (52%)
  starting transfers between devices  15.7 us (33%)
  waiting for transfers between devices  5.87 us (12%)
  between operations  0.84 us (2%)
    ppermute x6, starting transfers between devices, on_device(): lax.ppermute(both, 'ctx', xor_pairs(context_size, 2 * step))  8.91 us
    pallas_call x1, Pallas kernels, project(): pl.pallas_call(functools.partial(project_body, work, width, pieces), in_s...  5.28 us
    pallas_call x2, Pallas kernels, on_device(): pl.pallas_call(functools.partial(adjoint_body, (seg, start, rows), modes,...  4.91 us
    ppermute x2, starting transfers between devices, on_device(): lax.ppermute(piece, 'ch', xor_pairs(ch_size, order[0]))  4.52 us
    pallas_call x1, Pallas kernels, on_device(): pl.pallas_call(functools.partial(respond_body, segments, modes, tokens),...  3.15 us
    pallas_call x1, Pallas kernels, on_device(): pl.pallas_call(functools.partial(forward_body, segments, modes), out_shap...  3.03 us
    pallas_call x1, Pallas kernels, on_device(): pl.pallas_call(functools.partial(finish_body, segments, modes, tokens, le...  3.01 us
    pallas_call x2, Pallas kernels, on_device(): pl.pallas_call(functools.partial(local_body, segments, modes, seg), out_s...  2.63 us
  transfers between devices with their start and end apart: 12, of which 4 were waited for; matrix products, arithmetic and copies ran while one was open for 0% of the time, Pallas kernels for 29%

profile of v4, /device:TPU:0, one launch (start us, length us, event | category | flops | bytes accessed | tf_op | source)
XLA Modules:
  0.0 47.5 jit_solution(3394518282289363984)
XLA Ops:
  0.6 0.0 copy-start.1
  0.6 0.0 copy-start.6
  0.7 0.0 copy-start.5
  0.7 0.0 copy-start.4
  0.7 5.3 %project.1 = (bf16[512,512]{1,0:T(8,128)(2,1)}, bf16[512,512]{1,0:T(8,128)(2,1)}) custom-call(bf16[1024,2048]{1,0:T(8,128)(2,1)} %g_ref.3, bf16[1024,2048]{1,0:T(8,128)(2,1)} %w_ref.3), custom_call_target="tpu_custom_call" | custom-call | flops 5500000256 | tf_op jit(solution)/shard_map/project/pallas_call | solution.py:129
  6.0 3.0 %collective-permute-start = (bf16[512,512]{1,0:T(8,128)(2,1)}, bf16[512,512]{1,0:T(8,128)(2,1)S(1)}, u32[]{:S(2)}, u32[]{:S(2)}) collective-permute-start(bf16[512,512]{1,0:T(8,128)(2,1)} %get-tuple-element.42), channel_id=1, source_target_pairs={{0,2},{1,3},{2,0},{3,1},{4,6},{5,7},{6,4},{7,5},{8,10},{9,11},{10,... | collective-permute-start | bytes 1572872 | tf_op jit(solution)/shard_map/ppermute | solution.py:569
  9.0 1.5 %collective-permute-start.1 = (bf16[512,512]{1,0:T(8,128)(2,1)}, bf16[512,512]{1,0:T(8,128)(2,1)S(1)}, u32[]{:S(2)}, u32[]{:S(2)}) collective-permute-start(bf16[512,512]{1,0:T(8,128)(2,1)} %get-tuple-element.45), channel_id=1, source_target_pairs={{0,1},{1,0},{2,3},{3,2},{4,5},{5,4},{6,7},{7,6},{8,9},{9,8},{10,11... | collective-permute-start | bytes 1572872 | tf_op jit(solution)/shard_map/ppermute | solution.py:569
  10.5 0.0 copy-done.1
  10.5 0.0 copy-done.6
  10.5 0.0 copy-done.5
  10.5 0.0 copy-done.4
  10.5 0.0 copy-start.2
  10.5 0.0 copy-start.3
  10.5 3.0 %forward.1 = (f32[2,1024,128]{2,1,0:T(8,128)S(1)}, f32[2,2,128,128]{3,2,1,0:T(8,128)S(1)}, f32[2,2,128,128]{3,2,1,0:T(8,128)S(1)}, f32[32,256]{1,0:T(8,128)S(1)}) custom-call(bf16[1024,256]{1,0:T(8,128)(2,1)S(1)} %copy-done.4, bf16[1024,256]{1,0:T(8,128)(2,1)S(1)} %copy-done.5, f32[16,256]{1,0:T(8,128)S(1)} %get-tuple-element.78.a_ref.refs_7_.refs_10_.refs_2_.refs_1_, ...), custom_call_target="tpu_custom_call" | custom-call | flops 4070000128 | tf_op jit(solution)/shard_map/forward/pallas_call | solution.py:583
  13.6 0.1 collective-permute-start.2
  13.7 0.0 copy-done.2
  13.7 0.3 copy-done.3
  14.0 2.4 %project_kept.1 = (bf16[512,512]{1,0:T(8,128)(2,1)S(1)}, bf16[512,512]{1,0:T(8,128)(2,1)S(1)}) custom-call(bf16[1024,2048]{1,0:T(8,128)(2,1)S(1)} %copy-done.2, bf16[1024,2048]{1,0:T(8,128)(2,1)S(1)} %copy-done.3), custom_call_target="tpu_custom_call" | custom-call | flops 3300000000 | tf_op jit(solution)/shard_map/project_kept/pallas_call | solution.py:157
  16.4 0.0 collective-permute-done.2.partner_ref
  16.4 3.7 %collective-permute-start.7 = (f32[32,256]{1,0:T(8,128)S(1)}, f32[32,256]{1,0:T(8,128)S(1)}, u32[]{:S(2)}, u32[]{:S(2)}) collective-permute-start(f32[32,256]{1,0:T(8,128)S(1)} %forward_pair.1), channel_id=1, source_target_pairs={{0,24},{4,28},{8,16},{12,20},{16,8},{20,12},{24,0},{28,4},{1,25},{... | collective-permute-start | bytes 98312 | tf_op jit(solution)/shard_map/ppermute | solution.py:601
  20.1 0.0 collective-permute-start.6
  20.1 0.8 %collective-permute-start.5 = (f32[32,256]{1,0:T(8,128)S(1)}, f32[32,256]{1,0:T(8,128)S(1)}, u32[]{:S(2)}, u32[]{:S(2)}) collective-permute-start(f32[32,256]{1,0:T(8,128)S(1)} %forward_pair.1), channel_id=1, source_target_pairs={{0,8},{4,12},{8,0},{12,4},{16,24},{20,28},{24,16},{28,20},{1,9},{5... | collective-permute-start | bytes 98312 | tf_op jit(solution)/shard_map/ppermute | solution.py:601
  20.9 1.7 %collective-permute-done.1.refs_0_ = bf16[512,512]{1,0:T(8,128)(2,1)S(1)} collective-permute-done((bf16[512,512]{1,0:T(8,128)(2,1)}, bf16[512,512]{1,0:T(8,128)(2,1)S(1)}, u32[]{:S(2)}, u32[]{:S(2)}) %collective-permute-start.1) | collective-permute-done | bytes 524320 | tf_op jit(solution)/shard_map/ppermute | solution.py:569
  22.6 0.1 add_convert_fusion.1
  22.7 0.4 collective-permute-start.4
  23.1 0.0 collective-permute-done.refs_0_
  23.1 0.1 add_convert_fusion
  23.2 1.7 %collective-permute-start.3 = (bf16[512,256]{1,0:T(8,128)(2,1)S(1)}, bf16[512,256]{1,0:T(8,128)(2,1)S(1)}, u32[]{:S(2)}, u32[]{:S(2)}) collective-permute-start(bf16[512,256]{1,0:T(8,128)(2,1)S(1)} %add_convert_fusion), channel_id=1, source_target_pairs={{0,1},{1,0},{2,3},{3,2},{4,5},{5,4},{6,7},{7,6},{8,9},{9,8},{10,11... | collective-permute-start | bytes 786440 | tf_op jit(solution)/shard_map/ppermute | solution.py:618
  24.9 0.0 collective-permute-done.7.refs_2_
  24.9 0.0 collective-permute-done.6.refs_1_
  24.9 0.0 collective-permute-done.5.refs_0_
  24.9 0.0 copy-start
  24.9 3.2 %respond.1 = (f32[2,1024,128]{2,1,0:T(8,128)S(1)}, f32[2,16,1024,128]{3,2,1,0:T(8,128)S(1)}, f32[2,2,128,128]{3,2,1,0:T(8,128)S(1)}, f32[2,2,128,128]{3,2,1,0:T(8,128)S(1)}) custom-call(f32[2,2,128,128]{3,2,1,0:T(8,128)S(1)} %get-tuple-element.52.hb_ref, f32[2,2,128,128]{3,2,1,0:T(8,128)S(1)} %get-tuple-element.53.eb_ref, ...), custom_call_target="tpu_custom_call" | custom-call | flops 3849999872 | tf_op jit(solution)/shard_map/respond/pallas_call | solution.py:620
  28.1 1.5 %collective-permute-done.4.refs_1_ = bf16[512,256]{1,0:T(8,128)(2,1)S(1)} collective-permute-done((bf16[512,256]{1,0:T(8,128)(2,1)S(1)}, bf16[512,256]{1,0:T(8,128)(2,1)S(1)}, u32[]{:S(2)}, u32[]{:S(2)}) %collective-permute-start.4) | collective-permute-done | bytes 262176 | tf_op jit(solution)/shard_map/ppermute | solution.py:618
  29.6 0.0 copy-done
  29.6 2.5 %adjoint.2 = (bf16[1024,256]{1,0:T(8,128)(2,1)}, bf16[1024,256]{1,0:T(8,128)(2,1)}, bf16[1024,256]{1,0:T(8,128)(2,1)}, f32[2,512,128]{2,1,0:T(8,128)S(1)}, f32[2...) custom-call(bf16[512,512]{1,0:T(8,128)(2,1)S(1)} %get-tuple-element.44.kept_ref, ...), custom_call_target="tpu_custom_call" | custom-call | flops 2969999872 | tf_op jit(solution)/shard_map/adjoint/pallas_call | solution.py:633
  32.0 0.0 collective-permute-done.3.refs_1_
  32.1 2.5 %adjoint.3 = (bf16[1024,256]{1,0:T(8,128)(2,1)}, bf16[1024,256]{1,0:T(8,128)(2,1)}, bf16[1024,256]{1,0:T(8,128)(2,1)}, f32[2,512,128]{2,1,0:T(8,128)S(1)}, f32[2...) custom-call(bf16[512,512]{1,0:T(8,128)(2,1)S(1)} %get-tuple-element.41.ke, ...), custom_call_target="tpu_custom_call", output_to_operand_aliasing={{0}: (3, {}), {1}: (4, {}), {2}: (5, {})} | custom-call | flops 2969999872 | tf_op jit(solution)/shard_map/adjoint/pallas_call | solution.py:633
  34.5 0.1 totals.1.message_ref
  34.6 0.1 collective-permute-start.8
  34.7 1.2 %collective-permute-done.8.partner_ref.refs_7_ = f32[48,256]{1,0:T(8,128)S(1)} collective-permute-done((f32[48,256]{1,0:T(8,128)S(1)}, f32[48,256]{1,0:T(8,128)S(1)}, u32[]{:S(2)}, u32[]{:S(2)}) %collective-permute-start.8) | collective-permute-done | bytes 49184 | tf_op jit(solution)/shard_map/ppermute | solution.py:661
  35.9 0.2 backward_pair.1.refs_8_
  36.0 3.7 %collective-permute-start.11 = (f32[32,256]{1,0:T(8,128)S(1)}, f32[32,256]{1,0:T(8,128)S(1)}, u32[]{:S(2)}, u32[]{:S(2)}) collective-permute-start(f32[32,256]{1,0:T(8,128)S(1)} %backward_pair.1.refs_8_), channel_id=1, source_target_pairs={{0,24},{4,28},{8,16},{12,20},{16,8},{20,12},{24,0},{28,4},{1,25},{... | collective-permute-start | bytes 98312 | tf_op jit(solution)/shard_map/ppermute | solution.py:668
  39.7 0.0 collective-permute-start.10
  39.7 0.8 %collective-permute-start.9 = (f32[32,256]{1,0:T(8,128)S(1)}, f32[32,256]{1,0:T(8,128)S(1)}, u32[]{:S(2)}, u32[]{:S(2)}) collective-permute-start(f32[32,256]{1,0:T(8,128)S(1)} %backward_pair.1.refs_8_), channel_id=1, source_target_pairs={{0,8},{4,12},{8,0},{12,4},{16,24},{20,28},{24,16},{28,20},{1,9},{5... | collective-permute-start | bytes 98312 | tf_op jit(solution)/shard_map/ppermute | solution.py:668
  40.5 1.3 %local_adjoint.2.refs_0_ = f32[2,512,128]{2,1,0:T(8,128)S(1)} custom-call(f32[2,512,128]{2,1,0:T(8,128)S(1)} %get-tuple-element.69.uperm_ref, f32[2,128,128]{2,1,0:T(8,128)S(1)} %get-tuple-element.65.refs_0_, f32[2,128,128]{2,1,0:T(8,128)S(1)} %get-tuple-element.66.refs_1_.refs_0_, f32[16,256]{1,0:T(8,128)S(1)} %get-tuple-element.78.a_ref.refs_7_.refs_10_.refs_2_.refs_1_, ...), custom_call_target="tpu_custom_call" | custom-call | flops 1980000000 | tf_op jit(solution)/shard_map/local_adjoint/pallas_call | solution.py:671
  41.8 1.3 %local_adjoint.3.refs_1_ = f32[2,512,128]{2,1,0:T(8,128)S(1)} custom-call(f32[2,512,128]{2,1,0:T(8,128)S(1)} %get-tuple-element.70.uperm_ref, f32[2,128,128]{2,1,0:T(8,128)S(1)} %get-tuple-element.66.refs_1_.refs_0_, f32[16,256]{1,0:T(8,128)S(1)} %get-tuple-element.78.a_ref.refs_7_.refs_10_.refs_2_.refs_1_, ...), custom_call_target="tpu_custom_call" | custom-call | flops 1980000000 | tf_op jit(solution)/shard_map/local_adjoint/pallas_call | solution.py:671
  43.1 0.0 collective-permute-done.11.refs_11_
  43.1 1.4 %collective-permute-done.10.refs_10_ = f32[32,256]{1,0:T(8,128)S(1)} collective-permute-done((f32[32,256]{1,0:T(8,128)S(1)}, f32[32,256]{1,0:T(8,128)S(1)}, u32[]{:S(2)}, u32[]{:S(2)}) %collective-permute-start.10) | collective-permute-done | bytes 32800 | tf_op jit(solution)/shard_map/ppermute | solution.py:668
  44.5 0.0 collective-permute-done.9.refs_9_
  44.5 3.0 %finish.1 = (bf16[1024,256]{1,0:T(8,128)(2,1)}, bf16[1024,256]{1,0:T(8,128)(2,1)}, f32[16,32]{1,0:T(8,128)}, f32[16,32]{1,0:T(8,128)}) custom-call(f32[2,512,128]{2,1,0:T(8,128)S(1)} %local_adjoint.2.refs_0_, f32[2,512,128]{2,1,0:T(8,128)S(1)} %local_adjoint.3.refs_1_, ...), custom_call_target="tpu_custom_call", output_to_operand_aliasing={{0}: (12, {}), {1}: (13, {})} | custom-call | flops 3740000000 | tf_op jit(solution)/shard_map/finish/pallas_call | solution.py:682
  (3 shorter events, 0.0 us)
Async XLA Ops:
  0.6 9.9 %copy-start.1 = (f32[256,16]{0,1:T(8,128)S(1)}, f32[256,16]{0,1:T(8,128)}, u32[]{:S(2)}) copy-start(f32[256,16]{0,1:T(8,128)} %param.13) | copy-start | bytes 49156
  0.6 9.8 %copy-start.6 = (f32[256,16]{0,1:T(8,128)S(1)}, f32[256,16]{0,1:T(8,128)}, u32[]{:S(2)}) copy-start(f32[256,16]{0,1:T(8,128)} %param.12) | copy-start | bytes 49156
  0.7 9.8 %copy-start.5 = (bf16[1024,256]{1,0:T(8,128)(2,1)S(1)}, bf16[1024,256]{1,0:T(8,128)(2,1)}, u32[]{:S(2)}) copy-start(bf16[1024,256]{1,0:T(8,128)(2,1)} %refs_6_.1) | copy-start | bytes 1572868
  0.7 9.8 %copy-start.4 = (bf16[1024,256]{1,0:T(8,128)(2,1)S(1)}, bf16[1024,256]{1,0:T(8,128)(2,1)}, u32[]{:S(2)}) copy-start(bf16[1024,256]{1,0:T(8,128)(2,1)} %refs_5_.3) | copy-start | bytes 1572868
  6.0 17.1 %collective-permute-start = (bf16[512,512]{1,0:T(8,128)(2,1)}, bf16[512,512]{1,0:T(8,128)(2,1)S(1)}, u32[]{:S(2)}, u32[]{:S(2)}) collective-permute-start(bf16[512,512]{1,0:T(8,128)(2,1)} %get-tuple-element.42), channel_id=1, source_target_pairs={{0,2},{1,3},{2,0},{3,1},{4,6},{5,7},{6,4},{7,5},{8,10},{9,11},{10,... | collective-permute-start | bytes 1572872 | tf_op jit(solution)/shard_map/ppermute | solution.py:569
  9.0 13.6 %collective-permute-start.1 = (bf16[512,512]{1,0:T(8,128)(2,1)}, bf16[512,512]{1,0:T(8,128)(2,1)S(1)}, u32[]{:S(2)}, u32[]{:S(2)}) collective-permute-start(bf16[512,512]{1,0:T(8,128)(2,1)} %get-tuple-element.45), channel_id=1, source_target_pairs={{0,1},{1,0},{2,3},{3,2},{4,5},{5,4},{6,7},{7,6},{8,9},{9,8},{10,11... | collective-permute-start | bytes 1572872 | tf_op jit(solution)/shard_map/ppermute | solution.py:569
  10.5 3.1 %copy-start.2 = (bf16[1024,2048]{1,0:T(8,128)(2,1)S(1)}, bf16[1024,2048]{1,0:T(8,128)(2,1)}, u32[]{:S(2)}) copy-start(bf16[1024,2048]{1,0:T(8,128)(2,1)} %g_ref.3) | copy-start | bytes 12582916
  10.5 3.5 %copy-start.3 = (bf16[1024,2048]{1,0:T(8,128)(2,1)S(1)}, bf16[1024,2048]{1,0:T(8,128)(2,1)}, u32[]{:S(2)}) copy-start(bf16[1024,2048]{1,0:T(8,128)(2,1)} %w_ref.3) | copy-start | bytes 12582916
  13.6 2.8 %collective-permute-start.2 = (f32[32,256]{1,0:T(8,128)S(1)}, f32[32,256]{1,0:T(8,128)S(1)}, u32[]{:S(2)}, u32[]{:S(2)}) collective-permute-start(f32[32,256]{1,0:T(8,128)S(1)} %get-tuple-element.46.total_ref), channel_id=1, source_target_pairs={{0,4},{4,0},{8,12},{12,8},{16,20},{20,16},{24,28},{28,24},{1,5},{5... | collective-permute-start | bytes 98312 | tf_op jit(solution)/shard_map/ppermute | solution.py:594
  16.4 8.4 %collective-permute-start.7 = (f32[32,256]{1,0:T(8,128)S(1)}, f32[32,256]{1,0:T(8,128)S(1)}, u32[]{:S(2)}, u32[]{:S(2)}) collective-permute-start(f32[32,256]{1,0:T(8,128)S(1)} %forward_pair.1), channel_id=1, source_target_pairs={{0,24},{4,28},{8,16},{12,20},{16,8},{20,12},{24,0},{28,4},{1,25},{... | collective-permute-start | bytes 98312 | tf_op jit(solution)/shard_map/ppermute | solution.py:601
  20.1 4.8 %collective-permute-start.6 = (f32[32,256]{1,0:T(8,128)S(1)}, f32[32,256]{1,0:T(8,128)S(1)}, u32[]{:S(2)}, u32[]{:S(2)}) collective-permute-start(f32[32,256]{1,0:T(8,128)S(1)} %forward_pair.1), channel_id=1, source_target_pairs={{0,16},{4,20},{8,24},{12,28},{16,0},{20,4},{24,8},{28,12},{1,17},{... | collective-permute-start | bytes 98312 | tf_op jit(solution)/shard_map/ppermute | solution.py:601
  20.1 4.8 %collective-permute-start.5 = (f32[32,256]{1,0:T(8,128)S(1)}, f32[32,256]{1,0:T(8,128)S(1)}, u32[]{:S(2)}, u32[]{:S(2)}) collective-permute-start(f32[32,256]{1,0:T(8,128)S(1)} %forward_pair.1), channel_id=1, source_target_pairs={{0,8},{4,12},{8,0},{12,4},{16,24},{20,28},{24,16},{28,20},{1,9},{5... | collective-permute-start | bytes 98312 | tf_op jit(solution)/shard_map/ppermute | solution.py:601
  22.7 6.9 %collective-permute-start.4 = (bf16[512,256]{1,0:T(8,128)(2,1)S(1)}, bf16[512,256]{1,0:T(8,128)(2,1)S(1)}, u32[]{:S(2)}, u32[]{:S(2)}) collective-permute-start(bf16[512,256]{1,0:T(8,128)(2,1)S(1)} %add_convert_fusion.1), channel_id=1, source_target_pairs={{0,2},{1,3},{2,0},{3,1},{4,6},{5,7},{6,4},{7,5},{8,10},{9,11},{10,... | collective-permute-start | bytes 786440 | tf_op jit(solution)/shard_map/ppermute | solution.py:618
  23.2 8.9 %collective-permute-start.3 = (bf16[512,256]{1,0:T(8,128)(2,1)S(1)}, bf16[512,256]{1,0:T(8,128)(2,1)S(1)}, u32[]{:S(2)}, u32[]{:S(2)}) collective-permute-start(bf16[512,256]{1,0:T(8,128)(2,1)S(1)} %add_convert_fusion), channel_id=1, source_target_pairs={{0,1},{1,0},{2,3},{3,2},{4,5},{5,4},{6,7},{7,6},{8,9},{9,8},{10,11... | collective-permute-start | bytes 786440 | tf_op jit(solution)/shard_map/ppermute | solution.py:618
  24.9 4.7 %copy-start = (bf16[1024,256]{1,0:T(8,128)(2,1)S(1)}, bf16[1024,256]{1,0:T(8,128)(2,1)}, u32[]{:S(2)}) copy-start(bf16[1024,256]{1,0:T(8,128)(2,1)} %refs_5_.2) | copy-start | bytes 1572868
  34.6 1.3 %collective-permute-start.8 = (f32[48,256]{1,0:T(8,128)S(1)}, f32[48,256]{1,0:T(8,128)S(1)}, u32[]{:S(2)}, u32[]{:S(2)}) collective-permute-start(f32[48,256]{1,0:T(8,128)S(1)} %totals.1.message_ref), channel_id=1, source_target_pairs={{0,4},{4,0},{8,12},{12,8},{16,20},{20,16},{24,28},{28,24},{1,5},{5... | collective-permute-start | bytes 147464 | tf_op jit(solution)/shard_map/ppermute | solution.py:661
  36.0 7.1 %collective-permute-start.11 = (f32[32,256]{1,0:T(8,128)S(1)}, f32[32,256]{1,0:T(8,128)S(1)}, u32[]{:S(2)}, u32[]{:S(2)}) collective-permute-start(f32[32,256]{1,0:T(8,128)S(1)} %backward_pair.1.refs_8_), channel_id=1, source_target_pairs={{0,24},{4,28},{8,16},{12,20},{16,8},{20,12},{24,0},{28,4},{1,25},{... | collective-permute-start | bytes 98312 | tf_op jit(solution)/shard_map/ppermute | solution.py:668
  39.7 4.8 %collective-permute-start.10 = (f32[32,256]{1,0:T(8,128)S(1)}, f32[32,256]{1,0:T(8,128)S(1)}, u32[]{:S(2)}, u32[]{:S(2)}) collective-permute-start(f32[32,256]{1,0:T(8,128)S(1)} %backward_pair.1.refs_8_), channel_id=1, source_target_pairs={{0,16},{4,20},{8,24},{12,28},{16,0},{20,4},{24,8},{28,12},{1,17},{... | collective-permute-start | bytes 98312 | tf_op jit(solution)/shard_map/ppermute | solution.py:668
  39.7 4.8 %collective-permute-start.9 = (f32[32,256]{1,0:T(8,128)S(1)}, f32[32,256]{1,0:T(8,128)S(1)}, u32[]{:S(2)}, u32[]{:S(2)}) collective-permute-start(f32[32,256]{1,0:T(8,128)S(1)} %backward_pair.1.refs_8_), channel_id=1, source_target_pairs={{0,8},{4,12},{8,0},{12,4},{16,24},{20,28},{24,16},{28,20},{1,9},{5... | collective-permute-start | bytes 98312 | tf_op jit(solution)/shard_map/ppermute | solution.py:668

commit v5 on v4

--- a/solution.py
+++ b/solution.py
@@ -300,12 +300,11 @@
                 lax.fori_loop(0, steps // unroll, body, begin)
 
 
-def adjoint_body(segment, modes, received, has_previous, kept_ref, *refs):
+def adjoint_body(segment, modes, received, kept_ref, *refs):
     seg, start, rows = segment
     recv_refs = refs[:received]
-    refs = refs[received + has_previous:]
-    x1_ref, resp_ref, store_ref, hin_ref, kin_ref, a_ref, grad_ref = refs[:7]
-    uperm, gb_ref, sums_ref, nat, rb, qb, grad_here, sem = refs[-8:]
+    x1_ref, resp_ref, store_ref, hin_ref, kin_ref, a_ref = refs[received:received + 6]
+    grad_ref, uperm, gb_ref, sums_ref, nat, rb, qb = refs[received + 6:]
     steps = rows // BLOCKS
     channels = x1_ref.shape[1]
     unroll = 16
@@ -320,10 +319,8 @@
         grad_in = own(kept_ref).astype(F32)
         for recv_ref in recv_refs:
             grad_in = grad_in + own(recv_ref).astype(F32)
-        grad_here[:, lanes] = (grad_in * resp_ref[lane, window, :]).astype(BF16)
+        grad_ref[:, lanes] = (grad_in * resp_ref[lane, window, :]).astype(BF16)
         nat[lane] = (grad_in * x1_ref[window, lanes].astype(F32)).astype(BF16).astype(F32)
-    copy = pltpu.make_async_copy(grad_here, grad_ref.at[window, :], sem)
-    copy.start()
     for lane in range(channels // LANES):
         lanes = pl.ds(lane * LANES, LANES)
         for part in range(2):
@@ -364,7 +361,6 @@
             moment = moment + qb[rowsb, :] - rb[rowsb, :] + a * gb_ref[lane, rowsb, :] * before
         sums_ref[pl.ds(0, modes), lanes] = total
         sums_ref[pl.ds(modes, modes), lanes] = moment
-    copy.wait()
 
 
 def local_body(segments, modes, seg, uperm_ref, *refs):
@@ -460,10 +456,11 @@
 
 def finish_body(segments, modes, tokens, length, pairs, *refs):
     count = len(segments)
-    aloc_refs = refs[:count]
+    aloc_refs, grad_refs = refs[:count], refs[count:2 * count]
+    refs = refs[count:]
     a_ref, r_ref, decay_ref, x2_ref, v_ref, partner_ref, both_ref = refs[count:count + 7]
     got_refs = refs[count + 7:count + 6 + pairs]
-    gx2_ref, gv_ref, rgrad_ref, dgrad_ref, gin, nat, gx2_here, gv_here, r_here, d_here, sems = refs[-11:]
+    gx1_ref, gx2_ref, gv_ref, rgrad_ref, dgrad_ref, gin, nat, gx2_here, gv_here, r_here, d_here, sems = refs[-12:]
     channels = a_ref.shape[1]
     unroll = 16
     pair, core = place()
@@ -478,6 +475,9 @@
             state = state + weight * got_ref[pl.ds(0, modes), lanes]
         states.append(state)
     copies = []
+    for seg, grad_ref in enumerate(grad_refs):
+        copies.append(pltpu.make_async_copy(grad_ref, gx1_ref.at[pl.ds(*segments[seg]), :], sems.at[seg, 2]))
+        copies[-1].start()
     owned = rgrad_ref.shape[1]
     tiles = channels // LANES
     lower = pl.ds(modes, 2 * modes // tiles)
@@ -604,7 +604,8 @@
     arrived = [[piece] for piece in sent]
     away = both
     for level in range(1, len(bits)):
-        for which, (_, _, order) in enumerate(chunks):
+        for which in reversed(range(count)):
+            order = chunks[which][2]
             arrived[which][-1], _ = lax.optimization_barrier((arrived[which][-1], away))
             stop = cut >> level
             width = kept[which].shape[1]
@@ -626,32 +627,32 @@
         name="respond",
     )(hb, eb, xperm, a, r, decay_t, partner, *got)
 
-    previous = []
-    for seg, (start, rows) in enumerate(segments):
+    grads = []
+    for seg in reversed(range(count)):
+        start, rows = segments[seg]
         block_shape = jax.ShapeDtypeStruct((lane_tiles, BLOCKS * modes, LANES), F32)
         pieces = arrived[seg]
-        *buffers, uperm, gb, partial_sums = pl.pallas_call(
-            functools.partial(adjoint_body, (seg, start, rows), modes, len(pieces), len(previous)),
-            in_specs=in_vmem(1 + len(pieces)) + [pl.BlockSpec(memory_space=HBM)] * len(previous) + in_vmem(6),
-            out_specs=[pl.BlockSpec(memory_space=HBM)] * 3 + in_vmem(3),
-            out_shape=[jax.ShapeDtypeStruct((tokens, channels), BF16)] * 3
-            + [
+        grad, uperm, gb, partial_sums = pl.pallas_call(
+            functools.partial(adjoint_body, (seg, start, rows), modes, len(pieces)),
+            in_specs=in_vmem(7 + len(pieces)),
+            out_specs=in_vmem(4),
+            out_shape=[
+                       jax.ShapeDtypeStruct((rows, channels), BF16),
                        jax.ShapeDtypeStruct((lane_tiles, rows, LANES), F32),
                        block_shape,
                        jax.ShapeDtypeStruct((2 * modes, channels), F32)],
             scratch_shapes=[pltpu.VMEM((lane_tiles, rows, LANES), F32)]
-            + [pltpu.VMEM((BLOCKS * modes, LANES), F32)] * 2
-            + [pltpu.VMEM((rows, channels), BF16), pltpu.SemaphoreType.DMA(())],
-            input_output_aliases={1 + len(pieces) + j: j for j in range(len(previous))},
+            + [pltpu.VMEM((BLOCKS * modes, LANES), F32)] * 2,
             compiler_params=params(),
             cost_estimate=cost(2.7 * rows / 512),
             name="adjoint",
-        )(kept[seg], *pieces, *previous, gate_x1, resp, store, hin, kin, a)
-        previous = buffers
+        )(kept[seg], *pieces, gate_x1, resp, store, hin, kin, a)
+        grads.append(grad)
         uperms.append(uperm)
         gbs.append(gb)
         sums.append(partial_sums)
 
+    uperms, gbs, sums, grads = uperms[::-1], gbs[::-1], sums[::-1], grads[::-1]
     message = pl.pallas_call(
         functools.partial(gather_body, segments, modes),
         out_shape=jax.ShapeDtypeStruct((3 * modes, channels), F32),
@@ -679,11 +680,11 @@
         for seg, (_, rows) in enumerate(segments)
     ]
 
-    grad_x2, grad_v, residue_grad, decay_grad = pl.pallas_call(
+    grad_x1, grad_x2, grad_v, residue_grad, decay_grad = pl.pallas_call(
         functools.partial(finish_body, segments, modes, tokens, length, pairs),
-        in_specs=in_vmem(count + 6 + pairs) + [pl.BlockSpec(memory_space=HBM)] * 2,
-        out_specs=[pl.BlockSpec(memory_space=HBM)] * 4,
-        out_shape=[jax.ShapeDtypeStruct((tokens, channels), BF16)] * 2
+        in_specs=in_vmem(2 * count + 6 + pairs),
+        out_specs=[pl.BlockSpec(memory_space=HBM)] * 5,
+        out_shape=[jax.ShapeDtypeStruct((tokens, channels), BF16)] * 3
         + [jax.ShapeDtypeStruct((modes, owned), F32)] * 2,
         scratch_shapes=[pltpu.VMEM((BLOCKS * modes, LANES), F32),
                         pltpu.VMEM((lane_tiles, tokens, LANES), F32),
@@ -691,13 +692,12 @@
                         pltpu.VMEM((tokens, channels), BF16),
                         pltpu.VMEM((modes, owned), F32),
                         pltpu.VMEM((modes, owned), F32),
-                        pltpu.SemaphoreType.DMA((count + 1, 2))],
-        input_output_aliases={count + 6 + pairs: 0, count + 7 + pairs: 1},
+                        pltpu.SemaphoreType.DMA((count + 1, 3))],
         compiler_params=params(),
         cost_estimate=cost(3.4),
         name="finish",
-    )(*alocs, a, r, decay_t, gate_x2, value_v, partner, both, *got, *previous[1:])
-    return previous[0], grad_x2, grad_v, residue_grad.T, decay_grad.T
+    )(*alocs, *grads, a, r, decay_t, gate_x2, value_v, partner, both, *got)
+    return grad_x1, grad_x2, grad_v, residue_grad.T, decay_grad.T
 
 
 def solution(mesh):

time: 47.7 us -> 47.6 us (level)
  no operation moved by 1% of the time
where the time goes in v5:
time: 47.6 us; the launch traced here: 47.5 us
  Pallas kernels  24.6 us (52%)
  starting transfers between devices  15.8 us (33%)
  waiting for transfers between devices  5.76 us (12%)
  between operations  0.85 us (2%)
    ppermute x6, starting transfers between devices, on_device(): lax.ppermute(both, 'ctx', xor_pairs(context_size, 2 * step))  8.91 us
    pallas_call x1, Pallas kernels, project(): pl.pallas_call(functools.partial(project_body, work, width, pieces), in_s...  5.28 us
    pallas_call x2, Pallas kernels, on_device(): pl.pallas_call(functools.partial(adjoint_body, (seg, start, rows), modes,...  4.88 us
    ppermute x2, starting transfers between devices, on_device(): lax.ppermute(piece, 'ch', xor_pairs(ch_size, order[0]))  4.52 us
    pallas_call x1, Pallas kernels, on_device(): pl.pallas_call(functools.partial(respond_body, segments, modes, tokens),...  3.16 us
    pallas_call x1, Pallas kernels, on_device(): pl.pallas_call(functools.partial(finish_body, segments, modes, tokens, le...  3.04 us
    pallas_call x1, Pallas kernels, on_device(): pl.pallas_call(functools.partial(forward_body, segments, modes), out_shap...  3.03 us
    pallas_call x2, Pallas kernels, on_device(): pl.pallas_call(functools.partial(local_body, segments, modes, seg), out_s...  2.63 us
  transfers between devices with their start and end apart: 12, of which 4 were waited for; matrix products, arithmetic and copies ran while one was open for 0% of the time, Pallas kernels for 29%

profile of v5, /device:TPU:0, one launch (start us, length us, event | category | flops | bytes accessed | tf_op | source)
XLA Modules:
  0.0 47.5 jit_solution(4194560819355124220)
XLA Ops:
  0.6 0.0 copy-start.1
  0.6 0.0 copy-start.6
  0.7 0.0 copy-start.5
  0.7 0.0 copy-start.4
  0.7 5.3 %project.1 = (bf16[512,512]{1,0:T(8,128)(2,1)}, bf16[512,512]{1,0:T(8,128)(2,1)}) custom-call(bf16[1024,2048]{1,0:T(8,128)(2,1)} %g_ref.3, bf16[1024,2048]{1,0:T(8,128)(2,1)} %w_ref.3), custom_call_target="tpu_custom_call" | custom-call | flops 5500000256 | tf_op jit(solution)/shard_map/project/pallas_call | solution.py:129
  6.0 3.0 %collective-permute-start = (bf16[512,512]{1,0:T(8,128)(2,1)}, bf16[512,512]{1,0:T(8,128)(2,1)S(1)}, u32[]{:S(2)}, u32[]{:S(2)}) collective-permute-start(bf16[512,512]{1,0:T(8,128)(2,1)} %get-tuple-element.39), channel_id=1, source_target_pairs={{0,1},{1,0},{2,3},{3,2},{4,5},{5,4},{6,7},{7,6},{8,9},{9,8},{10,11... | collective-permute-start | bytes 1572872 | tf_op jit(solution)/shard_map/ppermute | solution.py:569
  9.0 1.5 %collective-permute-start.1 = (bf16[512,512]{1,0:T(8,128)(2,1)}, bf16[512,512]{1,0:T(8,128)(2,1)S(1)}, u32[]{:S(2)}, u32[]{:S(2)}) collective-permute-start(bf16[512,512]{1,0:T(8,128)(2,1)} %get-tuple-element.42), channel_id=1, source_target_pairs={{0,2},{1,3},{2,0},{3,1},{4,6},{5,7},{6,4},{7,5},{8,10},{9,11},{10,... | collective-permute-start | bytes 1572872 | tf_op jit(solution)/shard_map/ppermute | solution.py:569
  10.5 0.0 copy-done.1
  10.5 0.0 copy-done.6
  10.5 0.0 copy-done.5
  10.5 0.0 copy-done.4
  10.5 0.0 copy-start.2
  10.5 0.0 copy-start.3
  10.5 3.0 %forward.1 = (f32[2,1024,128]{2,1,0:T(8,128)S(1)}, f32[2,2,128,128]{3,2,1,0:T(8,128)S(1)}, f32[2,2,128,128]{3,2,1,0:T(8,128)S(1)}, f32[32,256]{1,0:T(8,128)S(1)}) custom-call(bf16[1024,256]{1,0:T(8,128)(2,1)S(1)} %copy-done.4, bf16[1024,256]{1,0:T(8,128)(2,1)S(1)} %copy-done.5, f32[16,256]{1,0:T(8,128)S(1)} %get-tuple-element.72.a_ref.refs_7_.refs_2_.refs_1_.refs_4_, ...), custom_call_target="tpu_custom_call" | custom-call | flops 4070000128 | tf_op jit(solution)/shard_map/forward/pallas_call | solution.py:583
  13.6 0.1 collective-permute-start.2
  13.7 0.0 copy-done.2
  13.7 0.3 copy-done.3
  14.0 2.4 %project_kept.1 = (bf16[512,512]{1,0:T(8,128)(2,1)S(1)}, bf16[512,512]{1,0:T(8,128)(2,1)S(1)}) custom-call(bf16[1024,2048]{1,0:T(8,128)(2,1)S(1)} %copy-done.2, bf16[1024,2048]{1,0:T(8,128)(2,1)S(1)} %copy-done.3), custom_call_target="tpu_custom_call" | custom-call | flops 3300000000 | tf_op jit(solution)/shard_map/project_kept/pallas_call | solution.py:157
  16.4 0.0 collective-permute-done.2.partner_ref
  16.4 3.7 %collective-permute-start.6 = (f32[32,256]{1,0:T(8,128)S(1)}, f32[32,256]{1,0:T(8,128)S(1)}, u32[]{:S(2)}, u32[]{:S(2)}) collective-permute-start(f32[32,256]{1,0:T(8,128)S(1)} %forward_pair.1), channel_id=1, source_target_pairs={{0,24},{4,28},{8,16},{12,20},{16,8},{20,12},{24,0},{28,4},{1,25},{... | collective-permute-start | bytes 98312 | tf_op jit(solution)/shard_map/ppermute | solution.py:601
  20.1 0.0 collective-permute-start.5
  20.1 0.8 %collective-permute-start.4 = (f32[32,256]{1,0:T(8,128)S(1)}, f32[32,256]{1,0:T(8,128)S(1)}, u32[]{:S(2)}, u32[]{:S(2)}) collective-permute-start(f32[32,256]{1,0:T(8,128)S(1)} %forward_pair.1), channel_id=1, source_target_pairs={{0,8},{4,12},{8,0},{12,4},{16,24},{20,28},{24,16},{28,20},{1,9},{5... | collective-permute-start | bytes 98312 | tf_op jit(solution)/shard_map/ppermute | solution.py:601
  20.9 1.7 %collective-permute-done.1.refs_0_ = bf16[512,512]{1,0:T(8,128)(2,1)S(1)} collective-permute-done((bf16[512,512]{1,0:T(8,128)(2,1)}, bf16[512,512]{1,0:T(8,128)(2,1)S(1)}, u32[]{:S(2)}, u32[]{:S(2)}) %collective-permute-start.1) | collective-permute-done | bytes 524320 | tf_op jit(solution)/shard_map/ppermute | solution.py:569
  22.6 0.1 add_convert_fusion.1
  22.6 0.4 collective-permute-start.7
  23.1 0.0 collective-permute-done.refs_0_
  23.1 0.1 add_convert_fusion
  23.1 1.8 %collective-permute-start.3 = (bf16[512,256]{1,0:T(8,128)(2,1)S(1)}, bf16[512,256]{1,0:T(8,128)(2,1)S(1)}, u32[]{:S(2)}, u32[]{:S(2)}) collective-permute-start(bf16[512,256]{1,0:T(8,128)(2,1)S(1)} %add_convert_fusion), channel_id=1, source_target_pairs={{0,2},{1,3},{2,0},{3,1},{4,6},{5,7},{6,4},{7,5},{8,10},{9,11},{10,... | collective-permute-start | bytes 786440 | tf_op jit(solution)/shard_map/ppermute | solution.py:619
  24.9 0.0 collective-permute-done.6.refs_2_
  24.9 0.0 collective-permute-done.5.refs_1_
  24.9 0.0 collective-permute-done.4.refs_0_
  24.9 0.0 copy-start
  24.9 3.2 %respond.1 = (f32[2,1024,128]{2,1,0:T(8,128)S(1)}, f32[2,16,1024,128]{3,2,1,0:T(8,128)S(1)}, f32[2,2,128,128]{3,2,1,0:T(8,128)S(1)}, f32[2,2,128,128]{3,2,1,0:T(8,128)S(1)}) custom-call(f32[2,2,128,128]{3,2,1,0:T(8,128)S(1)} %get-tuple-element.49.hb_ref, f32[2,2,128,128]{3,2,1,0:T(8,128)S(1)} %get-tuple-element.50.eb_ref, ...), custom_call_target="tpu_custom_call" | custom-call | flops 3849999872 | tf_op jit(solution)/shard_map/respond/pallas_call | solution.py:621
  28.1 1.5 %collective-permute-done.7.refs_1_ = bf16[512,256]{1,0:T(8,128)(2,1)S(1)} collective-permute-done((bf16[512,256]{1,0:T(8,128)(2,1)S(1)}, bf16[512,256]{1,0:T(8,128)(2,1)S(1)}, u32[]{:S(2)}, u32[]{:S(2)}) %collective-permute-start.7) | collective-permute-done | bytes 262176 | tf_op jit(solution)/shard_map/ppermute | solution.py:619
  29.6 0.0 copy-done
  29.6 2.4 %adjoint.3 = (bf16[512,256]{1,0:T(8,128)(2,1)S(1)}, f32[2,512,128]{2,1,0:T(8,128)S(1)}, f32[2,128,128]{2,1,0:T(8,128)S(1)}, f32[32,256]{1,0:T(8,128)S(1)}) custom-call(bf16[512,512]{1,0:T(8,128)(2,1)S(1)} %get-tuple-element.41.kept_ref, bf16[512,512]{1,0:T(8,128)(2,1)S(1)} %collective-permute-done.1.refs_0_, ...), custom_call_target="tpu_custom_call" | custom-call | flops 2969999872 | tf_op jit(solution)/shard_map/adjoint/pallas_call | solution.py:635
  32.0 0.0 collective-permute-done.3.refs_1_
  32.0 2.4 %adjoint.2 = (bf16[512,256]{1,0:T(8,128)(2,1)S(1)}, f32[2,512,128]{2,1,0:T(8,128)S(1)}, f32[2,128,128]{2,1,0:T(8,128)S(1)}, f32[32,256]{1,0:T(8,128)S(1)}) custom-call(bf16[512,512]{1,0:T(8,128)(2,1)S(1)} %get-tuple-element.38.kept_ref, bf16[512,512]{1,0:T(8,128)(2,1)S(1)} %collective-permute-done.refs_0_, ...), custom_call_target="tpu_custom_call" | custom-call | flops 2969999872 | tf_op jit(solution)/shard_map/adjoint/pallas_call | solution.py:635
  34.5 0.1 totals.1.message_ref
  34.5 0.1 collective-permute-start.8
  34.6 1.2 %collective-permute-done.8.partner_ref.refs_9_ = f32[48,256]{1,0:T(8,128)S(1)} collective-permute-done((f32[48,256]{1,0:T(8,128)S(1)}, f32[48,256]{1,0:T(8,128)S(1)}, u32[]{:S(2)}, u32[]{:S(2)}) %collective-permute-start.8) | collective-permute-done | bytes 49184 | tf_op jit(solution)/shard_map/ppermute | solution.py:662
  35.8 0.2 backward_pair.1.refs_10_
  36.0 3.7 %collective-permute-start.11 = (f32[32,256]{1,0:T(8,128)S(1)}, f32[32,256]{1,0:T(8,128)S(1)}, u32[]{:S(2)}, u32[]{:S(2)}) collective-permute-start(f32[32,256]{1,0:T(8,128)S(1)} %backward_pair.1.refs_10_), channel_id=1, source_target_pairs={{0,24},{4,28},{8,16},{12,20},{16,8},{20,12},{24,0},{28,4},{1,25},{... | collective-permute-start | bytes 98312 | tf_op jit(solution)/shard_map/ppermute | solution.py:669
  39.6 0.0 collective-permute-start.10
  39.6 0.8 %collective-permute-start.9 = (f32[32,256]{1,0:T(8,128)S(1)}, f32[32,256]{1,0:T(8,128)S(1)}, u32[]{:S(2)}, u32[]{:S(2)}) collective-permute-start(f32[32,256]{1,0:T(8,128)S(1)} %backward_pair.1.refs_10_), channel_id=1, source_target_pairs={{0,8},{4,12},{8,0},{12,4},{16,24},{20,28},{24,16},{28,20},{1,9},{5... | collective-permute-start | bytes 98312 | tf_op jit(solution)/shard_map/ppermute | solution.py:669
  40.4 1.3 %local_adjoint.2.refs_0_ = f32[2,512,128]{2,1,0:T(8,128)S(1)} custom-call(f32[2,512,128]{2,1,0:T(8,128)S(1)} %get-tuple-element.62.uperm_ref, f32[2,128,128]{2,1,0:T(8,128)S(1)} %get-tuple-element.58.refs_0_, f32[2,128,128]{2,1,0:T(8,128)S(1)} %get-tuple-element.59.refs_1_.refs_0_, f32[16,256]{1,0:T(8,128)S(1)} %get-tuple-element.72.a_ref.refs_7_.refs_2_.refs_1_.refs_4_, ...), custom_call_target="tpu_custom_call" | custom-call | flops 1980000000 | tf_op jit(solution)/shard_map/local_adjoint/pallas_call | solution.py:672
  41.8 1.3 %local_adjoint.3.refs_1_ = f32[2,512,128]{2,1,0:T(8,128)S(1)} custom-call(f32[2,512,128]{2,1,0:T(8,128)S(1)} %get-tuple-element.63.uperm_ref, f32[2,128,128]{2,1,0:T(8,128)S(1)} %get-tuple-element.59.refs_1_.refs_0_, f32[16,256]{1,0:T(8,128)S(1)} %get-tuple-element.72.a_ref.refs_7_.refs_2_.refs_1_.refs_4_, ...), custom_call_target="tpu_custom_call" | custom-call | flops 1980000000 | tf_op jit(solution)/shard_map/local_adjoint/pallas_call | solution.py:672
  43.1 0.0 collective-permute-done.11.refs_13_
  43.1 1.4 %collective-permute-done.10.refs_12_ = f32[32,256]{1,0:T(8,128)S(1)} collective-permute-done((f32[32,256]{1,0:T(8,128)S(1)}, f32[32,256]{1,0:T(8,128)S(1)}, u32[]{:S(2)}, u32[]{:S(2)}) %collective-permute-start.10) | collective-permute-done | bytes 32800 | tf_op jit(solution)/shard_map/ppermute | solution.py:669
  44.4 0.0 collective-permute-done.9.refs_11_
  44.5 3.0 %finish.1 = (bf16[1024,256]{1,0:T(8,128)(2,1)}, bf16[1024,256]{1,0:T(8,128)(2,1)}, bf16[1024,256]{1,0:T(8,128)(2,1)}, f32[16,32]{1,0:T(8,128)}, f32[16,32]{1,0:T(8,128)}) custom-call(f32[2,512,128]{2,1,0:T(8,128)S(1)} %local_adjoint.2.refs_0_, f32[2,512,128]{2,1,0:T(8,128)S(1)} %local_adjoint.3.refs_1_, bf16[512,256]{1,0:T(8,128)(2,1)S(1)} %get-tuple-element.64.refs_2_, ...), custom_call_target="tpu_custom_call" | custom-call | flops 3740000000 | tf_op jit(solution)/shard_map/finish/pallas_call | solution.py:683
  (3 shorter events, 0.0 us)
Async XLA Ops:
  0.6 9.9 %copy-start.1 = (f32[256,16]{0,1:T(8,128)S(1)}, f32[256,16]{0,1:T(8,128)}, u32[]{:S(2)}) copy-start(f32[256,16]{0,1:T(8,128)} %param.13) | copy-start | bytes 49156
  0.6 9.8 %copy-start.6 = (f32[256,16]{0,1:T(8,128)S(1)}, f32[256,16]{0,1:T(8,128)}, u32[]{:S(2)}) copy-start(f32[256,16]{0,1:T(8,128)} %param.12) | copy-start | bytes 49156
  0.7 9.8 %copy-start.5 = (bf16[1024,256]{1,0:T(8,128)(2,1)S(1)}, bf16[1024,256]{1,0:T(8,128)(2,1)}, u32[]{:S(2)}) copy-start(bf16[1024,256]{1,0:T(8,128)(2,1)} %refs_8_.1) | copy-start | bytes 1572868
  0.7 9.8 %copy-start.4 = (bf16[1024,256]{1,0:T(8,128)(2,1)S(1)}, bf16[1024,256]{1,0:T(8,128)(2,1)}, u32[]{:S(2)}) copy-start(bf16[1024,256]{1,0:T(8,128)(2,1)} %refs_7_.1) | copy-start | bytes 1572868
  6.0 17.1 %collective-permute-start = (bf16[512,512]{1,0:T(8,128)(2,1)}, bf16[512,512]{1,0:T(8,128)(2,1)S(1)}, u32[]{:S(2)}, u32[]{:S(2)}) collective-permute-start(bf16[512,512]{1,0:T(8,128)(2,1)} %get-tuple-element.39), channel_id=1, source_target_pairs={{0,1},{1,0},{2,3},{3,2},{4,5},{5,4},{6,7},{7,6},{8,9},{9,8},{10,11... | collective-permute-start | bytes 1572872 | tf_op jit(solution)/shard_map/ppermute | solution.py:569
  9.0 13.6 %collective-permute-start.1 = (bf16[512,512]{1,0:T(8,128)(2,1)}, bf16[512,512]{1,0:T(8,128)(2,1)S(1)}, u32[]{:S(2)}, u32[]{:S(2)}) collective-permute-start(bf16[512,512]{1,0:T(8,128)(2,1)} %get-tuple-element.42), channel_id=1, source_target_pairs={{0,2},{1,3},{2,0},{3,1},{4,6},{5,7},{6,4},{7,5},{8,10},{9,11},{10,... | collective-permute-start | bytes 1572872 | tf_op jit(solution)/shard_map/ppermute | solution.py:569
  10.5 3.1 %copy-start.2 = (bf16[1024,2048]{1,0:T(8,128)(2,1)S(1)}, bf16[1024,2048]{1,0:T(8,128)(2,1)}, u32[]{:S(2)}) copy-start(bf16[1024,2048]{1,0:T(8,128)(2,1)} %g_ref.3) | copy-start | bytes 12582916
  10.5 3.5 %copy-start.3 = (bf16[1024,2048]{1,0:T(8,128)(2,1)S(1)}, bf16[1024,2048]{1,0:T(8,128)(2,1)}, u32[]{:S(2)}) copy-start(bf16[1024,2048]{1,0:T(8,128)(2,1)} %w_ref.3) | copy-start | bytes 12582916
  13.6 2.8 %collective-permute-start.2 = (f32[32,256]{1,0:T(8,128)S(1)}, f32[32,256]{1,0:T(8,128)S(1)}, u32[]{:S(2)}, u32[]{:S(2)}) collective-permute-start(f32[32,256]{1,0:T(8,128)S(1)} %get-tuple-element.43.total_ref), channel_id=1, source_target_pairs={{0,4},{4,0},{8,12},{12,8},{16,20},{20,16},{24,28},{28,24},{1,5},{5... | collective-permute-start | bytes 98312 | tf_op jit(solution)/shard_map/ppermute | solution.py:594
  16.4 8.5 %collective-permute-start.6 = (f32[32,256]{1,0:T(8,128)S(1)}, f32[32,256]{1,0:T(8,128)S(1)}, u32[]{:S(2)}, u32[]{:S(2)}) collective-permute-start(f32[32,256]{1,0:T(8,128)S(1)} %forward_pair.1), channel_id=1, source_target_pairs={{0,24},{4,28},{8,16},{12,20},{16,8},{20,12},{24,0},{28,4},{1,25},{... | collective-permute-start | bytes 98312 | tf_op jit(solution)/shard_map/ppermute | solution.py:601
  20.1 4.8 %collective-permute-start.5 = (f32[32,256]{1,0:T(8,128)S(1)}, f32[32,256]{1,0:T(8,128)S(1)}, u32[]{:S(2)}, u32[]{:S(2)}) collective-permute-start(f32[32,256]{1,0:T(8,128)S(1)} %forward_pair.1), channel_id=1, source_target_pairs={{0,16},{4,20},{8,24},{12,28},{16,0},{20,4},{24,8},{28,12},{1,17},{... | collective-permute-start | bytes 98312 | tf_op jit(solution)/shard_map/ppermute | solution.py:601
  20.1 4.8 %collective-permute-start.4 = (f32[32,256]{1,0:T(8,128)S(1)}, f32[32,256]{1,0:T(8,128)S(1)}, u32[]{:S(2)}, u32[]{:S(2)}) collective-permute-start(f32[32,256]{1,0:T(8,128)S(1)} %forward_pair.1), channel_id=1, source_target_pairs={{0,8},{4,12},{8,0},{12,4},{16,24},{20,28},{24,16},{28,20},{1,9},{5... | collective-permute-start | bytes 98312 | tf_op jit(solution)/shard_map/ppermute | solution.py:601
  22.6 6.9 %collective-permute-start.7 = (bf16[512,256]{1,0:T(8,128)(2,1)S(1)}, bf16[512,256]{1,0:T(8,128)(2,1)S(1)}, u32[]{:S(2)}, u32[]{:S(2)}) collective-permute-start(bf16[512,256]{1,0:T(8,128)(2,1)S(1)} %add_convert_fusion.1), channel_id=1, source_target_pairs={{0,1},{1,0},{2,3},{3,2},{4,5},{5,4},{6,7},{7,6},{8,9},{9,8},{10,11... | collective-permute-start | bytes 786440 | tf_op jit(solution)/shard_map/ppermute | solution.py:619
  23.1 8.9 %collective-permute-start.3 = (bf16[512,256]{1,0:T(8,128)(2,1)S(1)}, bf16[512,256]{1,0:T(8,128)(2,1)S(1)}, u32[]{:S(2)}, u32[]{:S(2)}) collective-permute-start(bf16[512,256]{1,0:T(8,128)(2,1)S(1)} %add_convert_fusion), channel_id=1, source_target_pairs={{0,2},{1,3},{2,0},{3,1},{4,6},{5,7},{6,4},{7,5},{8,10},{9,11},{10,... | collective-permute-start | bytes 786440 | tf_op jit(solution)/shard_map/ppermute | solution.py:619
  24.9 4.6 %copy-start = (bf16[1024,256]{1,0:T(8,128)(2,1)S(1)}, bf16[1024,256]{1,0:T(8,128)(2,1)}, u32[]{:S(2)}) copy-start(bf16[1024,256]{1,0:T(8,128)(2,1)} %refs_2_.3) | copy-start | bytes 1572868
  34.5 1.3 %collective-permute-start.8 = (f32[48,256]{1,0:T(8,128)S(1)}, f32[48,256]{1,0:T(8,128)S(1)}, u32[]{:S(2)}, u32[]{:S(2)}) collective-permute-start(f32[48,256]{1,0:T(8,128)S(1)} %totals.1.message_ref), channel_id=1, source_target_pairs={{0,4},{4,0},{8,12},{12,8},{16,20},{20,16},{24,28},{28,24},{1,5},{5... | collective-permute-start | bytes 147464 | tf_op jit(solution)/shard_map/ppermute | solution.py:662
  36.0 7.1 %collective-permute-start.11 = (f32[32,256]{1,0:T(8,128)S(1)}, f32[32,256]{1,0:T(8,128)S(1)}, u32[]{:S(2)}, u32[]{:S(2)}) collective-permute-start(f32[32,256]{1,0:T(8,128)S(1)} %backward_pair.1.refs_10_), channel_id=1, source_target_pairs={{0,24},{4,28},{8,16},{12,20},{16,8},{20,12},{24,0},{28,4},{1,25},{... | collective-permute-start | bytes 98312 | tf_op jit(solution)/shard_map/ppermute | solution.py:669
  39.6 4.8 %collective-permute-start.10 = (f32[32,256]{1,0:T(8,128)S(1)}, f32[32,256]{1,0:T(8,128)S(1)}, u32[]{:S(2)}, u32[]{:S(2)}) collective-permute-start(f32[32,256]{1,0:T(8,128)S(1)} %backward_pair.1.refs_10_), channel_id=1, source_target_pairs={{0,16},{4,20},{8,24},{12,28},{16,0},{20,4},{24,8},{28,12},{1,17},{... | collective-permute-start | bytes 98312 | tf_op jit(solution)/shard_map/ppermute | solution.py:669
  39.6 4.8 %collective-permute-start.9 = (f32[32,256]{1,0:T(8,128)S(1)}, f32[32,256]{1,0:T(8,128)S(1)}, u32[]{:S(2)}, u32[]{:S(2)}) collective-permute-start(f32[32,256]{1,0:T(8,128)S(1)} %backward_pair.1.refs_10_), channel_id=1, source_target_pairs={{0,8},{4,12},{8,0},{12,4},{16,24},{20,28},{24,16},{28,20},{1,9},{5... | collective-permute-start | bytes 98312 | tf_op jit(solution)/shard_map/ppermute | solution.py:669

commit v6 on v5

--- a/solution.py
+++ b/solution.py
@@ -101,22 +101,28 @@
                 copy = pending.pop(key, None)
                 if copy is not None:
                     copy.wait()
-            for spots, where in block_runs(offsets, arranged):
-                product = lax.dot_general(
-                    g_here[pl.ds(start, rows), columns],
-                    w_here[pl.ds(where * width, len(spots) * width), columns],
-                    CONTRACT_LAST, preferred_element_type=F32)
-                for k, spot in enumerate(spots):
-                    here = pl.ds(spot * width, width)
-                    value = product[:, k * width:(k + 1) * width]
-                    if piece > 0:
-                        value = value + total[:, here]
-                    if piece < pieces - 1:
-                        total[:, here] = value
-                    else:
-                        out_ref[:, here] = value.astype(out_ref.dtype)
-        leaving.append(pltpu.make_async_copy(out_ref, out_refs[which], out_sems.at[which]))
-        leaving[-1].start()
+            parts = 2 if piece == pieces - 1 else 1
+            for part in range(parts):
+                height = rows // parts
+                window = pl.ds(part * height, height)
+                for spots, where in block_runs(offsets, arranged):
+                    product = lax.dot_general(
+                        g_here[pl.ds(start + part * height, height), columns],
+                        w_here[pl.ds(where * width, len(spots) * width), columns],
+                        CONTRACT_LAST, preferred_element_type=F32)
+                    for k, spot in enumerate(spots):
+                        here = pl.ds(spot * width, width)
+                        value = product[:, k * width:(k + 1) * width]
+                        if piece > 0:
+                            value = value + total[window, here]
+                        if piece < pieces - 1:
+                            total[window, here] = value
+                        else:
+                            out_ref[window, here] = value.astype(out_ref.dtype)
+                if piece == pieces - 1:
+                    leaving.append(pltpu.make_async_copy(
+                        out_ref.at[window, :], out_refs[which].at[window, :], out_sems.at[which, part]))
+                    leaving[-1].start()
     for copy in leaving:
         copy.wait()
 
@@ -137,7 +143,7 @@
             pltpu.VMEM(shapes[0].shape, F32),
             pltpu.SemaphoreType.DMA((groups, pieces)),
             pltpu.SemaphoreType.DMA((blocks, pieces)),
-            pltpu.SemaphoreType.DMA((len(work),)),
+            pltpu.SemaphoreType.DMA((len(work), 2)),
         ],
         compiler_params=params(60),
         cost_estimate=cost(5),
@@ -180,7 +186,7 @@
 def forward_body(segments, modes, x2_ref, v_ref, a_ref, decay_ref,
                  xperm_ref, hb_ref, eb_ref, total_ref, nat):
     channels = x2_ref.shape[1]
-    unroll = 16
+    unroll = 32
     group = modes // FPARTS
     for lane in range(channels // LANES):
         lanes = pl.ds(lane * LANES, LANES)
@@ -249,7 +255,7 @@
     half = modes // 2
     pair, core = place()
     channels = a_ref.shape[1]
-    unroll = 16
+    unroll = 32
     for lane in range(channels // LANES):
         lanes = pl.ds(lane * LANES, LANES)
         a = a_ref[:, lanes]
@@ -307,7 +313,7 @@
     grad_ref, uperm, gb_ref, sums_ref, nat, rb, qb = refs[received + 6:]
     steps = rows // BLOCKS
     channels = x1_ref.shape[1]
-    unroll = 16
+    unroll = 32
     half = modes // 2
     window = pl.ds(start, rows)
     for lane in range(channels // LANES):
@@ -368,7 +374,7 @@
     gb_refs = refs[:count - seg]
     a_ref, r_ref, decay_ref, aloc_ref, gin = refs[count - seg:]
     channels = a_ref.shape[1]
-    unroll = 16
+    unroll = 32
     half = modes // 2
     for lane in range(channels // LANES):
         lanes = pl.ds(lane * LANES, LANES)

time: 47.6 us -> 47.5 us (level)
  no operation moved by 1% of the time
where the time goes in v6:
time: 47.5 us; the launch traced here: 47.4 us
  Pallas kernels  24.3 us (51%)
  starting transfers between devices  15.8 us (33%)
  waiting for transfers between devices  5.88 us (12%)
  between operations  1.01 us (2%)
    ppermute x6, starting transfers between devices, on_device(): lax.ppermute(both, 'ctx', xor_pairs(context_size, 2 * step))  8.91 us
    pallas_call x1, Pallas kernels, project(): pl.pallas_call(functools.partial(project_body, work, width, pieces), in_s...  5.2 us
    pallas_call x2, Pallas kernels, on_device(): pl.pallas_call(functools.partial(adjoint_body, (seg, start, rows), modes,...  4.68 us
    ppermute x2, starting transfers between devices, on_device(): lax.ppermute(piece, 'ch', xor_pairs(ch_size, order[0]))  4.52 us
    pallas_call x1, Pallas kernels, on_device(): pl.pallas_call(functools.partial(forward_body, segments, modes), out_shap...  3.11 us
    pallas_call x1, Pallas kernels, on_device(): pl.pallas_call(functools.partial(respond_body, segments, modes, tokens),...  3.09 us
    pallas_call x1, Pallas kernels, on_device(): pl.pallas_call(functools.partial(finish_body, segments, modes, tokens, le...  3.04 us
    pallas_call x2, Pallas kernels, on_device(): pl.pallas_call(functools.partial(local_body, segments, modes, seg), out_s...  2.58 us
  transfers between devices with their start and end apart: 12, of which 4 were waited for; matrix products, arithmetic and copies ran while one was open for 0% of the time, Pallas kernels for 29%

profile of v6, /device:TPU:0, one launch (start us, length us, event | category | flops | bytes accessed | tf_op | source)
XLA Modules:
  0.0 47.4 jit_solution(2501891065245640628)
XLA Ops:
  0.6 0.0 copy-start.1
  0.6 0.0 copy-start.6
  0.7 0.0 copy-start.5
  0.7 0.0 copy-start.4
  0.7 5.2 %project.1 = (bf16[512,512]{1,0:T(8,128)(2,1)}, bf16[512,512]{1,0:T(8,128)(2,1)}) custom-call(bf16[1024,2048]{1,0:T(8,128)(2,1)} %g_ref.3, bf16[1024,2048]{1,0:T(8,128)(2,1)} %w_ref.3), custom_call_target="tpu_custom_call" | custom-call | flops 5500000256 | tf_op jit(solution)/shard_map/project/pallas_call | solution.py:135
  5.9 3.0 %collective-permute-start = (bf16[512,512]{1,0:T(8,128)(2,1)}, bf16[512,512]{1,0:T(8,128)(2,1)S(1)}, u32[]{:S(2)}, u32[]{:S(2)}) collective-permute-start(bf16[512,512]{1,0:T(8,128)(2,1)} %get-tuple-element.39), channel_id=1, source_target_pairs={{0,1},{1,0},{2,3},{3,2},{4,5},{5,4},{6,7},{7,6},{8,9},{9,8},{10,11... | collective-permute-start | bytes 1572872 | tf_op jit(solution)/shard_map/ppermute | solution.py:575
  8.9 1.5 %collective-permute-start.1 = (bf16[512,512]{1,0:T(8,128)(2,1)}, bf16[512,512]{1,0:T(8,128)(2,1)S(1)}, u32[]{:S(2)}, u32[]{:S(2)}) collective-permute-start(bf16[512,512]{1,0:T(8,128)(2,1)} %get-tuple-element.42), channel_id=1, source_target_pairs={{0,2},{1,3},{2,0},{3,1},{4,6},{5,7},{6,4},{7,5},{8,10},{9,11},{10,... | collective-permute-start | bytes 1572872 | tf_op jit(solution)/shard_map/ppermute | solution.py:575
  10.4 0.0 copy-done.1
  10.4 0.0 copy-done.6
  10.4 0.0 copy-done.5
  10.4 0.0 copy-done.4
  10.4 0.0 copy-start.2
  10.4 0.0 copy-start.3
  10.5 3.1 %forward.1 = (f32[2,1024,128]{2,1,0:T(8,128)S(1)}, f32[2,2,128,128]{3,2,1,0:T(8,128)S(1)}, f32[2,2,128,128]{3,2,1,0:T(8,128)S(1)}, f32[32,256]{1,0:T(8,128)S(1)}) custom-call(bf16[1024,256]{1,0:T(8,128)(2,1)S(1)} %copy-done.4, bf16[1024,256]{1,0:T(8,128)(2,1)S(1)} %copy-done.5, f32[16,256]{1,0:T(8,128)S(1)} %get-tuple-element.72.a_ref.refs_7_.refs_2_.refs_1_.refs_4_, ...), custom_call_target="tpu_custom_call" | custom-call | flops 4070000128 | tf_op jit(solution)/shard_map/forward/pallas_call | solution.py:589
  13.6 0.1 collective-permute-start.2
  13.7 0.0 copy-done.2
  13.7 0.2 copy-done.3
  13.9 2.4 %project_kept.1 = (bf16[512,512]{1,0:T(8,128)(2,1)S(1)}, bf16[512,512]{1,0:T(8,128)(2,1)S(1)}) custom-call(bf16[1024,2048]{1,0:T(8,128)(2,1)S(1)} %copy-done.2, bf16[1024,2048]{1,0:T(8,128)(2,1)S(1)} %copy-done.3), custom_call_target="tpu_custom_call" | custom-call | flops 3300000000 | tf_op jit(solution)/shard_map/project_kept/pallas_call | solution.py:163
  16.3 0.0 collective-permute-done.2.partner_ref
  16.3 3.7 %collective-permute-start.6 = (f32[32,256]{1,0:T(8,128)S(1)}, f32[32,256]{1,0:T(8,128)S(1)}, u32[]{:S(2)}, u32[]{:S(2)}) collective-permute-start(f32[32,256]{1,0:T(8,128)S(1)} %forward_pair.1), channel_id=1, source_target_pairs={{0,24},{4,28},{8,16},{12,20},{16,8},{20,12},{24,0},{28,4},{1,25},{... | collective-permute-start | bytes 98312 | tf_op jit(solution)/shard_map/ppermute | solution.py:607
  20.0 0.0 collective-permute-start.5
  20.0 0.8 %collective-permute-start.4 = (f32[32,256]{1,0:T(8,128)S(1)}, f32[32,256]{1,0:T(8,128)S(1)}, u32[]{:S(2)}, u32[]{:S(2)}) collective-permute-start(f32[32,256]{1,0:T(8,128)S(1)} %forward_pair.1), channel_id=1, source_target_pairs={{0,8},{4,12},{8,0},{12,4},{16,24},{20,28},{24,16},{28,20},{1,9},{5... | collective-permute-start | bytes 98312 | tf_op jit(solution)/shard_map/ppermute | solution.py:607
  20.8 1.7 %collective-permute-done.1.refs_0_ = bf16[512,512]{1,0:T(8,128)(2,1)S(1)} collective-permute-done((bf16[512,512]{1,0:T(8,128)(2,1)}, bf16[512,512]{1,0:T(8,128)(2,1)S(1)}, u32[]{:S(2)}, u32[]{:S(2)}) %collective-permute-start.1) | collective-permute-done | bytes 524320 | tf_op jit(solution)/shard_map/ppermute | solution.py:575
  22.5 0.1 add_convert_fusion.1
  22.6 0.4 collective-permute-start.7
  23.0 0.0 collective-permute-done.refs_0_
  23.0 0.1 add_convert_fusion
  23.1 1.8 %collective-permute-start.3 = (bf16[512,256]{1,0:T(8,128)(2,1)S(1)}, bf16[512,256]{1,0:T(8,128)(2,1)S(1)}, u32[]{:S(2)}, u32[]{:S(2)}) collective-permute-start(bf16[512,256]{1,0:T(8,128)(2,1)S(1)} %add_convert_fusion), channel_id=1, source_target_pairs={{0,2},{1,3},{2,0},{3,1},{4,6},{5,7},{6,4},{7,5},{8,10},{9,11},{10,... | collective-permute-start | bytes 786440 | tf_op jit(solution)/shard_map/ppermute | solution.py:625
  24.8 0.0 collective-permute-done.6.refs_2_
  24.8 0.0 collective-permute-done.5.refs_1_
  24.8 0.0 collective-permute-done.4.refs_0_
  24.8 0.0 copy-start
  24.8 3.1 %respond.1 = (f32[2,1024,128]{2,1,0:T(8,128)S(1)}, f32[2,16,1024,128]{3,2,1,0:T(8,128)S(1)}, f32[2,2,128,128]{3,2,1,0:T(8,128)S(1)}, f32[2,2,128,128]{3,2,1,0:T(8,128)S(1)}) custom-call(f32[2,2,128,128]{3,2,1,0:T(8,128)S(1)} %get-tuple-element.49.hb_ref, f32[2,2,128,128]{3,2,1,0:T(8,128)S(1)} %get-tuple-element.50.eb_ref, ...), custom_call_target="tpu_custom_call" | custom-call | flops 3849999872 | tf_op jit(solution)/shard_map/respond/pallas_call | solution.py:627
  27.9 1.5 %collective-permute-done.7.refs_1_ = bf16[512,256]{1,0:T(8,128)(2,1)S(1)} collective-permute-done((bf16[512,256]{1,0:T(8,128)(2,1)S(1)}, bf16[512,256]{1,0:T(8,128)(2,1)S(1)}, u32[]{:S(2)}, u32[]{:S(2)}) %collective-permute-start.7) | collective-permute-done | bytes 262176 | tf_op jit(solution)/shard_map/ppermute | solution.py:625
  29.5 0.0 copy-done
  29.5 2.3 %adjoint.3 = (bf16[512,256]{1,0:T(8,128)(2,1)S(1)}, f32[2,512,128]{2,1,0:T(8,128)S(1)}, f32[2,128,128]{2,1,0:T(8,128)S(1)}, f32[32,256]{1,0:T(8,128)S(1)}) custom-call(bf16[512,512]{1,0:T(8,128)(2,1)S(1)} %get-tuple-element.41.kept_ref, bf16[512,512]{1,0:T(8,128)(2,1)S(1)} %collective-permute-done.1.refs_0_, ...), custom_call_target="tpu_custom_call" | custom-call | flops 2969999872 | tf_op jit(solution)/shard_map/adjoint/pallas_call | solution.py:641
  31.8 0.0 collective-permute-done.3.refs_1_
  31.8 2.3 %adjoint.2 = (bf16[512,256]{1,0:T(8,128)(2,1)S(1)}, f32[2,512,128]{2,1,0:T(8,128)S(1)}, f32[2,128,128]{2,1,0:T(8,128)S(1)}, f32[32,256]{1,0:T(8,128)S(1)}) custom-call(bf16[512,512]{1,0:T(8,128)(2,1)S(1)} %get-tuple-element.38.kept_ref, bf16[512,512]{1,0:T(8,128)(2,1)S(1)} %collective-permute-done.refs_0_, ...), custom_call_target="tpu_custom_call" | custom-call | flops 2969999872 | tf_op jit(solution)/shard_map/adjoint/pallas_call | solution.py:641
  34.2 0.1 totals.1.message_ref
  34.2 0.1 collective-permute-start.8
  34.3 1.2 %collective-permute-done.8.partner_ref.refs_9_ = f32[48,256]{1,0:T(8,128)S(1)} collective-permute-done((f32[48,256]{1,0:T(8,128)S(1)}, f32[48,256]{1,0:T(8,128)S(1)}, u32[]{:S(2)}, u32[]{:S(2)}) %collective-permute-start.8) | collective-permute-done | bytes 49184 | tf_op jit(solution)/shard_map/ppermute | solution.py:668
  35.5 0.2 backward_pair.1.refs_10_
  35.7 3.7 %collective-permute-start.11 = (f32[32,256]{1,0:T(8,128)S(1)}, f32[32,256]{1,0:T(8,128)S(1)}, u32[]{:S(2)}, u32[]{:S(2)}) collective-permute-start(f32[32,256]{1,0:T(8,128)S(1)} %backward_pair.1.refs_10_), channel_id=1, source_target_pairs={{0,24},{4,28},{8,16},{12,20},{16,8},{20,12},{24,0},{28,4},{1,25},{... | collective-permute-start | bytes 98312 | tf_op jit(solution)/shard_map/ppermute | solution.py:675
  39.4 0.0 collective-permute-start.10
  39.4 0.8 %collective-permute-start.9 = (f32[32,256]{1,0:T(8,128)S(1)}, f32[32,256]{1,0:T(8,128)S(1)}, u32[]{:S(2)}, u32[]{:S(2)}) collective-permute-start(f32[32,256]{1,0:T(8,128)S(1)} %backward_pair.1.refs_10_), channel_id=1, source_target_pairs={{0,8},{4,12},{8,0},{12,4},{16,24},{20,28},{24,16},{28,20},{1,9},{5... | collective-permute-start | bytes 98312 | tf_op jit(solution)/shard_map/ppermute | solution.py:675
  40.1 1.3 %local_adjoint.2.refs_0_ = f32[2,512,128]{2,1,0:T(8,128)S(1)} custom-call(f32[2,512,128]{2,1,0:T(8,128)S(1)} %get-tuple-element.62.uperm_ref, f32[2,128,128]{2,1,0:T(8,128)S(1)} %get-tuple-element.58.refs_0_, f32[2,128,128]{2,1,0:T(8,128)S(1)} %get-tuple-element.59.refs_1_.refs_0_, f32[16,256]{1,0:T(8,128)S(1)} %get-tuple-element.72.a_ref.refs_7_.refs_2_.refs_1_.refs_4_, ...), custom_call_target="tpu_custom_call" | custom-call | flops 1980000000 | tf_op jit(solution)/shard_map/local_adjoint/pallas_call | solution.py:678
  41.5 1.3 %local_adjoint.3.refs_1_ = f32[2,512,128]{2,1,0:T(8,128)S(1)} custom-call(f32[2,512,128]{2,1,0:T(8,128)S(1)} %get-tuple-element.63.uperm_ref, f32[2,128,128]{2,1,0:T(8,128)S(1)} %get-tuple-element.59.refs_1_.refs_0_, f32[16,256]{1,0:T(8,128)S(1)} %get-tuple-element.72.a_ref.refs_7_.refs_2_.refs_1_.refs_4_, ...), custom_call_target="tpu_custom_call" | custom-call | flops 1980000000 | tf_op jit(solution)/shard_map/local_adjoint/pallas_call | solution.py:678
  42.7 0.0 collective-permute-done.11.refs_13_
  42.7 1.4 %collective-permute-done.10.refs_12_ = f32[32,256]{1,0:T(8,128)S(1)} collective-permute-done((f32[32,256]{1,0:T(8,128)S(1)}, f32[32,256]{1,0:T(8,128)S(1)}, u32[]{:S(2)}, u32[]{:S(2)}) %collective-permute-start.10) | collective-permute-done | bytes 32800 | tf_op jit(solution)/shard_map/ppermute | solution.py:675
  44.2 0.0 collective-permute-done.9.refs_11_
  44.2 3.0 %finish.1 = (bf16[1024,256]{1,0:T(8,128)(2,1)}, bf16[1024,256]{1,0:T(8,128)(2,1)}, bf16[1024,256]{1,0:T(8,128)(2,1)}, f32[16,32]{1,0:T(8,128)}, f32[16,32]{1,0:T(8,128)}) custom-call(f32[2,512,128]{2,1,0:T(8,128)S(1)} %local_adjoint.2.refs_0_, f32[2,512,128]{2,1,0:T(8,128)S(1)} %local_adjoint.3.refs_1_, bf16[512,256]{1,0:T(8,128)(2,1)S(1)} %get-tuple-element.64.refs_2_, ...), custom_call_target="tpu_custom_call" | custom-call | flops 3740000000 | tf_op jit(solution)/shard_map/finish/pallas_call | solution.py:689
  (3 shorter events, 0.0 us)
Async XLA Ops:
  0.6 9.8 %copy-start.1 = (f32[256,16]{0,1:T(8,128)S(1)}, f32[256,16]{0,1:T(8,128)}, u32[]{:S(2)}) copy-start(f32[256,16]{0,1:T(8,128)} %param.13) | copy-start | bytes 49156
  0.6 9.8 %copy-start.6 = (f32[256,16]{0,1:T(8,128)S(1)}, f32[256,16]{0,1:T(8,128)}, u32[]{:S(2)}) copy-start(f32[256,16]{0,1:T(8,128)} %param.12) | copy-start | bytes 49156
  0.7 9.8 %copy-start.5 = (bf16[1024,256]{1,0:T(8,128)(2,1)S(1)}, bf16[1024,256]{1,0:T(8,128)(2,1)}, u32[]{:S(2)}) copy-start(bf16[1024,256]{1,0:T(8,128)(2,1)} %refs_8_.1) | copy-start | bytes 1572868
  0.7 9.8 %copy-start.4 = (bf16[1024,256]{1,0:T(8,128)(2,1)S(1)}, bf16[1024,256]{1,0:T(8,128)(2,1)}, u32[]{:S(2)}) copy-start(bf16[1024,256]{1,0:T(8,128)(2,1)} %refs_7_.1) | copy-start | bytes 1572868
  5.9 17.1 %collective-permute-start = (bf16[512,512]{1,0:T(8,128)(2,1)}, bf16[512,512]{1,0:T(8,128)(2,1)S(1)}, u32[]{:S(2)}, u32[]{:S(2)}) collective-permute-start(bf16[512,512]{1,0:T(8,128)(2,1)} %get-tuple-element.39), channel_id=1, source_target_pairs={{0,1},{1,0},{2,3},{3,2},{4,5},{5,4},{6,7},{7,6},{8,9},{9,8},{10,11... | collective-permute-start | bytes 1572872 | tf_op jit(solution)/shard_map/ppermute | solution.py:575
  8.9 13.6 %collective-permute-start.1 = (bf16[512,512]{1,0:T(8,128)(2,1)}, bf16[512,512]{1,0:T(8,128)(2,1)S(1)}, u32[]{:S(2)}, u32[]{:S(2)}) collective-permute-start(bf16[512,512]{1,0:T(8,128)(2,1)} %get-tuple-element.42), channel_id=1, source_target_pairs={{0,2},{1,3},{2,0},{3,1},{4,6},{5,7},{6,4},{7,5},{8,10},{9,11},{10,... | collective-permute-start | bytes 1572872 | tf_op jit(solution)/shard_map/ppermute | solution.py:575
  10.4 3.2 %copy-start.2 = (bf16[1024,2048]{1,0:T(8,128)(2,1)S(1)}, bf16[1024,2048]{1,0:T(8,128)(2,1)}, u32[]{:S(2)}) copy-start(bf16[1024,2048]{1,0:T(8,128)(2,1)} %g_ref.3) | copy-start | bytes 12582916
  10.4 3.5 %copy-start.3 = (bf16[1024,2048]{1,0:T(8,128)(2,1)S(1)}, bf16[1024,2048]{1,0:T(8,128)(2,1)}, u32[]{:S(2)}) copy-start(bf16[1024,2048]{1,0:T(8,128)(2,1)} %w_ref.3) | copy-start | bytes 12582916
  13.6 2.7 %collective-permute-start.2 = (f32[32,256]{1,0:T(8,128)S(1)}, f32[32,256]{1,0:T(8,128)S(1)}, u32[]{:S(2)}, u32[]{:S(2)}) collective-permute-start(f32[32,256]{1,0:T(8,128)S(1)} %get-tuple-element.43.total_ref), channel_id=1, source_target_pairs={{0,4},{4,0},{8,12},{12,8},{16,20},{20,16},{24,28},{28,24},{1,5},{5... | collective-permute-start | bytes 98312 | tf_op jit(solution)/shard_map/ppermute | solution.py:600
  16.3 8.5 %collective-permute-start.6 = (f32[32,256]{1,0:T(8,128)S(1)}, f32[32,256]{1,0:T(8,128)S(1)}, u32[]{:S(2)}, u32[]{:S(2)}) collective-permute-start(f32[32,256]{1,0:T(8,128)S(1)} %forward_pair.1), channel_id=1, source_target_pairs={{0,24},{4,28},{8,16},{12,20},{16,8},{20,12},{24,0},{28,4},{1,25},{... | collective-permute-start | bytes 98312 | tf_op jit(solution)/shard_map/ppermute | solution.py:607
  20.0 4.8 %collective-permute-start.5 = (f32[32,256]{1,0:T(8,128)S(1)}, f32[32,256]{1,0:T(8,128)S(1)}, u32[]{:S(2)}, u32[]{:S(2)}) collective-permute-start(f32[32,256]{1,0:T(8,128)S(1)} %forward_pair.1), channel_id=1, source_target_pairs={{0,16},{4,20},{8,24},{12,28},{16,0},{20,4},{24,8},{28,12},{1,17},{... | collective-permute-start | bytes 98312 | tf_op jit(solution)/shard_map/ppermute | solution.py:607
  20.0 4.8 %collective-permute-start.4 = (f32[32,256]{1,0:T(8,128)S(1)}, f32[32,256]{1,0:T(8,128)S(1)}, u32[]{:S(2)}, u32[]{:S(2)}) collective-permute-start(f32[32,256]{1,0:T(8,128)S(1)} %forward_pair.1), channel_id=1, source_target_pairs={{0,8},{4,12},{8,0},{12,4},{16,24},{20,28},{24,16},{28,20},{1,9},{5... | collective-permute-start | bytes 98312 | tf_op jit(solution)/shard_map/ppermute | solution.py:607
  22.6 6.9 %collective-permute-start.7 = (bf16[512,256]{1,0:T(8,128)(2,1)S(1)}, bf16[512,256]{1,0:T(8,128)(2,1)S(1)}, u32[]{:S(2)}, u32[]{:S(2)}) collective-permute-start(bf16[512,256]{1,0:T(8,128)(2,1)S(1)} %add_convert_fusion.1), channel_id=1, source_target_pairs={{0,1},{1,0},{2,3},{3,2},{4,5},{5,4},{6,7},{7,6},{8,9},{9,8},{10,11... | collective-permute-start | bytes 786440 | tf_op jit(solution)/shard_map/ppermute | solution.py:625
  23.1 8.8 %collective-permute-start.3 = (bf16[512,256]{1,0:T(8,128)(2,1)S(1)}, bf16[512,256]{1,0:T(8,128)(2,1)S(1)}, u32[]{:S(2)}, u32[]{:S(2)}) collective-permute-start(bf16[512,256]{1,0:T(8,128)(2,1)S(1)} %add_convert_fusion), channel_id=1, source_target_pairs={{0,2},{1,3},{2,0},{3,1},{4,6},{5,7},{6,4},{7,5},{8,10},{9,11},{10,... | collective-permute-start | bytes 786440 | tf_op jit(solution)/shard_map/ppermute | solution.py:625
  24.8 4.6 %copy-start = (bf16[1024,256]{1,0:T(8,128)(2,1)S(1)}, bf16[1024,256]{1,0:T(8,128)(2,1)}, u32[]{:S(2)}) copy-start(bf16[1024,256]{1,0:T(8,128)(2,1)} %refs_2_.3) | copy-start | bytes 1572868
  34.2 1.3 %collective-permute-start.8 = (f32[48,256]{1,0:T(8,128)S(1)}, f32[48,256]{1,0:T(8,128)S(1)}, u32[]{:S(2)}, u32[]{:S(2)}) collective-permute-start(f32[48,256]{1,0:T(8,128)S(1)} %totals.1.message_ref), channel_id=1, source_target_pairs={{0,4},{4,0},{8,12},{12,8},{16,20},{20,16},{24,28},{28,24},{1,5},{5... | collective-permute-start | bytes 147464 | tf_op jit(solution)/shard_map/ppermute | solution.py:668
  35.7 7.0 %collective-permute-start.11 = (f32[32,256]{1,0:T(8,128)S(1)}, f32[32,256]{1,0:T(8,128)S(1)}, u32[]{:S(2)}, u32[]{:S(2)}) collective-permute-start(f32[32,256]{1,0:T(8,128)S(1)} %backward_pair.1.refs_10_), channel_id=1, source_target_pairs={{0,24},{4,28},{8,16},{12,20},{16,8},{20,12},{24,0},{28,4},{1,25},{... | collective-permute-start | bytes 98312 | tf_op jit(solution)/shard_map/ppermute | solution.py:675
  39.4 4.8 %collective-permute-start.10 = (f32[32,256]{1,0:T(8,128)S(1)}, f32[32,256]{1,0:T(8,128)S(1)}, u32[]{:S(2)}, u32[]{:S(2)}) collective-permute-start(f32[32,256]{1,0:T(8,128)S(1)} %backward_pair.1.refs_10_), channel_id=1, source_target_pairs={{0,16},{4,20},{8,24},{12,28},{16,0},{20,4},{24,8},{28,12},{1,17},{... | collective-permute-start | bytes 98312 | tf_op jit(solution)/shard_map/ppermute | solution.py:675
  39.4 4.8 %collective-permute-start.9 = (f32[32,256]{1,0:T(8,128)S(1)}, f32[32,256]{1,0:T(8,128)S(1)}, u32[]{:S(2)}, u32[]{:S(2)}) collective-permute-start(f32[32,256]{1,0:T(8,128)S(1)} %backward_pair.1.refs_10_), channel_id=1, source_target_pairs={{0,8},{4,12},{8,0},{12,4},{16,24},{20,28},{24,16},{28,20},{1,9},{5... | collective-permute-start | bytes 98312 | tf_op jit(solution)/shard_map/ppermute | solution.py:675

commit v7 on v6

--- a/solution.py
+++ b/solution.py
@@ -255,7 +255,7 @@
     half = modes // 2
     pair, core = place()
     channels = a_ref.shape[1]
-    unroll = 32
+    unroll = 64
     for lane in range(channels // LANES):
         lanes = pl.ds(lane * LANES, LANES)
         a = a_ref[:, lanes]
@@ -313,7 +313,7 @@
     grad_ref, uperm, gb_ref, sums_ref, nat, rb, qb = refs[received + 6:]
     steps = rows // BLOCKS
     channels = x1_ref.shape[1]
-    unroll = 32
+    unroll = 64
     half = modes // 2
     window = pl.ds(start, rows)
     for lane in range(channels // LANES):

time: 47.5 us -> 47.2 us (level)
  Pallas kernels: 24.3 us -> 23.8 us
  transfers between devices with their start and end apart: 12 -> 12, of which waited for: 4 -> 4; matrix products, arithmetic and copies ran while one was open for 0% -> 0% of each run, Pallas kernels for 29% -> 28%
where the time goes in v7:
time: 47.2 us; the launch traced here: 47 us
  Pallas kernels  23.8 us (50%)
  starting transfers between devices  15.8 us (33%)
  waiting for transfers between devices  6.01 us (13%)
  between operations  1 us (2%)
    ppermute x6, starting transfers between devices, on_device(): lax.ppermute(both, 'ctx', xor_pairs(context_size, 2 * step))  8.91 us
    pallas_call x1, Pallas kernels, project(): pl.pallas_call(functools.partial(project_body, work, width, pieces), in_s...  5.2 us
    ppermute x2, starting transfers between devices, on_device(): lax.ppermute(piece, 'ch', xor_pairs(ch_size, order[0]))  4.52 us
    pallas_call x2, Pallas kernels, on_device(): pl.pallas_call(functools.partial(adjoint_body, (seg, start, rows), modes,...  4.35 us
    pallas_call x1, Pallas kernels, on_device(): pl.pallas_call(functools.partial(forward_body, segments, modes), out_shap...  3.1 us
    pallas_call x1, Pallas kernels, on_device(): pl.pallas_call(functools.partial(finish_body, segments, modes, tokens, le...  3.04 us
    pallas_call x1, Pallas kernels, on_device(): pl.pallas_call(functools.partial(respond_body, segments, modes, tokens),...  2.97 us
    pallas_call x2, Pallas kernels, on_device(): pl.pallas_call(functools.partial(local_body, segments, modes, seg), out_s...  2.58 us
  transfers between devices with their start and end apart: 12, of which 4 were waited for; matrix products, arithmetic and copies ran while one was open for 0% of the time, Pallas kernels for 28%

profile of v7, /device:TPU:0, one launch (start us, length us, event | category | flops | bytes accessed | tf_op | source)
XLA Modules:
  0.0 47.0 jit_solution(14194434023800579064)
XLA Ops:
  0.6 0.0 copy-start.1
  0.6 0.0 copy-start.6
  0.7 0.0 copy-start.5
  0.7 0.0 copy-start.4
  0.7 5.2 %project.1 = (bf16[512,512]{1,0:T(8,128)(2,1)}, bf16[512,512]{1,0:T(8,128)(2,1)}) custom-call(bf16[1024,2048]{1,0:T(8,128)(2,1)} %g_ref.3, bf16[1024,2048]{1,0:T(8,128)(2,1)} %w_ref.3), custom_call_target="tpu_custom_call" | custom-call | flops 5500000256 | tf_op jit(solution)/shard_map/project/pallas_call | solution.py:135
  5.9 3.0 %collective-permute-start = (bf16[512,512]{1,0:T(8,128)(2,1)}, bf16[512,512]{1,0:T(8,128)(2,1)S(1)}, u32[]{:S(2)}, u32[]{:S(2)}) collective-permute-start(bf16[512,512]{1,0:T(8,128)(2,1)} %get-tuple-element.39), channel_id=1, source_target_pairs={{0,1},{1,0},{2,3},{3,2},{4,5},{5,4},{6,7},{7,6},{8,9},{9,8},{10,11... | collective-permute-start | bytes 1572872 | tf_op jit(solution)/shard_map/ppermute | solution.py:575
  8.9 1.5 %collective-permute-start.1 = (bf16[512,512]{1,0:T(8,128)(2,1)}, bf16[512,512]{1,0:T(8,128)(2,1)S(1)}, u32[]{:S(2)}, u32[]{:S(2)}) collective-permute-start(bf16[512,512]{1,0:T(8,128)(2,1)} %get-tuple-element.42), channel_id=1, source_target_pairs={{0,2},{1,3},{2,0},{3,1},{4,6},{5,7},{6,4},{7,5},{8,10},{9,11},{10,... | collective-permute-start | bytes 1572872 | tf_op jit(solution)/shard_map/ppermute | solution.py:575
  10.4 0.0 copy-done.1
  10.4 0.0 copy-done.6
  10.4 0.0 copy-done.5
  10.4 0.0 copy-done.4
  10.4 0.0 copy-start.2
  10.4 0.0 copy-start.3
  10.5 3.1 %forward.1 = (f32[2,1024,128]{2,1,0:T(8,128)S(1)}, f32[2,2,128,128]{3,2,1,0:T(8,128)S(1)}, f32[2,2,128,128]{3,2,1,0:T(8,128)S(1)}, f32[32,256]{1,0:T(8,128)S(1)}) custom-call(bf16[1024,256]{1,0:T(8,128)(2,1)S(1)} %copy-done.4, bf16[1024,256]{1,0:T(8,128)(2,1)S(1)} %copy-done.5, f32[16,256]{1,0:T(8,128)S(1)} %get-tuple-element.72.a_ref.refs_7_.refs_2_.refs_1_.refs_4_, ...), custom_call_target="tpu_custom_call" | custom-call | flops 4070000128 | tf_op jit(solution)/shard_map/forward/pallas_call | solution.py:589
  13.6 0.1 collective-permute-start.2
  13.6 0.0 copy-done.2
  13.7 0.2 copy-done.3
  13.9 2.4 %project_kept.1 = (bf16[512,512]{1,0:T(8,128)(2,1)S(1)}, bf16[512,512]{1,0:T(8,128)(2,1)S(1)}) custom-call(bf16[1024,2048]{1,0:T(8,128)(2,1)S(1)} %copy-done.2, bf16[1024,2048]{1,0:T(8,128)(2,1)S(1)} %copy-done.3), custom_call_target="tpu_custom_call" | custom-call | flops 3300000000 | tf_op jit(solution)/shard_map/project_kept/pallas_call | solution.py:163
  16.3 0.0 collective-permute-done.2.partner_ref
  16.3 3.7 %collective-permute-start.6 = (f32[32,256]{1,0:T(8,128)S(1)}, f32[32,256]{1,0:T(8,128)S(1)}, u32[]{:S(2)}, u32[]{:S(2)}) collective-permute-start(f32[32,256]{1,0:T(8,128)S(1)} %forward_pair.1), channel_id=1, source_target_pairs={{0,24},{4,28},{8,16},{12,20},{16,8},{20,12},{24,0},{28,4},{1,25},{... | collective-permute-start | bytes 98312 | tf_op jit(solution)/shard_map/ppermute | solution.py:607
  20.0 0.0 collective-permute-start.5
  20.0 0.8 %collective-permute-start.4 = (f32[32,256]{1,0:T(8,128)S(1)}, f32[32,256]{1,0:T(8,128)S(1)}, u32[]{:S(2)}, u32[]{:S(2)}) collective-permute-start(f32[32,256]{1,0:T(8,128)S(1)} %forward_pair.1), channel_id=1, source_target_pairs={{0,8},{4,12},{8,0},{12,4},{16,24},{20,28},{24,16},{28,20},{1,9},{5... | collective-permute-start | bytes 98312 | tf_op jit(solution)/shard_map/ppermute | solution.py:607
  20.8 1.7 %collective-permute-done.1.refs_0_ = bf16[512,512]{1,0:T(8,128)(2,1)S(1)} collective-permute-done((bf16[512,512]{1,0:T(8,128)(2,1)}, bf16[512,512]{1,0:T(8,128)(2,1)S(1)}, u32[]{:S(2)}, u32[]{:S(2)}) %collective-permute-start.1) | collective-permute-done | bytes 524320 | tf_op jit(solution)/shard_map/ppermute | solution.py:575
  22.5 0.1 add_convert_fusion.1
  22.6 0.4 collective-permute-start.7
  23.0 0.0 collective-permute-done.refs_0_
  23.0 0.1 add_convert_fusion
  23.1 1.8 %collective-permute-start.3 = (bf16[512,256]{1,0:T(8,128)(2,1)S(1)}, bf16[512,256]{1,0:T(8,128)(2,1)S(1)}, u32[]{:S(2)}, u32[]{:S(2)}) collective-permute-start(bf16[512,256]{1,0:T(8,128)(2,1)S(1)} %add_convert_fusion), channel_id=1, source_target_pairs={{0,2},{1,3},{2,0},{3,1},{4,6},{5,7},{6,4},{7,5},{8,10},{9,11},{10,... | collective-permute-start | bytes 786440 | tf_op jit(solution)/shard_map/ppermute | solution.py:625
  24.8 0.0 collective-permute-done.6.refs_2_
  24.8 0.0 collective-permute-done.5.refs_1_
  24.8 0.0 collective-permute-done.4.refs_0_
  24.8 0.0 copy-start
  24.8 3.0 %respond.1 = (f32[2,1024,128]{2,1,0:T(8,128)S(1)}, f32[2,16,1024,128]{3,2,1,0:T(8,128)S(1)}, f32[2,2,128,128]{3,2,1,0:T(8,128)S(1)}, f32[2,2,128,128]{3,2,1,0:T(8,128)S(1)}) custom-call(f32[2,2,128,128]{3,2,1,0:T(8,128)S(1)} %get-tuple-element.49.hb_ref, f32[2,2,128,128]{3,2,1,0:T(8,128)S(1)} %get-tuple-element.50.eb_ref, ...), custom_call_target="tpu_custom_call" | custom-call | flops 3849999872 | tf_op jit(solution)/shard_map/respond/pallas_call | solution.py:627
  27.8 1.7 %collective-permute-done.7.refs_1_ = bf16[512,256]{1,0:T(8,128)(2,1)S(1)} collective-permute-done((bf16[512,256]{1,0:T(8,128)(2,1)S(1)}, bf16[512,256]{1,0:T(8,128)(2,1)S(1)}, u32[]{:S(2)}, u32[]{:S(2)}) %collective-permute-start.7) | collective-permute-done | bytes 262176 | tf_op jit(solution)/shard_map/ppermute | solution.py:625
  29.5 0.0 copy-done
  29.5 2.2 %adjoint.3 = (bf16[512,256]{1,0:T(8,128)(2,1)S(1)}, f32[2,512,128]{2,1,0:T(8,128)S(1)}, f32[2,128,128]{2,1,0:T(8,128)S(1)}, f32[32,256]{1,0:T(8,128)S(1)}) custom-call(bf16[512,512]{1,0:T(8,128)(2,1)S(1)} %get-tuple-element.41.kept_ref, bf16[512,512]{1,0:T(8,128)(2,1)S(1)} %collective-permute-done.1.refs_0_, ...), custom_call_target="tpu_custom_call" | custom-call | flops 2969999872 | tf_op jit(solution)/shard_map/adjoint/pallas_call | solution.py:641
  31.7 0.0 collective-permute-done.3.refs_1_
  31.7 2.2 %adjoint.2 = (bf16[512,256]{1,0:T(8,128)(2,1)S(1)}, f32[2,512,128]{2,1,0:T(8,128)S(1)}, f32[2,128,128]{2,1,0:T(8,128)S(1)}, f32[32,256]{1,0:T(8,128)S(1)}) custom-call(bf16[512,512]{1,0:T(8,128)(2,1)S(1)} %get-tuple-element.38.kept_ref, bf16[512,512]{1,0:T(8,128)(2,1)S(1)} %collective-permute-done.refs_0_, ...), custom_call_target="tpu_custom_call" | custom-call | flops 2969999872 | tf_op jit(solution)/shard_map/adjoint/pallas_call | solution.py:641
  33.8 0.1 totals.1.message_ref
  33.9 0.1 collective-permute-start.8
  34.0 1.2 %collective-permute-done.8.partner_ref.refs_9_ = f32[48,256]{1,0:T(8,128)S(1)} collective-permute-done((f32[48,256]{1,0:T(8,128)S(1)}, f32[48,256]{1,0:T(8,128)S(1)}, u32[]{:S(2)}, u32[]{:S(2)}) %collective-permute-start.8) | collective-permute-done | bytes 49184 | tf_op jit(solution)/shard_map/ppermute | solution.py:668
  35.2 0.2 backward_pair.1.refs_10_
  35.4 3.7 %collective-permute-start.11 = (f32[32,256]{1,0:T(8,128)S(1)}, f32[32,256]{1,0:T(8,128)S(1)}, u32[]{:S(2)}, u32[]{:S(2)}) collective-permute-start(f32[32,256]{1,0:T(8,128)S(1)} %backward_pair.1.refs_10_), channel_id=1, source_target_pairs={{0,24},{4,28},{8,16},{12,20},{16,8},{20,12},{24,0},{28,4},{1,25},{... | collective-permute-start | bytes 98312 | tf_op jit(solution)/shard_map/ppermute | solution.py:675
  39.0 0.0 collective-permute-start.10
  39.0 0.8 %collective-permute-start.9 = (f32[32,256]{1,0:T(8,128)S(1)}, f32[32,256]{1,0:T(8,128)S(1)}, u32[]{:S(2)}, u32[]{:S(2)}) collective-permute-start(f32[32,256]{1,0:T(8,128)S(1)} %backward_pair.1.refs_10_), channel_id=1, source_target_pairs={{0,8},{4,12},{8,0},{12,4},{16,24},{20,28},{24,16},{28,20},{1,9},{5... | collective-permute-start | bytes 98312 | tf_op jit(solution)/shard_map/ppermute | solution.py:675
  39.8 1.3 %local_adjoint.2.refs_0_ = f32[2,512,128]{2,1,0:T(8,128)S(1)} custom-call(f32[2,512,128]{2,1,0:T(8,128)S(1)} %get-tuple-element.62.uperm_ref, f32[2,128,128]{2,1,0:T(8,128)S(1)} %get-tuple-element.58.refs_0_, f32[2,128,128]{2,1,0:T(8,128)S(1)} %get-tuple-element.59.refs_1_.refs_0_, f32[16,256]{1,0:T(8,128)S(1)} %get-tuple-element.72.a_ref.refs_7_.refs_2_.refs_1_.refs_4_, ...), custom_call_target="tpu_custom_call" | custom-call | flops 1980000000 | tf_op jit(solution)/shard_map/local_adjoint/pallas_call | solution.py:678
  41.1 1.3 %local_adjoint.3.refs_1_ = f32[2,512,128]{2,1,0:T(8,128)S(1)} custom-call(f32[2,512,128]{2,1,0:T(8,128)S(1)} %get-tuple-element.63.uperm_ref, f32[2,128,128]{2,1,0:T(8,128)S(1)} %get-tuple-element.59.refs_1_.refs_0_, f32[16,256]{1,0:T(8,128)S(1)} %get-tuple-element.72.a_ref.refs_7_.refs_2_.refs_1_.refs_4_, ...), custom_call_target="tpu_custom_call" | custom-call | flops 1980000000 | tf_op jit(solution)/shard_map/local_adjoint/pallas_call | solution.py:678
  42.4 0.0 collective-permute-done.11.refs_13_
  42.4 1.4 %collective-permute-done.10.refs_12_ = f32[32,256]{1,0:T(8,128)S(1)} collective-permute-done((f32[32,256]{1,0:T(8,128)S(1)}, f32[32,256]{1,0:T(8,128)S(1)}, u32[]{:S(2)}, u32[]{:S(2)}) %collective-permute-start.10) | collective-permute-done | bytes 32800 | tf_op jit(solution)/shard_map/ppermute | solution.py:675
  43.8 0.0 collective-permute-done.9.refs_11_
  43.8 3.0 %finish.1 = (bf16[1024,256]{1,0:T(8,128)(2,1)}, bf16[1024,256]{1,0:T(8,128)(2,1)}, bf16[1024,256]{1,0:T(8,128)(2,1)}, f32[16,32]{1,0:T(8,128)}, f32[16,32]{1,0:T(8,128)}) custom-call(f32[2,512,128]{2,1,0:T(8,128)S(1)} %local_adjoint.2.refs_0_, f32[2,512,128]{2,1,0:T(8,128)S(1)} %local_adjoint.3.refs_1_, bf16[512,256]{1,0:T(8,128)(2,1)S(1)} %get-tuple-element.64.refs_2_, ...), custom_call_target="tpu_custom_call" | custom-call | flops 3740000000 | tf_op jit(solution)/shard_map/finish/pallas_call | solution.py:689
  (3 shorter events, 0.0 us)
Async XLA Ops:
  0.6 9.8 %copy-start.1 = (f32[256,16]{0,1:T(8,128)S(1)}, f32[256,16]{0,1:T(8,128)}, u32[]{:S(2)}) copy-start(f32[256,16]{0,1:T(8,128)} %param.13) | copy-start | bytes 49156
  0.6 9.8 %copy-start.6 = (f32[256,16]{0,1:T(8,128)S(1)}, f32[256,16]{0,1:T(8,128)}, u32[]{:S(2)}) copy-start(f32[256,16]{0,1:T(8,128)} %param.12) | copy-start | bytes 49156
  0.7 9.8 %copy-start.5 = (bf16[1024,256]{1,0:T(8,128)(2,1)S(1)}, bf16[1024,256]{1,0:T(8,128)(2,1)}, u32[]{:S(2)}) copy-start(bf16[1024,256]{1,0:T(8,128)(2,1)} %refs_8_.1) | copy-start | bytes 1572868
  0.7 9.8 %copy-start.4 = (bf16[1024,256]{1,0:T(8,128)(2,1)S(1)}, bf16[1024,256]{1,0:T(8,128)(2,1)}, u32[]{:S(2)}) copy-start(bf16[1024,256]{1,0:T(8,128)(2,1)} %refs_7_.1) | copy-start | bytes 1572868
  5.9 17.1 %collective-permute-start = (bf16[512,512]{1,0:T(8,128)(2,1)}, bf16[512,512]{1,0:T(8,128)(2,1)S(1)}, u32[]{:S(2)}, u32[]{:S(2)}) collective-permute-start(bf16[512,512]{1,0:T(8,128)(2,1)} %get-tuple-element.39), channel_id=1, source_target_pairs={{0,1},{1,0},{2,3},{3,2},{4,5},{5,4},{6,7},{7,6},{8,9},{9,8},{10,11... | collective-permute-start | bytes 1572872 | tf_op jit(solution)/shard_map/ppermute | solution.py:575
  8.9 13.6 %collective-permute-start.1 = (bf16[512,512]{1,0:T(8,128)(2,1)}, bf16[512,512]{1,0:T(8,128)(2,1)S(1)}, u32[]{:S(2)}, u32[]{:S(2)}) collective-permute-start(bf16[512,512]{1,0:T(8,128)(2,1)} %get-tuple-element.42), channel_id=1, source_target_pairs={{0,2},{1,3},{2,0},{3,1},{4,6},{5,7},{6,4},{7,5},{8,10},{9,11},{10,... | collective-permute-start | bytes 1572872 | tf_op jit(solution)/shard_map/ppermute | solution.py:575
  10.4 3.2 %copy-start.2 = (bf16[1024,2048]{1,0:T(8,128)(2,1)S(1)}, bf16[1024,2048]{1,0:T(8,128)(2,1)}, u32[]{:S(2)}) copy-start(bf16[1024,2048]{1,0:T(8,128)(2,1)} %g_ref.3) | copy-start | bytes 12582916
  10.4 3.5 %copy-start.3 = (bf16[1024,2048]{1,0:T(8,128)(2,1)S(1)}, bf16[1024,2048]{1,0:T(8,128)(2,1)}, u32[]{:S(2)}) copy-start(bf16[1024,2048]{1,0:T(8,128)(2,1)} %w_ref.3) | copy-start | bytes 12582916
  13.6 2.7 %collective-permute-start.2 = (f32[32,256]{1,0:T(8,128)S(1)}, f32[32,256]{1,0:T(8,128)S(1)}, u32[]{:S(2)}, u32[]{:S(2)}) collective-permute-start(f32[32,256]{1,0:T(8,128)S(1)} %get-tuple-element.43.total_ref), channel_id=1, source_target_pairs={{0,4},{4,0},{8,12},{12,8},{16,20},{20,16},{24,28},{28,24},{1,5},{5... | collective-permute-start | bytes 98312 | tf_op jit(solution)/shard_map/ppermute | solution.py:600
  16.3 8.5 %collective-permute-start.6 = (f32[32,256]{1,0:T(8,128)S(1)}, f32[32,256]{1,0:T(8,128)S(1)}, u32[]{:S(2)}, u32[]{:S(2)}) collective-permute-start(f32[32,256]{1,0:T(8,128)S(1)} %forward_pair.1), channel_id=1, source_target_pairs={{0,24},{4,28},{8,16},{12,20},{16,8},{20,12},{24,0},{28,4},{1,25},{... | collective-permute-start | bytes 98312 | tf_op jit(solution)/shard_map/ppermute | solution.py:607
  20.0 4.8 %collective-permute-start.5 = (f32[32,256]{1,0:T(8,128)S(1)}, f32[32,256]{1,0:T(8,128)S(1)}, u32[]{:S(2)}, u32[]{:S(2)}) collective-permute-start(f32[32,256]{1,0:T(8,128)S(1)} %forward_pair.1), channel_id=1, source_target_pairs={{0,16},{4,20},{8,24},{12,28},{16,0},{20,4},{24,8},{28,12},{1,17},{... | collective-permute-start | bytes 98312 | tf_op jit(solution)/shard_map/ppermute | solution.py:607
  20.0 4.8 %collective-permute-start.4 = (f32[32,256]{1,0:T(8,128)S(1)}, f32[32,256]{1,0:T(8,128)S(1)}, u32[]{:S(2)}, u32[]{:S(2)}) collective-permute-start(f32[32,256]{1,0:T(8,128)S(1)} %forward_pair.1), channel_id=1, source_target_pairs={{0,8},{4,12},{8,0},{12,4},{16,24},{20,28},{24,16},{28,20},{1,9},{5... | collective-permute-start | bytes 98312 | tf_op jit(solution)/shard_map/ppermute | solution.py:607
  22.6 6.9 %collective-permute-start.7 = (bf16[512,256]{1,0:T(8,128)(2,1)S(1)}, bf16[512,256]{1,0:T(8,128)(2,1)S(1)}, u32[]{:S(2)}, u32[]{:S(2)}) collective-permute-start(bf16[512,256]{1,0:T(8,128)(2,1)S(1)} %add_convert_fusion.1), channel_id=1, source_target_pairs={{0,1},{1,0},{2,3},{3,2},{4,5},{5,4},{6,7},{7,6},{8,9},{9,8},{10,11... | collective-permute-start | bytes 786440 | tf_op jit(solution)/shard_map/ppermute | solution.py:625
  23.1 8.6 %collective-permute-start.3 = (bf16[512,256]{1,0:T(8,128)(2,1)S(1)}, bf16[512,256]{1,0:T(8,128)(2,1)S(1)}, u32[]{:S(2)}, u32[]{:S(2)}) collective-permute-start(bf16[512,256]{1,0:T(8,128)(2,1)S(1)} %add_convert_fusion), channel_id=1, source_target_pairs={{0,2},{1,3},{2,0},{3,1},{4,6},{5,7},{6,4},{7,5},{8,10},{9,11},{10,... | collective-permute-start | bytes 786440 | tf_op jit(solution)/shard_map/ppermute | solution.py:625
  24.8 4.6 %copy-start = (bf16[1024,256]{1,0:T(8,128)(2,1)S(1)}, bf16[1024,256]{1,0:T(8,128)(2,1)}, u32[]{:S(2)}) copy-start(bf16[1024,256]{1,0:T(8,128)(2,1)} %refs_2_.3) | copy-start | bytes 1572868
  33.9 1.3 %collective-permute-start.8 = (f32[48,256]{1,0:T(8,128)S(1)}, f32[48,256]{1,0:T(8,128)S(1)}, u32[]{:S(2)}, u32[]{:S(2)}) collective-permute-start(f32[48,256]{1,0:T(8,128)S(1)} %totals.1.message_ref), channel_id=1, source_target_pairs={{0,4},{4,0},{8,12},{12,8},{16,20},{20,16},{24,28},{28,24},{1,5},{5... | collective-permute-start | bytes 147464 | tf_op jit(solution)/shard_map/ppermute | solution.py:668
  35.4 7.0 %collective-permute-start.11 = (f32[32,256]{1,0:T(8,128)S(1)}, f32[32,256]{1,0:T(8,128)S(1)}, u32[]{:S(2)}, u32[]{:S(2)}) collective-permute-start(f32[32,256]{1,0:T(8,128)S(1)} %backward_pair.1.refs_10_), channel_id=1, source_target_pairs={{0,24},{4,28},{8,16},{12,20},{16,8},{20,12},{24,0},{28,4},{1,25},{... | collective-permute-start | bytes 98312 | tf_op jit(solution)/shard_map/ppermute | solution.py:675
  39.0 4.8 %collective-permute-start.10 = (f32[32,256]{1,0:T(8,128)S(1)}, f32[32,256]{1,0:T(8,128)S(1)}, u32[]{:S(2)}, u32[]{:S(2)}) collective-permute-start(f32[32,256]{1,0:T(8,128)S(1)} %backward_pair.1.refs_10_), channel_id=1, source_target_pairs={{0,16},{4,20},{8,24},{12,28},{16,0},{20,4},{24,8},{28,12},{1,17},{... | collective-permute-start | bytes 98312 | tf_op jit(solution)/shard_map/ppermute | solution.py:675
  39.0 4.8 %collective-permute-start.9 = (f32[32,256]{1,0:T(8,128)S(1)}, f32[32,256]{1,0:T(8,128)S(1)}, u32[]{:S(2)}, u32[]{:S(2)}) collective-permute-start(f32[32,256]{1,0:T(8,128)S(1)} %backward_pair.1.refs_10_), channel_id=1, source_target_pairs={{0,8},{4,12},{8,0},{12,4},{16,24},{20,28},{24,16},{28,20},{1,9},{5... | collective-permute-start | bytes 98312 | tf_op jit(solution)/shard_map/ppermute | solution.py:675
